TPU v7x, 32 devices: a whole 2x2x4 slice. The times are simulated.
32 devices in a mesh: row: 4 (over x, core), col: 8 (over z, y).
Axes of the slice: x: 2, y: 2, z: 4, core: 2. Of those that a mesh axis runs over, the one named last changes fastest.
Arguments:
- features: float32 [4096, 256], P(('row', 'col')), may hold values from -6 to 6
- adj_tiles: bfloat16 [4, 8, 96, 128, 128], P('row', 'col'), may hold values from 0 to 1, as said below
- tile_dst: int32 [4, 8, 96], P('row', 'col'), may hold values from 0 to 3, as said below
- tile_src: int32 [4, 8, 96], P('row', 'col'), may hold values from 0 to 7, as said below
- tile_count: int32 [4, 8], P('row', 'col'), may hold values from 1 to 96, as said below
- self_weight: float32 [256, 256], replicated, may hold values from -0.375 to 0.375
- neighbor_weight: float32 [256, 256], replicated, may hold values from -1.5 to 1.5
- layer_bias: float32 [256], replicated, may hold values from -3 to 3
Outputs:
- activated: float32 [4096, 256], P(('row', 'col'))
Inputs may be any that keep to these rules, and one draw needn't show every extreme that they name: `adj_tiles`: every entry is 0 or 1. `tile_dst`: a destination tile within the column group of the device. `tile_src`: a source tile within the row group of the device. `tile_count`: list entries at and beyond a device's count are padding; every device holds at least one listed tile; some device holds exactly 96.
All inputs are finite; a program needn't handle non-finite values.
Results may differ from a plain program's by a relative error of at most 0.0003.
Values sent between devices are 32-bit elements; how exact they have to be, the bound alone decides.
No kernel may reach another device: no remote copies, remote signals or barrier semaphores. Data moves between devices by JAX's collectives and lax.ppermute only.
A program may use at most 64 MiB of HBM per device.

v0:
```python
import jax
import jax.numpy as jnp
from jax import lax
from jax.sharding import PartitionSpec as P


def accumulate(blocks, source_tiles, sources, targets, valid_count, state_pair):

    def visit(group, inner_pair):
        aggregate, degrees = inner_pair
        first_slot = group * 8
        block_group = lax.dynamic_slice_in_dim(blocks, first_slot, 8, 0).astype(jnp.float32)
        source_ids = lax.dynamic_slice_in_dim(sources, first_slot, 8, 0)
        source_group = jnp.take(source_tiles, source_ids, axis=0)
        target_group = lax.dynamic_slice_in_dim(targets, first_slot, 8, 0)
        live_slots = (first_slot + jnp.arange(8, dtype=jnp.int32) < valid_count).astype(jnp.float32)
        products = jnp.einsum(
            "kij,kjf->kif", block_group, source_group, precision=lax.Precision.HIGHEST
        )
        row_sums = jnp.sum(block_group, axis=2)
        for slot in range(8):
            target_id = target_group[slot]
            current = lax.dynamic_slice_in_dim(aggregate, target_id, 1, 0)
            aggregate = lax.dynamic_update_slice_in_dim(
                aggregate, current + live_slots[slot] * products[slot][None], target_id, 0
            )
            current_deg = lax.dynamic_slice_in_dim(degrees, target_id, 1, 0)
            degrees = lax.dynamic_update_slice_in_dim(
                degrees, current_deg + live_slots[slot] * row_sums[slot][None], target_id, 0
            )
        return (aggregate, degrees)

    group_count = (valid_count + 7) // 8
    return lax.fori_loop(0, group_count, visit, state_pair)


def on_device(
    features, adj_tiles, tile_dst, tile_src, tile_count, self_weight, neighbor_weight, layer_bias
):
    tile_size = adj_tiles.shape[-1]
    feat_width = features.shape[1]
    node_rows = features.shape[0]
    adjacency = adj_tiles[0, 0]
    targets = tile_dst[0, 0]
    sources = tile_src[0, 0]
    valid_total = tile_count[0, 0]
    gathered = lax.all_gather(features, "col", axis=0, tiled=True)
    source_tiles = gathered.reshape(-1, tile_size, feat_width)
    target_count = lax.axis_size("row") * node_rows // tile_size
    start_pair = (
        jnp.zeros((target_count, tile_size, feat_width), jnp.float32),
        jnp.zeros((target_count, tile_size), jnp.float32),
    )
    state_pair = accumulate(adjacency, source_tiles, sources, targets, valid_total, start_pair)
    aggregate = state_pair[0].reshape(-1, feat_width)
    degrees = state_pair[1].reshape(-1)
    summed_rows, summed_degrees = lax.psum((aggregate, degrees), "row")
    first_row = lax.axis_index("row") * node_rows
    own_rows = lax.dynamic_slice_in_dim(summed_rows, first_row, node_rows, 0)
    own_degrees = lax.dynamic_slice_in_dim(summed_degrees, first_row, node_rows, 0)
    neighbor_mean = own_rows / jnp.maximum(own_degrees, 1.0)[:, None]
    own_part = jnp.dot(
        features, self_weight, precision=lax.Precision.HIGHEST, preferred_element_type=jnp.float32
    )
    neighbor_part = jnp.dot(
        neighbor_mean,
        neighbor_weight,
        precision=lax.Precision.HIGHEST,
        preferred_element_type=jnp.float32,
    )
    return jnp.maximum(own_part + neighbor_part + layer_bias, 0.0)


def solution(mesh):
    placed = (
        P(("row", "col"), None),
        P("row", "col", None, None, None),
        P("row", "col", None),
        P("row", "col", None),
        P("row", "col"),
        P(),
        P(),
        P(),
    )
    return jax.shard_map(
        on_device, mesh=mesh, in_specs=placed, out_specs=P(("row", "col"), None), check_vma=False
    )
```

profile of v0, /device:TPU:0, one launch (start us, length us, event | category | flops | bytes accessed | tf_op | source)
XLA Modules:
  0.0 556.7 jit_solution(17998743664892988330)
XLA Ops:
  8.0 44.4 %all-gather.2.cloned.1.call-done = f32[1024,256]{1,0:T(8,128)} async-done(((f32[128,256]{1,0:T(8,128)}), f32[1024,256]{1,0:T(8,128)}) %all-gather.2.cloned.1.call-update) | async-done | bytes 1048592 | tf_op jit(solution)/shard_map/all_gather | solution.py:47
  52.5 464.2 %while.12 = (s32[]{:T(128)}, f32[4,128,256]{2,1,0:T(8,128)S(1)}, f32[4,128]{1,0:T(4,128)S(1)}, s32[]{:T(128)}, s32[96]{0:T(128)}, /*index=5*/s32[]{:T(128)}, bf1...) while((s32[]{:T(128)}, f32[4,128,256]{2,1,0:T(8,128)S(1)}, ...), condition=%wide.region_2.3_spmd, body=%wide.region_0.2_spmd.sunk | while | flops 403703872 | bytes 7910407 | solution.py:34
  55.9 1.4 compare_and_fusion.2
  64.9 1.3 fusion.79
  74.6 1.4 fusion.82
  82.4 1.8 gather_fusion
  84.2 1.7 fusion.67
  94.6 1.4 compare_and_fusion.2
  103.5 1.3 fusion.79
  113.2 1.4 fusion.82
  121.0 1.8 gather_fusion
  122.9 1.7 fusion.67
  133.3 1.4 compare_and_fusion.2
  142.2 1.3 fusion.79
  151.9 1.4 fusion.82
  159.7 1.8 gather_fusion
  161.6 1.7 fusion.67
  171.9 1.4 compare_and_fusion.2
  180.9 1.3 fusion.79
  190.6 1.4 fusion.82
  198.4 1.8 gather_fusion
  200.2 1.7 fusion.67
  210.6 1.4 compare_and_fusion.2
  219.6 1.3 fusion.79
  229.3 1.4 fusion.82
  237.1 1.8 gather_fusion
  238.9 1.7 fusion.67
  249.3 1.4 compare_and_fusion.2
  258.2 1.3 fusion.79
  268.0 1.4 fusion.82
  275.8 1.8 gather_fusion
  277.6 1.7 fusion.67
  288.0 1.4 compare_and_fusion.2
  296.9 1.3 fusion.79
  306.6 1.4 fusion.82
  314.4 1.8 gather_fusion
  316.3 1.7 fusion.67
  326.6 1.4 compare_and_fusion.2
  335.6 1.3 fusion.79
  345.3 1.4 fusion.82
  353.1 1.8 gather_fusion
  355.0 1.7 fusion.67
  365.3 1.4 compare_and_fusion.2
  374.3 1.3 fusion.79
  384.0 1.4 fusion.82
  391.8 1.8 gather_fusion
  393.6 1.7 fusion.67
  404.0 1.4 compare_and_fusion.2
  413.0 1.3 fusion.79
  422.7 1.4 fusion.82
  430.5 1.8 gather_fusion
  432.3 1.7 fusion.67
  442.7 1.4 compare_and_fusion.2
  451.6 1.3 fusion.79
  461.3 1.4 fusion.82
  469.1 1.8 gather_fusion
  471.0 1.7 fusion.67
  481.4 1.4 compare_and_fusion.2
  500.0 1.4 fusion.82
  507.8 1.8 gather_fusion
  509.7 1.7 fusion.67
  517.8 5.8 %psum.15 = f32[512]{0:T(512)S(1)} all-reduce(f32[512]{0:T(512)S(1)} %bitcast.62), channel_id=1, replica_groups=mesh['row'=4,'col'=8] {'row'}, use_global_device_ids=true, to_apply=%region_4.5 | all-reduce | flops 512 | bytes 4096 | tf_op jit(solution)/shard_map/psum | solution.py:57
  523.7 24.3 %all-reduce.2.cloned.1.call-done = f32[512,256]{1,0:T(8,128)} async-done(((f32[512,256]{1,0:T(8,128)}), f32[512,256]{1,0:T(8,128)}) %all-reduce.2.cloned.1.call-update) | async-done | bytes 524304 | tf_op jit(solution)/shard_map/psum | solution.py:57
  548.0 1.9 fusion.32
  (367 shorter events, 192.8 us)
Async XLA Ops:
  6.5 510.9 %copy-start = (f32[256,256]{1,0:T(8,128)S(1)}, f32[256,256]{1,0:T(8,128)}, u32[]{:S(2)}) copy-start(f32[256,256]{1,0:T(8,128)} %param.15) | copy-start | bytes 786436
  6.5 45.8 %all-gather.2.cloned.1.call-start = ((), (), s32[]{:S(2)}) async-start(), calls=%async_computation | async-start | bytes 1179648 | tf_op jit(solution)/shard_map/all_gather | solution.py:47
  7.3 540.7 %all-reduce.2.cloned.1.call-start = ((), (), s32[]{:S(2)}) async-start(), calls=%async_computation.1 | async-start | bytes 1048576 | tf_op jit(solution)/shard_map/psum | solution.py:57
  52.4 465.1 %copy-start.2 = (f32[128,256]{1,0:T(8,128)S(1)}, f32[128,256]{1,0:T(8,128)}, u32[]{:S(2)}) copy-start(f32[128,256]{1,0:T(8,128)} %param.10) | copy-start | bytes 393220
  52.4 495.5 %copy-start.4 = (f32[256,256]{1,0:T(8,128)S(1)}, f32[256,256]{1,0:T(8,128)}, u32[]{:S(2)}) copy-start(f32[256,256]{1,0:T(8,128)} %param.16) | copy-start | bytes 786436
  52.4 495.5 %copy-start.5 = (f32[256]{0:T(256)S(1)}, f32[256]{0:T(256)}, u32[]{:S(2)}) copy-start(f32[256]{0:T(256)} %param.17) | copy-start | bytes 3076
  59.1 2.8 copy-start.3
  97.7 2.8 copy-start.3
  136.4 2.8 copy-start.3
  175.1 2.8 copy-start.3
  213.8 2.8 copy-start.3
  252.4 2.8 copy-start.3
  291.1 2.8 copy-start.3
  329.8 2.8 copy-start.3
  368.5 2.8 copy-start.3
  407.2 2.8 copy-start.3
  445.8 2.8 copy-start.3
  484.5 2.8 copy-start.3
  516.7 0.8 copy-start.1
Sparse Core Ops, SparseCore 0:
  9.5 42.8 all-gather.1
  517.6 30.3 all-reduce.1
where the time goes:
time: 565 us; the launch traced here: 557 us
  other arithmetic  210 us (37%)
  loops' own time  183 us (32%)
  waiting for transfers between devices  69.4 us (12%)
  local copies, waits for them, and re-layouts  51.2 us (9%)
  matrix products  23.1 us (4%)
  between operations  14.2 us (3%)
  blocking collectives  5.82 us (1%)
    another operation x1, loops' own time, accumulate(): return lax.fori_loop(0, group_count, visit, state_pair)  183 us
    add x96, other arithmetic, visit(): current_deg + live_slots[slot] * row_sums[slot][None]  118 us
    dynamic_update_slice x96, other arithmetic, visit(): lax.dynamic_update_slice_in_dim(aggregate, current + live_slots[slot] * p...  62.1 us
    all_gather x1, waiting for transfers between devices, on_device(): gathered = lax.all_gather(features, 'col', axis=0, tiled=True)  44.4 us
    psum x1, waiting for transfers between devices, on_device(): summed_rows, summed_degrees = lax.psum((aggregate, degrees), 'row')  24.3 us
    gather x12, local copies, waits for them, and re-layouts, visit(): source_group = jnp.take(source_tiles, source_ids, axis=0)  22 us
    dot_general x12, matrix products, visit(): jnp.einsum('kij,kjf->kif', block_group, source_group, precision=lax.Preci...  20.9 us
    and x12, other arithmetic, visit(): source_group = jnp.take(source_tiles, source_ids, axis=0)  16.6 us
  transfers between devices with their start and end apart: 2, of which 2 were waited for; matrix products, arithmetic and copies ran while one was open for 0% of the time, Pallas kernels for 0%

commit v1 on v0

v1 whole, which is shorter than its diff:
```python
import functools

import jax
import jax.numpy as jnp
from jax import lax
from jax.experimental import pallas as pl
from jax.experimental.pallas import tpu as pltpu
from jax.sharding import PartitionSpec as P

CHUNK = 8
PAD = 8
VMEM_BYTES = 48 * 1024 * 1024


def whole(space):
    return pl.BlockSpec(memory_space=space)


def split_bf16(value):
    high = value.astype(jnp.bfloat16)
    low = (value - high.astype(jnp.float32)).astype(jnp.bfloat16)
    return high, low


def matmul_f32(left, right):
    left_high, left_low = split_bf16(left)
    right_high, right_low = split_bf16(right)
    dot = functools.partial(jnp.dot, preferred_element_type=jnp.float32)
    return dot(left_high, right_high) + dot(left_high, right_low) + dot(left_low, right_high)


def combine_kernel(
    dst_ref, src_ref, count_ref, adj_ref, x_ref, ws_ref, b_ref,
    a_ref, deg_ref, own_ref, held, sems,
):
    maxt, tile = adj_ref.shape[0], adj_ref.shape[1]
    n_src, n_dst = a_ref.shape[0], a_ref.shape[1] // tile
    copies = []
    for first in range(0, maxt, CHUNK):
        part = pl.ds(first, CHUNK)
        copy = pltpu.make_async_copy(adj_ref.at[part], held.at[part], sems.at[first // CHUNK])
        copy.start()
        copies.append(copy)

    def clear(s, carry):
        a_ref[s] = jnp.zeros(a_ref.shape[1:], a_ref.dtype)
        return carry

    lax.fori_loop(0, n_src, clear, 0)
    own_ref[...] = matmul_f32(x_ref[...], ws_ref[...]) + b_ref[...]
    count = count_ref[0]

    def add_tile(k, carry):
        rows = pl.ds(pl.multiple_of(dst_ref[k] * tile, tile), tile)
        source = src_ref[k]
        a_ref[source, rows, :] = a_ref[source, rows, :] + held[k]
        return carry

    for index, copy in enumerate(copies):
        copy.wait()
        first = index * CHUNK
        lax.fori_loop(first, jnp.minimum(first + CHUNK, count), add_tile, 0)

    ones = jnp.ones((PAD, tile), jnp.bfloat16)

    def row_sums(d, carry):
        rows = pl.ds(pl.multiple_of(d * tile, tile), tile)

        def add_source(s, total):
            return total + lax.dot_general(
                ones, a_ref[s, rows, :], (((1,), (1,)), ((), ())),
                preferred_element_type=jnp.float32,
            )

        deg_ref[d] = lax.fori_loop(0, n_src, add_source, jnp.zeros((PAD, tile), jnp.float32))
        return carry

    lax.fori_loop(0, n_dst, row_sums, 0)


def combine(adj, dst, src, count, x, ws, b, n_src, n_dst):
    maxt, tile = adj.shape[0], adj.shape[1]
    return pl.pallas_call(
        combine_kernel,
        in_specs=[whole(pltpu.SMEM)] * 3 + [whole(pl.ANY)] + [whole(pltpu.VMEM)] * 3,
        out_specs=[whole(pltpu.VMEM)] * 3,
        out_shape=[
            jax.ShapeDtypeStruct((n_src, n_dst * tile, tile), jnp.bfloat16),
            jax.ShapeDtypeStruct((n_dst, PAD, tile), jnp.float32),
            jax.ShapeDtypeStruct((x.shape[0], ws.shape[1]), jnp.float32),
        ],
        scratch_shapes=[
            pltpu.VMEM(adj.shape, adj.dtype),
            pltpu.SemaphoreType.DMA((maxt // CHUNK,)),
        ],
        compiler_params=pltpu.CompilerParams(vmem_limit_bytes=VMEM_BYTES),
        name="combine_tiles",
    )(dst, src, count, adj, x, ws, b)


def product_rows(place_ref, a_ref, tile_refs, masks, halves, rows):
    total = None
    for index, mask in enumerate(masks):
        a = a_ref[place_ref[1] ^ mask, rows, :]
        term = jnp.dot(
            jnp.concatenate([a, a], axis=1), halves[index], preferred_element_type=jnp.float32
        )
        total = term if total is None else total + term
    return total


def stack_halves(tile_refs, halves):
    tile = tile_refs[0].shape[0]
    for index, ref in enumerate(tile_refs):
        high, low = split_bf16(ref[...])
        halves[index, 0:tile, :] = high
        halves[index, tile:, :] = low


def early_kernel(masks, place_ref, a_ref, *refs):
    tile_refs, acc_ref, halves = refs[: len(masks)], refs[-2], refs[-1]
    tile = tile_refs[0].shape[0]
    stack_halves(tile_refs, halves)

    def visit(d, carry):
        rows = pl.ds(pl.multiple_of(d * tile, tile), tile)
        acc_ref[rows, :] = product_rows(place_ref, a_ref, tile_refs, masks, halves, rows)
        return carry

    lax.fori_loop(0, acc_ref.shape[0] // tile, visit, 0)


def late_kernel(masks, place_ref, a_ref, deg_ref, acc_ref, *refs):
    tile_refs, out_refs, halves = refs[: len(masks)], refs[len(masks) : -1], refs[-1]
    tile, feat = tile_refs[0].shape
    stack_halves(tile_refs, halves)
    for step, out_ref in enumerate(out_refs):
        d = place_ref[0] ^ step
        rows = pl.ds(pl.multiple_of(d * tile, tile), tile)
        out_ref[0:tile, :] = acc_ref[rows, :] + product_rows(
            place_ref, a_ref, tile_refs, masks, halves, rows
        )
        out_ref[tile:, :] = jnp.concatenate([deg_ref[d]] * (feat // tile), axis=1)


def early(place, a, tiles, masks):
    tile, feat = tiles[0].shape
    return pl.pallas_call(
        functools.partial(early_kernel, masks),
        in_specs=[whole(pltpu.SMEM)] + [whole(pltpu.VMEM)] * (1 + len(tiles)),
        out_specs=whole(pltpu.VMEM),
        out_shape=jax.ShapeDtypeStruct((a.shape[1], feat), jnp.float32),
        scratch_shapes=[pltpu.VMEM((len(tiles), 2 * tile, feat), jnp.bfloat16)],
        compiler_params=pltpu.CompilerParams(vmem_limit_bytes=VMEM_BYTES),
        name="early_products",
    )(place, a, *tiles)


def late(place, a, deg, acc, tiles, masks, n_row):
    tile, feat = tiles[0].shape
    return pl.pallas_call(
        functools.partial(late_kernel, masks),
        in_specs=[whole(pltpu.SMEM)] + [whole(pltpu.VMEM)] * (3 + len(tiles)),
        out_specs=[whole(pltpu.VMEM)] * n_row,
        out_shape=[jax.ShapeDtypeStruct((tile + PAD, feat), jnp.float32)] * n_row,
        scratch_shapes=[pltpu.VMEM((len(tiles), 2 * tile, feat), jnp.bfloat16)],
        compiler_params=pltpu.CompilerParams(vmem_limit_bytes=VMEM_BYTES),
        name="late_products",
    )(place, a, deg, acc, *tiles)


def finish_kernel(own_ref, wn_ref, *refs):
    part_refs, out_ref = refs[:-1], refs[-1]
    tile = own_ref.shape[0]
    total = part_refs[0][...]
    for ref in part_refs[1:]:
        total = total + ref[...]
    degree = jnp.broadcast_to(total[tile : tile + 1, 0:tile], (tile, tile)).T
    degree = jnp.maximum(degree, 1.0)
    degree = jnp.concatenate([degree] * (total.shape[1] // tile), axis=1)
    mean = total[0:tile, :] / degree
    out_ref[...] = jnp.maximum(own_ref[...] + matmul_f32(mean, wn_ref[...]), 0.0)


def finish(own, wn, parts):
    return pl.pallas_call(
        finish_kernel,
        in_specs=[whole(pltpu.VMEM)] * (2 + len(parts)),
        out_specs=whole(pltpu.VMEM),
        out_shape=jax.ShapeDtypeStruct(own.shape, jnp.float32),
        compiler_params=pltpu.CompilerParams(vmem_limit_bytes=VMEM_BYTES),
        name="finish_rows",
    )(own, wn, *parts)


def exchange(value, axis, mask):
    pairs = [(i, i ^ mask) for i in range(lax.axis_size(axis))]
    return lax.ppermute(value, axis, pairs)


def on_device(
    features, adj_tiles, tile_dst, tile_src, tile_count, self_weight, neighbor_weight, layer_bias
):
    n_row, n_col = lax.axis_size("row"), lax.axis_size("col")
    tile = adj_tiles.shape[-1]
    assert features.shape[0] == tile and adj_tiles.shape[2] <= 256
    place = jnp.stack([lax.axis_index("row"), lax.axis_index("col")]).astype(jnp.int32)

    tiles = {0: features}
    bit = n_col // 2
    while bit:
        for mask in list(tiles):
            tiles[mask | bit] = exchange(tiles[mask], "col", bit)
        bit //= 2

    a, deg, own = combine(
        adj_tiles[0, 0], tile_dst[0, 0], tile_src[0, 0], tile_count[0], features,
        self_weight, layer_bias[None, :], n_col, n_row,
    )
    first = [m for m in tiles if m % 2 == 0]
    last = [m for m in tiles if m % 2 == 1]
    acc = early(place, a, [tiles[m] for m in first], first)
    parts = late(place, a, deg, acc, [tiles[m] for m in last], last, n_row)
    received = [parts[0]] + [exchange(parts[k], "row", k) for k in range(1, n_row)]
    return finish(own, neighbor_weight, received)


def solution(mesh):
    placed = (
        P(("row", "col"), None),
        P("row", "col", None, None, None),
        P("row", "col", None),
        P("row", "col", None),
        P("row", "col"),
        P(),
        P(),
        P(),
    )
    return jax.shard_map(
        on_device, mesh=mesh, in_specs=placed, out_specs=P(("row", "col"), None), check_vma=False
    )
```

time: 565 us -> 43.3 us (0.08); the launches traced: 557 us -> 43 us
  other arithmetic: 210 us -> 0.08 us
  loops' own time: 183 us -> 0 us
  waiting for transfers between devices: 69.4 us -> 12.5 us
  local copies, waits for them, and re-layouts: 51.2 us -> 5.73 us
  matrix products: 23.1 us -> 0 us
  between operations: 14.2 us -> 0.74 us
  starting transfers between devices: 0.04 us -> 13.4 us
  Pallas kernels: 0 us -> 10.6 us
  blocking collectives: 5.82 us -> 0 us
    another operation x1 -> x0, loops' own time: 183 us -> none  [accumulate(): return lax.fori_loop(0, group_count, visit, state_pair)]
    add x96 -> x0, other arithmetic: 118 us -> none  [visit(): current_deg + live_slots[slot] * row_sums[slot][None]]
    dynamic_update_slice x96 -> x0, other arithmetic: 62.1 us -> none  [visit(): lax.dynamic_update_slice_in_dim(aggregate, current + live_slots[slot] * p...]
    all_gather x1 -> x0, waiting for transfers between devices: 44.4 us -> none  [on_device(): gathered = lax.all_gather(features, 'col', axis=0, tiled=True)]
    psum x1 -> x0, waiting for transfers between devices: 24.3 us -> none  [on_device(): summed_rows, summed_degrees = lax.psum((aggregate, degrees), 'row')]
    dot_general x14 -> x0, matrix products: 23.1 us -> none  [the longest x12 20.9 us: visit(): jnp.einsum('kij,kjf->kif', block_group, source_group, precision=lax.Preci...]
    gather x12 -> x0, local copies, waits for them, and re-layouts: 22 us -> none  [visit(): source_group = jnp.take(source_tiles, source_ids, axis=0)]
    and x12 -> x0, other arithmetic: 16.6 us -> none  [visit(): source_group = jnp.take(source_tiles, source_ids, axis=0)]
  transfers between devices with their start and end apart: 2 -> 10, of which waited for: 2 -> 4; matrix products, arithmetic and copies ran while one was open for 0% -> 0% of each run, Pallas kernels for 0% -> 20%
where the time goes in v1:
time: 43.3 us; the launch traced here: 43 us
  starting transfers between devices  13.4 us (31%)
  waiting for transfers between devices  12.5 us (29%)
  Pallas kernels  10.6 us (24%)
  local copies, waits for them, and re-layouts  5.73 us (13%)
  between operations  0.74 us (2%)
    ppermute x10, starting transfers between devices, exchange(): return lax.ppermute(value, axis, pairs)  13.4 us
    ppermute x10, waiting for transfers between devices, exchange(): return lax.ppermute(value, axis, pairs)  12.5 us
    pallas_call x1, Pallas kernels, combine(): pl.pallas_call(combine_kernel, in_specs=[whole(pltpu.SMEM)] * 3 + [whole(...  7.11 us
    unnamed x16, local copies, waits for them, and re-layouts  5.73 us
    pallas_call x1, Pallas kernels, early(): pl.pallas_call(functools.partial(early_kernel, masks), in_specs=[whole(pl...  1.57 us
    pallas_call x1, Pallas kernels, late(): pl.pallas_call(functools.partial(late_kernel, masks), in_specs=[whole(plt...  1 us
    pallas_call x1, Pallas kernels, finish(): pl.pallas_call(finish_kernel, in_specs=[whole(pltpu.VMEM)] * (2 + len(par...  0.93 us
  transfers between devices with their start and end apart: 10, of which 4 were waited for; matrix products, arithmetic and copies ran while one was open for 0% of the time, Pallas kernels for 20%

profile of v1, /device:TPU:0, one launch (start us, length us, event | category | flops | bytes accessed | tf_op | source)
XLA Modules:
  0.0 43.0 jit_solution(12459384047031257908)
XLA Ops:
  0.0 4.0 %collective-permute-start = (f32[128,256]{1,0:T(8,128)}, f32[128,256]{1,0:T(8,128)S(1)}, u32[]{:S(2)}, u32[]{:S(2)}) collective-permute-start(f32[128,256]{1,0:T(8,128)} %refs_0_.1), channel_id=1, source_target_pairs={{0,4},{1,5},{2,6},{3,7},{4,0},{5,1},{6,2},{7,3},{8,12},{9,13},{10,... | collective-permute-start | bytes 393224 | tf_op jit(solution)/shard_map/ppermute | solution.py:198
  4.0 1.6 %collective-permute-start.1 = (f32[128,256]{1,0:T(8,128)}, f32[128,256]{1,0:T(8,128)S(1)}, u32[]{:S(2)}, u32[]{:S(2)}) collective-permute-start(f32[128,256]{1,0:T(8,128)} %refs_0_.1), channel_id=1, source_target_pairs={{0,2},{1,3},{2,0},{3,1},{4,6},{5,7},{6,4},{7,5},{8,10},{9,11},{10,... | collective-permute-start | bytes 393224 | tf_op jit(solution)/shard_map/ppermute | solution.py:198
  5.6 5.0 %collective-permute-done.refs_1_ = f32[128,256]{1,0:T(8,128)S(1)} collective-permute-done((f32[128,256]{1,0:T(8,128)}, f32[128,256]{1,0:T(8,128)S(1)}, u32[]{:S(2)}, u32[]{:S(2)}) %collective-permute-start) | collective-permute-done | bytes 131104 | tf_op jit(solution)/shard_map/ppermute | solution.py:198
  10.7 0.7 %collective-permute-start.2 = (f32[128,256]{1,0:T(8,128)S(1)}, f32[128,256]{1,0:T(8,128)S(1)}, u32[]{:S(2)}, u32[]{:S(2)}) collective-permute-start(f32[128,256]{1,0:T(8,128)S(1)} %collective-permute-done.refs_1_), channel_id=1, source_target_pairs={{0,2},{1,3},{2,0},{3,1},{4,6},{5,7},{6,4},{7,5},{8,10},{9,11},{10,... | collective-permute-start | bytes 393224 | tf_op jit(solution)/shard_map/ppermute | solution.py:198
  11.4 1.5 %collective-permute-start.3 = (f32[128,256]{1,0:T(8,128)}, f32[128,256]{1,0:T(8,128)S(1)}, u32[]{:S(2)}, u32[]{:S(2)}) collective-permute-start(f32[128,256]{1,0:T(8,128)} %refs_0_.1), channel_id=1, source_target_pairs={{0,1},{1,0},{2,3},{3,2},{4,5},{5,4},{6,7},{7,6},{8,9},{9,8},{10,11... | collective-permute-start | bytes 393224 | tf_op jit(solution)/shard_map/ppermute | solution.py:198
  12.9 0.5 %collective-permute-start.4 = (f32[128,256]{1,0:T(8,128)S(1)}, f32[128,256]{1,0:T(8,128)S(1)}, u32[]{:S(2)}, u32[]{:S(2)}) collective-permute-start(f32[128,256]{1,0:T(8,128)S(1)} %collective-permute-done.refs_1_), channel_id=1, source_target_pairs={{0,1},{1,0},{2,3},{3,2},{4,5},{5,4},{6,7},{7,6},{8,9},{9,8},{10,11... | collective-permute-start | bytes 393224 | tf_op jit(solution)/shard_map/ppermute | solution.py:198
  13.4 0.0 collective-permute-done.1.refs_2_
  13.4 1.5 %collective-permute-start.5 = (f32[128,256]{1,0:T(8,128)S(1)}, f32[128,256]{1,0:T(8,128)S(1)}, u32[]{:S(2)}, u32[]{:S(2)}) collective-permute-start(f32[128,256]{1,0:T(8,128)S(1)} %collective-permute-done.1.refs_2_), channel_id=1, source_target_pairs={{0,1},{1,0},{2,3},{3,2},{4,5},{5,4},{6,7},{7,6},{8,9},{9,8},{10,11... | collective-permute-start | bytes 393224 | tf_op jit(solution)/shard_map/ppermute | solution.py:198
  14.9 0.7 %collective-permute-done.2.refs_3_ = f32[128,256]{1,0:T(8,128)S(1)} collective-permute-done((f32[128,256]{1,0:T(8,128)S(1)}, f32[128,256]{1,0:T(8,128)S(1)}, u32[]{:S(2)}, u32[]{:S(2)}) %collective-permute-start.2) | collective-permute-done | bytes 131104 | tf_op jit(solution)/shard_map/ppermute | solution.py:198
  15.6 1.6 %collective-permute-start.6 = (f32[128,256]{1,0:T(8,128)S(1)}, f32[128,256]{1,0:T(8,128)S(1)}, u32[]{:S(2)}, u32[]{:S(2)}) collective-permute-start(f32[128,256]{1,0:T(8,128)S(1)} %collective-permute-done.2.refs_3_), channel_id=1, source_target_pairs={{0,1},{1,0},{2,3},{3,2},{4,5},{5,4},{6,7},{7,6},{8,9},{9,8},{10,11... | collective-permute-start | bytes 393224 | tf_op jit(solution)/shard_map/ppermute | solution.py:198
  17.8 0.0 copy-start
  17.9 1.9 %copy-done = bf16[1,1,96,128,128]{4,3,2,1,0:T(8,128)(2,1)S(1)} copy-done((bf16[1,1,96,128,128]{4,3,2,1,0:T(8,128)(2,1)S(1)}, bf16[1,1,96,128,128]{4,3,2,1,0:T(8,128)(2,1)}, u32[]{:S(2)}) %copy-start) | copy-done | bytes 3145752
  19.7 0.0 copy-start.1
  19.7 0.9 %copy-done.1 = f32[128,256]{1,0:T(8,128)S(1)} copy-done((f32[128,256]{1,0:T(8,128)S(1)}, f32[128,256]{1,0:T(8,128)}, u32[]{:S(2)}) %copy-start.1) | copy-done | bytes 131096
  20.6 0.0 copy-start.3
  20.6 0.9 %copy-done.3 = f32[256,256]{1,0:T(8,128)S(1)} copy-done((f32[256,256]{1,0:T(8,128)S(1)}, f32[256,256]{1,0:T(8,128)}, u32[]{:S(2)}) %copy-start.3) | copy-done | bytes 262168
  21.6 0.0 copy-start.5
  21.6 0.7 %copy-done.5 = f32[256]{0:T(256)S(1)} copy-done((f32[256]{0:T(256)S(1)}, f32[256]{0:T(256)}, u32[]{:S(2)}) %copy-start.5) | copy-done | bytes 1048
  22.3 0.0 copy-start.6
  22.3 0.7 %copy-done.6 = s32[1,1,96]{2,1,0:T(1,128)S(1)} copy-done((s32[1,1,96]{2,1,0:T(1,128)S(1)}, s32[1,1,96]{2,1,0:T(1,128)}, u32[]{:S(2)}) %copy-start.6) | copy-done | bytes 408
  22.9 0.0 copy-start.7
  22.9 0.7 %copy-done.7 = s32[1,1,96]{2,1,0:T(1,128)S(1)} copy-done((s32[1,1,96]{2,1,0:T(1,128)S(1)}, s32[1,1,96]{2,1,0:T(1,128)}, u32[]{:S(2)}) %copy-start.7) | copy-done | bytes 408
  23.6 0.0 copy-start.2
  23.6 0.0 copy-start.4
  23.6 7.1 %combine_tiles.1 = (bf16[8,512,128]{2,1,0:T(8,128)(2,1)S(1)}, f32[4,8,128]{2,1,0:T(8,128)S(1)}, f32[128,256]{1,0:T(8,128)S(1)}) custom-call(s32[96]{0:T(128)S(1)} %bitcast.10, s32[96]{0:T(128)S(1)} %bitcast.11, s32[1]{0:T(128)} %bitcast.7.count_ref, bf16[96,128,128]{2,1,0:T(8,128)(2,1)S(1)} %bitcast.8, f32[128,256]{1,0:T(8,128)S(1)} %copy-done.1, ...), custom_call_target="tpu_custom_call" | custom-call | tf_op jit(solution)/shard_map/combine_tiles/pallas_call | solution.py:83
  30.7 0.1 pad_add_fusion.place_ref
  30.8 0.0 copy-done.2
  30.8 1.6 %early_products.1.acc_ref = f32[512,256]{1,0:T(8,128)S(1)} custom-call(s32[2]{0:T(128)S(1)} %pad_add_fusion.place_ref, bf16[8,512,128]{2,1,0:T(8,128)(2,1)S(1)} %get-tuple-element.13.a_ref, f32[128,256]{1,0:T(8,128)S(1)} %copy-done.2, f32[128,256]{1,0:T(8,128)S(1)} %collective-permute-done.refs_1_, f32[128,256]{1,0:T(8,128)S(1)} %collective-permute-done.1.refs_2_, ...), custom_call_target="tpu_custom_call" | custom-call | tf_op jit(solution)/shard_map/early_products/pallas_call | solution.py:148
  32.4 0.0 collective-permute-done.3.refs_0_
  32.4 0.0 collective-permute-done.5.refs_2_
  32.4 0.0 collective-permute-done.4.refs_1_
  32.4 0.0 collective-permute-done.6.refs_3_
  32.4 1.0 %late_products.1 = (f32[136,256]{1,0:T(8,128)S(1)}, f32[136,256]{1,0:T(8,128)S(1)}, f32[136,256]{1,0:T(8,128)S(1)}, f32[136,256]{1,0:T(8,128)S(1)}) custom-call(s32[2]{0:T(128)S(1)} %pad_add_fusion.place_ref, bf16[8,512,128]{2,1,0:T(8,128)(2,1)S(1)} %get-tuple-element.13.a_ref, f32[4,8,128]{2,1,0:T(8,128)S(1)} %get-tuple-element.14.deg_ref, ...), custom_call_target="tpu_custom_call" | custom-call | tf_op jit(solution)/shard_map/late_products/pallas_call | solution.py:161
  33.4 0.1 collective-permute-start.7
  33.5 1.0 %collective-permute-start.8 = (f32[136,256]{1,0:T(8,128)S(1)}, f32[136,256]{1,0:T(8,128)S(1)}, u32[]{:S(2)}, u32[]{:S(2)}) collective-permute-start(f32[136,256]{1,0:T(8,128)S(1)} %get-tuple-element.17), channel_id=1, source_target_pairs={{0,16},{8,24},{16,0},{24,8},{1,17},{9,25},{17,1},{25,9},{2,18},{10... | collective-permute-start | bytes 417800 | tf_op jit(solution)/shard_map/ppermute | solution.py:198
  34.4 0.9 %collective-permute-start.9 = (f32[136,256]{1,0:T(8,128)S(1)}, f32[136,256]{1,0:T(8,128)S(1)}, u32[]{:S(2)}, u32[]{:S(2)}) collective-permute-start(f32[136,256]{1,0:T(8,128)S(1)} %get-tuple-element.18), channel_id=1, source_target_pairs={{0,24},{8,16},{16,8},{24,0},{1,25},{9,17},{17,9},{25,1},{2,26},{10... | collective-permute-start | bytes 417800 | tf_op jit(solution)/shard_map/ppermute | solution.py:198
  35.4 0.0 collective-permute-done.7.refs_1_
  35.4 4.7 %collective-permute-done.8.refs_2_ = f32[136,256]{1,0:T(8,128)S(1)} collective-permute-done((f32[136,256]{1,0:T(8,128)S(1)}, f32[136,256]{1,0:T(8,128)S(1)}, u32[]{:S(2)}, u32[]{:S(2)}) %collective-permute-start.8) | collective-permute-done | bytes 139296 | tf_op jit(solution)/shard_map/ppermute | solution.py:198
  40.0 2.1 %collective-permute-done.9.refs_3_ = f32[136,256]{1,0:T(8,128)S(1)} collective-permute-done((f32[136,256]{1,0:T(8,128)S(1)}, f32[136,256]{1,0:T(8,128)S(1)}, u32[]{:S(2)}, u32[]{:S(2)}) %collective-permute-start.9) | collective-permute-done | bytes 139296 | tf_op jit(solution)/shard_map/ppermute | solution.py:198
  42.1 0.0 copy-done.4
  42.1 0.9 %finish_rows.1 = f32[128,256]{1,0:T(8,128)} custom-call(f32[128,256]{1,0:T(8,128)S(1)} %get-tuple-element.12.own_ref, f32[256,256]{1,0:T(8,128)S(1)} %copy-done.4, f32[136,256]{1,0:T(8,128)S(1)} %get-tuple-element.15.refs_0_, f32[136,256]{1,0:T(8,128)S(1)} %collective-permute-done.7.refs_1_, f32[136,256]{1,0:T(8,128)S(1)} %collective-permute-done.8.refs_2_, ...), custom_call_target="tpu_custom_call" | custom-call | tf_op jit(solution)/shard_map/finish_rows/pallas_call | solution.py:186
Async XLA Ops:
  0.0 10.7 %collective-permute-start = (f32[128,256]{1,0:T(8,128)}, f32[128,256]{1,0:T(8,128)S(1)}, u32[]{:S(2)}, u32[]{:S(2)}) collective-permute-start(f32[128,256]{1,0:T(8,128)} %refs_0_.1), channel_id=1, source_target_pairs={{0,4},{1,5},{2,6},{3,7},{4,0},{5,1},{6,2},{7,3},{8,12},{9,13},{10,... | collective-permute-start | bytes 393224 | tf_op jit(solution)/shard_map/ppermute | solution.py:198
  4.0 9.4 %collective-permute-start.1 = (f32[128,256]{1,0:T(8,128)}, f32[128,256]{1,0:T(8,128)S(1)}, u32[]{:S(2)}, u32[]{:S(2)}) collective-permute-start(f32[128,256]{1,0:T(8,128)} %refs_0_.1), channel_id=1, source_target_pairs={{0,2},{1,3},{2,0},{3,1},{4,6},{5,7},{6,4},{7,5},{8,10},{9,11},{10,... | collective-permute-start | bytes 393224 | tf_op jit(solution)/shard_map/ppermute | solution.py:198
  10.7 5.0 %collective-permute-start.2 = (f32[128,256]{1,0:T(8,128)S(1)}, f32[128,256]{1,0:T(8,128)S(1)}, u32[]{:S(2)}, u32[]{:S(2)}) collective-permute-start(f32[128,256]{1,0:T(8,128)S(1)} %collective-permute-done.refs_1_), channel_id=1, source_target_pairs={{0,2},{1,3},{2,0},{3,1},{4,6},{5,7},{6,4},{7,5},{8,10},{9,11},{10,... | collective-permute-start | bytes 393224 | tf_op jit(solution)/shard_map/ppermute | solution.py:198
  11.4 21.0 %collective-permute-start.3 = (f32[128,256]{1,0:T(8,128)}, f32[128,256]{1,0:T(8,128)S(1)}, u32[]{:S(2)}, u32[]{:S(2)}) collective-permute-start(f32[128,256]{1,0:T(8,128)} %refs_0_.1), channel_id=1, source_target_pairs={{0,1},{1,0},{2,3},{3,2},{4,5},{5,4},{6,7},{7,6},{8,9},{9,8},{10,11... | collective-permute-start | bytes 393224 | tf_op jit(solution)/shard_map/ppermute | solution.py:198
  12.9 19.5 %collective-permute-start.4 = (f32[128,256]{1,0:T(8,128)S(1)}, f32[128,256]{1,0:T(8,128)S(1)}, u32[]{:S(2)}, u32[]{:S(2)}) collective-permute-start(f32[128,256]{1,0:T(8,128)S(1)} %collective-permute-done.refs_1_), channel_id=1, source_target_pairs={{0,1},{1,0},{2,3},{3,2},{4,5},{5,4},{6,7},{7,6},{8,9},{9,8},{10,11... | collective-permute-start | bytes 393224 | tf_op jit(solution)/shard_map/ppermute | solution.py:198
  13.4 19.0 %collective-permute-start.5 = (f32[128,256]{1,0:T(8,128)S(1)}, f32[128,256]{1,0:T(8,128)S(1)}, u32[]{:S(2)}, u32[]{:S(2)}) collective-permute-start(f32[128,256]{1,0:T(8,128)S(1)} %collective-permute-done.1.refs_2_), channel_id=1, source_target_pairs={{0,1},{1,0},{2,3},{3,2},{4,5},{5,4},{6,7},{7,6},{8,9},{9,8},{10,11... | collective-permute-start | bytes 393224 | tf_op jit(solution)/shard_map/ppermute | solution.py:198
  15.6 16.8 %collective-permute-start.6 = (f32[128,256]{1,0:T(8,128)S(1)}, f32[128,256]{1,0:T(8,128)S(1)}, u32[]{:S(2)}, u32[]{:S(2)}) collective-permute-start(f32[128,256]{1,0:T(8,128)S(1)} %collective-permute-done.2.refs_3_), channel_id=1, source_target_pairs={{0,1},{1,0},{2,3},{3,2},{4,5},{5,4},{6,7},{7,6},{8,9},{9,8},{10,11... | collective-permute-start | bytes 393224 | tf_op jit(solution)/shard_map/ppermute | solution.py:198
  17.8 1.9 %copy-start = (bf16[1,1,96,128,128]{4,3,2,1,0:T(8,128)(2,1)S(1)}, bf16[1,1,96,128,128]{4,3,2,1,0:T(8,128)(2,1)}, u32[]{:S(2)}) copy-start(bf16[1,1,96,128,128]{4,3,2,1,0:T(8,128)(2,1)} %param.9) | copy-start | bytes 9437188
  19.7 0.9 %copy-start.1 = (f32[128,256]{1,0:T(8,128)S(1)}, f32[128,256]{1,0:T(8,128)}, u32[]{:S(2)}) copy-start(f32[128,256]{1,0:T(8,128)} %refs_0_.1) | copy-start | bytes 393220
  20.6 0.9 %copy-start.3 = (f32[256,256]{1,0:T(8,128)S(1)}, f32[256,256]{1,0:T(8,128)}, u32[]{:S(2)}) copy-start(f32[256,256]{1,0:T(8,128)} %ws_ref.1) | copy-start | bytes 786436
  21.6 0.7 %copy-start.5 = (f32[256]{0:T(256)S(1)}, f32[256]{0:T(256)}, u32[]{:S(2)}) copy-start(f32[256]{0:T(256)} %param.15) | copy-start | bytes 3076
  22.3 0.7 %copy-start.6 = (s32[1,1,96]{2,1,0:T(1,128)S(1)}, s32[1,1,96]{2,1,0:T(1,128)}, u32[]{:S(2)}) copy-start(s32[1,1,96]{2,1,0:T(1,128)} %param.10) | copy-start | bytes 1156
  22.9 0.7 %copy-start.7 = (s32[1,1,96]{2,1,0:T(1,128)S(1)}, s32[1,1,96]{2,1,0:T(1,128)}, u32[]{:S(2)}) copy-start(s32[1,1,96]{2,1,0:T(1,128)} %param.11) | copy-start | bytes 1156
  23.6 7.2 %copy-start.2 = (f32[128,256]{1,0:T(8,128)S(1)}, f32[128,256]{1,0:T(8,128)}, u32[]{:S(2)}) copy-start(f32[128,256]{1,0:T(8,128)} %refs_0_.1) | copy-start | bytes 393220
  23.6 18.5 %copy-start.4 = (f32[256,256]{1,0:T(8,128)S(1)}, f32[256,256]{1,0:T(8,128)}, u32[]{:S(2)}) copy-start(f32[256,256]{1,0:T(8,128)} %wn_ref.1) | copy-start | bytes 786436
  33.4 1.9 %collective-permute-start.7 = (f32[136,256]{1,0:T(8,128)S(1)}, f32[136,256]{1,0:T(8,128)S(1)}, u32[]{:S(2)}, u32[]{:S(2)}) collective-permute-start(f32[136,256]{1,0:T(8,128)S(1)} %get-tuple-element.16), channel_id=1, source_target_pairs={{0,8},{8,0},{16,24},{24,16},{1,9},{9,1},{17,25},{25,17},{2,10},{10... | collective-permute-start | bytes 417800 | tf_op jit(solution)/shard_map/ppermute | solution.py:198
  33.5 6.5 %collective-permute-start.8 = (f32[136,256]{1,0:T(8,128)S(1)}, f32[136,256]{1,0:T(8,128)S(1)}, u32[]{:S(2)}, u32[]{:S(2)}) collective-permute-start(f32[136,256]{1,0:T(8,128)S(1)} %get-tuple-element.17), channel_id=1, source_target_pairs={{0,16},{8,24},{16,0},{24,8},{1,17},{9,25},{17,1},{25,9},{2,18},{10... | collective-permute-start | bytes 417800 | tf_op jit(solution)/shard_map/ppermute | solution.py:198
  34.4 7.7 %collective-permute-start.9 = (f32[136,256]{1,0:T(8,128)S(1)}, f32[136,256]{1,0:T(8,128)S(1)}, u32[]{:S(2)}, u32[]{:S(2)}) collective-permute-start(f32[136,256]{1,0:T(8,128)S(1)} %get-tuple-element.18), channel_id=1, source_target_pairs={{0,24},{8,16},{16,8},{24,0},{1,25},{9,17},{17,9},{25,1},{2,26},{10... | collective-permute-start | bytes 417800 | tf_op jit(solution)/shard_map/ppermute | solution.py:198

commit v2 on v1

v2 whole, which is shorter than its diff:
```python
import functools

import jax
import jax.numpy as jnp
from jax import lax
from jax.experimental import pallas as pl
from jax.experimental.pallas import tpu as pltpu
from jax.sharding import PartitionSpec as P

CHUNK = 8
PAD = 8
VMEM_BYTES = 32 * 1024 * 1024
COMBINE_VMEM = 51 * 1024 * 1024


def whole(space):
    return pl.BlockSpec(memory_space=space)


def split_bf16(value):
    high = value.astype(jnp.bfloat16)
    low = (value - high.astype(jnp.float32)).astype(jnp.bfloat16)
    return high, low


def matmul_f32(left, right):
    left_high, left_low = split_bf16(left)
    right_high, right_low = split_bf16(right)
    dot = functools.partial(jnp.dot, preferred_element_type=jnp.float32)
    return dot(left_high, right_high) + dot(left_high, right_low) + dot(left_low, right_high)


def combine_kernel(lists_hbm, adj_hbm, a_ref, deg_ref, lists_ref, held, list_sem, sems):
    maxt, tile = held.shape[0], held.shape[1]
    n_src, n_dst = a_ref.shape[0], a_ref.shape[1] // tile
    lists = pltpu.make_async_copy(lists_hbm, lists_ref, list_sem)
    lists.start()
    blocks = []
    for first in range(0, maxt, CHUNK):
        part = pl.ds(first, CHUNK)
        copy = pltpu.make_async_copy(
            adj_hbm.at[0, 0, part], held.at[part], sems.at[first // CHUNK]
        )
        copy.start()
        blocks.append(copy)

    def clear(s, carry):
        a_ref[s] = jnp.zeros(a_ref.shape[1:], a_ref.dtype)
        return carry

    lax.fori_loop(0, n_src, clear, 0)
    lists.wait()
    count = lists_ref[2 * maxt]

    def add_tile(k, carry):
        rows = pl.ds(pl.multiple_of(lists_ref[k] * tile, tile), tile)
        source = lists_ref[maxt + k]
        a_ref[source, rows, :] = a_ref[source, rows, :] + held[k]
        return carry

    for index, copy in enumerate(blocks):
        copy.wait()
        first = index * CHUNK
        lax.fori_loop(first, jnp.minimum(first + CHUNK, count), add_tile, 0)

    ones = jnp.ones((PAD, tile), jnp.bfloat16)

    def row_sums(d, carry):
        rows = pl.ds(pl.multiple_of(d * tile, tile), tile)
        joined = lax.fori_loop(
            1, n_src, lambda s, total: total + a_ref[s, rows, :], a_ref[0, rows, :]
        )
        deg_ref[d] = lax.dot_general(
            ones, joined, (((1,), (1,)), ((), ())), preferred_element_type=jnp.float32
        )
        return carry

    lax.fori_loop(0, n_dst, row_sums, 0)


def combine(adj, dst, src, count, n_src, n_dst):
    maxt, tile = adj.shape[2], adj.shape[3]
    fill = -(2 * maxt + 1) % 128
    lists = jnp.concatenate([dst[0, 0], src[0, 0], count[0], jnp.zeros((fill,), jnp.int32)])
    return pl.pallas_call(
        combine_kernel,
        in_specs=[whole(pltpu.HBM)] * 2,
        out_specs=[whole(pltpu.VMEM)] * 2,
        out_shape=[
            jax.ShapeDtypeStruct((n_src, n_dst * tile, tile), jnp.bfloat16),
            jax.ShapeDtypeStruct((n_dst, PAD, tile), jnp.float32),
        ],
        scratch_shapes=[
            pltpu.SMEM(lists.shape, jnp.int32),
            pltpu.VMEM(adj.shape[2:], adj.dtype),
            pltpu.SemaphoreType.DMA(()),
            pltpu.SemaphoreType.DMA((maxt // CHUNK,)),
        ],
        compiler_params=pltpu.CompilerParams(vmem_limit_bytes=COMBINE_VMEM),
        name="combine_tiles",
    )(lists, adj)


def own_kernel(x_ref, ws_ref, b_ref, own_ref):
    own_ref[...] = matmul_f32(x_ref[...], ws_ref[...]) + b_ref[...][None, :]


def own_rows(x, ws, b):
    return pl.pallas_call(
        own_kernel,
        in_specs=[whole(pltpu.VMEM)] * 3,
        out_specs=whole(pltpu.VMEM),
        out_shape=jax.ShapeDtypeStruct((x.shape[0], ws.shape[1]), jnp.float32),
        compiler_params=pltpu.CompilerParams(vmem_limit_bytes=VMEM_BYTES),
        name="own_rows",
    )(x, ws, b)


def product_rows(a_ref, tile_refs, masks, halves, rows):
    total = None
    for index, mask in enumerate(masks):
        a = a_ref[lax.axis_index("col") ^ mask, rows, :]
        term = jnp.dot(
            jnp.concatenate([a, a], axis=1), halves[index], preferred_element_type=jnp.float32
        )
        total = term if total is None else total + term
    return total


def stack_halves(tile_refs, halves):
    tile = tile_refs[0].shape[0]
    for index, ref in enumerate(tile_refs):
        high, low = split_bf16(ref[...])
        halves[index, 0:tile, :] = high
        halves[index, tile:, :] = low


def early_kernel(masks, a_ref, *refs):
    tile_refs, acc_ref, halves = refs[: len(masks)], refs[-2], refs[-1]
    tile = tile_refs[0].shape[0]
    stack_halves(tile_refs, halves)

    def visit(d, carry):
        rows = pl.ds(pl.multiple_of(d * tile, tile), tile)
        acc_ref[rows, :] = product_rows(a_ref, tile_refs, masks, halves, rows)
        return carry

    lax.fori_loop(0, acc_ref.shape[0] // tile, visit, 0)


def late_kernel(masks, a_ref, deg_ref, acc_ref, *refs):
    tile_refs, out_refs, halves = refs[: len(masks)], refs[len(masks) : -1], refs[-1]
    tile, feat = tile_refs[0].shape
    stack_halves(tile_refs, halves)
    step = tile + PAD
    for index in range(acc_ref.shape[0] // tile):
        d = lax.axis_index("row") ^ index
        rows = pl.ds(pl.multiple_of(d * tile, tile), tile)
        out_ref, first = out_refs[index % 2], index // 2 * step
        out_ref[first : first + tile, :] = acc_ref[rows, :] + product_rows(
            a_ref, tile_refs, masks, halves, rows
        )
        out_ref[first + tile : first + step, :] = jnp.concatenate(
            [deg_ref[d]] * (feat // tile), axis=1
        )


def fold_kernel(step, keep_ref, came_ref, stay_ref, leave_ref):
    for index in range(keep_ref.shape[0] // step):
        out_ref, first = (stay_ref, leave_ref)[index % 2], index // 2 * step
        rows = slice(index * step, (index + 1) * step)
        out_ref[first : first + step, :] = keep_ref[rows, :] + came_ref[rows, :]


def fold(keep, came, step):
    half = jax.ShapeDtypeStruct((keep.shape[0] // 2, keep.shape[1]), jnp.float32)
    return pl.pallas_call(
        functools.partial(fold_kernel, step),
        in_specs=[whole(pltpu.VMEM)] * 2,
        out_specs=[whole(pltpu.VMEM)] * 2,
        out_shape=[half, half],
        compiler_params=pltpu.CompilerParams(vmem_limit_bytes=VMEM_BYTES),
        name="fold_sums",
    )(keep, came)


def early(a, tiles, masks):
    tile, feat = tiles[0].shape
    return pl.pallas_call(
        functools.partial(early_kernel, masks),
        in_specs=[whole(pltpu.VMEM)] * (1 + len(tiles)),
        out_specs=whole(pltpu.VMEM),
        out_shape=jax.ShapeDtypeStruct((a.shape[1], feat), jnp.float32),
        scratch_shapes=[pltpu.VMEM((len(tiles), 2 * tile, feat), jnp.bfloat16)],
        compiler_params=pltpu.CompilerParams(vmem_limit_bytes=VMEM_BYTES),
        name="early_products",
    )(a, *tiles)


def late(a, deg, acc, tiles, masks, n_row):
    tile, feat = tiles[0].shape
    return pl.pallas_call(
        functools.partial(late_kernel, masks),
        in_specs=[whole(pltpu.VMEM)] * (3 + len(tiles)),
        out_specs=[whole(pltpu.VMEM)] * 2,
        out_shape=[jax.ShapeDtypeStruct((n_row // 2 * (tile + PAD), feat), jnp.float32)] * 2,
        scratch_shapes=[pltpu.VMEM((len(tiles), 2 * tile, feat), jnp.bfloat16)],
        compiler_params=pltpu.CompilerParams(vmem_limit_bytes=VMEM_BYTES),
        name="late_products",
    )(a, deg, acc, *tiles)


def finish_kernel(own_ref, wn_ref, *refs):
    part_refs, out_ref = refs[:-1], refs[-1]
    tile = own_ref.shape[0]
    total = part_refs[0][...]
    for ref in part_refs[1:]:
        total = total + ref[...]
    degree = jnp.broadcast_to(total[tile : tile + 1, 0:tile], (tile, tile)).T
    degree = jnp.maximum(degree, 1.0)
    degree = jnp.concatenate([degree] * (total.shape[1] // tile), axis=1)
    mean = total[0:tile, :] / degree
    out_ref[...] = jnp.maximum(own_ref[...] + matmul_f32(mean, wn_ref[...]), 0.0)


def finish(own, wn, parts):
    return pl.pallas_call(
        finish_kernel,
        in_specs=[whole(pltpu.VMEM)] * (2 + len(parts)),
        out_specs=whole(pltpu.VMEM),
        out_shape=jax.ShapeDtypeStruct(own.shape, jnp.float32),
        compiler_params=pltpu.CompilerParams(vmem_limit_bytes=VMEM_BYTES),
        name="finish_rows",
    )(own, wn, *parts)


def exchange(value, axis, mask):
    pairs = [(i, i ^ mask) for i in range(lax.axis_size(axis))]
    return lax.ppermute(value, axis, pairs)


def on_device(
    features, adj_tiles, tile_dst, tile_src, tile_count, self_weight, neighbor_weight, layer_bias
):
    n_row, n_col = lax.axis_size("row"), lax.axis_size("col")
    tile = adj_tiles.shape[-1]
    assert features.shape[0] == tile and adj_tiles.shape[2] <= 256

    a, deg = combine(adj_tiles, tile_dst, tile_src, tile_count, n_col, n_row)
    tiles = {0: features}
    bits = [1 << k for k in reversed(range(1, n_col.bit_length() - 1))]
    for bit in bits:
        tiles[bit] = exchange(features, "col", bit)
    near = exchange(features, "col", 1)
    heads = [tiles[bit] for bit in bits]
    heads, a = lax.optimization_barrier((heads, a))
    tiles.update(zip(bits, heads))
    ready = [0] + bits
    for bit in bits:
        tiles[bit | 1] = exchange(tiles[bit], "col", 1)
    done = [0]
    for bit in bits:
        for mask in done[1:]:
            tiles[mask | bit] = exchange(tiles[mask], "col", bit)
        done = done + [mask | bit for mask in done]
    rest = [m for m in done if m not in ready]
    values = [tiles[m] for m in rest]
    values, near = lax.optimization_barrier((values, near))
    tiles[1] = near
    for mask, value in zip(rest, values):
        tiles[mask] = value
        tiles[mask | 1] = exchange(value, "col", 1)

    first = ready + [1]
    last = [m for m in tiles if m not in first]
    acc = early(a, [tiles[m] for m in first], first)
    own = own_rows(features, self_weight, layer_bias)
    keep, send = late(a, deg, acc, [tiles[m] for m in last], last, n_row)
    bit = 1
    while 2 * bit < n_row:
        keep, send = fold(keep, exchange(send, "row", bit), tile + PAD)
        bit *= 2
    return finish(own, neighbor_weight, [keep, exchange(send, "row", bit)])


def solution(mesh):
    placed = (
        P(("row", "col"), None),
        P("row", "col", None, None, None),
        P("row", "col", None),
        P("row", "col", None),
        P("row", "col"),
        P(),
        P(),
        P(),
    )
    return jax.shard_map(
        on_device, mesh=mesh, in_specs=placed, out_specs=P(("row", "col"), None), check_vma=False
    )
```

time: 43.3 us -> 31.1 us (0.72)
  local copies, waits for them, and re-layouts: 5.73 us -> 0.03 us
  Pallas kernels: 10.6 us -> 5.38 us
  waiting for transfers between devices: 12.5 us -> 11.3 us
  starting transfers between devices: 13.4 us -> 12.7 us
  other arithmetic: 0.08 us -> 0.75 us
    unnamed x16 -> x8, local copies, waits for them, and re-layouts: 5.73 us -> 0.02 us
    pallas_call x1 -> x3, Pallas kernels: 7.11 us -> 3 us  [the longest x1 2.75 us: combine(): pl.pallas_call(combine_kernel, in_specs=[whole(pltpu.HBM)] * 2, out_specs...]
    ppermute x10 -> x9, waiting for transfers between devices: 12.5 us -> 11.3 us  [exchange(): return lax.ppermute(value, axis, pairs)]
    concatenate x0 -> x1, other arithmetic: none -> 0.75 us  [combine(): jnp.concatenate([dst[0, 0], src[0, 0], count[0], jnp.zeros((fill,), jnp.i...]
    ppermute x10 -> x9, starting transfers between devices: 13.4 us -> 12.7 us  [exchange(): return lax.ppermute(value, axis, pairs)]
    pallas_call x1, Pallas kernels: 1.57 us -> 1.01 us  [early(): pl.pallas_call(functools.partial(early_kernel, masks), in_specs=[whole(pl...]
    pallas_call x1, Pallas kernels: 1 us -> 0.45 us  [late(): pl.pallas_call(functools.partial(late_kernel, masks), in_specs=[whole(plt...]
  transfers between devices with their start and end apart: 10 -> 9, of which waited for: 4 -> 6; matrix products, arithmetic and copies ran while one was open for 0% -> 2% of each run, Pallas kernels for 20% -> 13%
where the time goes in v2:
time: 31.1 us; the launch traced here: 31 us
  starting transfers between devices  12.7 us (41%)
  waiting for transfers between devices  11.3 us (36%)
  Pallas kernels  5.38 us (17%)
  other arithmetic  0.75 us (2%)
  between operations  0.75 us (2%)
    ppermute x9, starting transfers between devices, exchange(): return lax.ppermute(value, axis, pairs)  12.7 us
    ppermute x9, waiting for transfers between devices, exchange(): return lax.ppermute(value, axis, pairs)  11.3 us
    pallas_call x1, Pallas kernels, combine(): pl.pallas_call(combine_kernel, in_specs=[whole(pltpu.HBM)] * 2, out_specs...  2.75 us
    pallas_call x1, Pallas kernels, early(): pl.pallas_call(functools.partial(early_kernel, masks), in_specs=[whole(pl...  1.01 us
    pallas_call x1, Pallas kernels, finish(): pl.pallas_call(finish_kernel, in_specs=[whole(pltpu.VMEM)] * (2 + len(par...  0.92 us
    concatenate x1, other arithmetic, combine(): jnp.concatenate([dst[0, 0], src[0, 0], count[0], jnp.zeros((fill,), jnp.i...  0.75 us
  transfers between devices with their start and end apart: 9, of which 6 were waited for; matrix products, arithmetic and copies ran while one was open for 2% of the time, Pallas kernels for 13%

profile of v2, /device:TPU:0, one launch (start us, length us, event | category | flops | bytes accessed | tf_op | source)
XLA Modules:
  0.0 31.0 jit_solution(14874971633121700067)
XLA Ops:
  0.0 0.0 copy-start
  0.0 4.0 %collective-permute-start = (f32[128,256]{1,0:T(8,128)}, f32[128,256]{1,0:T(8,128)S(1)}, u32[]{:S(2)}, u32[]{:S(2)}) collective-permute-start(f32[128,256]{1,0:T(8,128)} %refs_0_.1), channel_id=1, source_target_pairs={{0,4},{1,5},{2,6},{3,7},{4,0},{5,1},{6,2},{7,3},{8,12},{9,13},{10,... | collective-permute-start | bytes 393224 | tf_op jit(solution)/shard_map/ppermute | solution.py:239
  4.0 1.6 %collective-permute-start.1 = (f32[128,256]{1,0:T(8,128)}, f32[128,256]{1,0:T(8,128)S(1)}, u32[]{:S(2)}, u32[]{:S(2)}) collective-permute-start(f32[128,256]{1,0:T(8,128)} %refs_0_.1), channel_id=1, source_target_pairs={{0,2},{1,3},{2,0},{3,1},{4,6},{5,7},{6,4},{7,5},{8,10},{9,11},{10,... | collective-permute-start | bytes 393224 | tf_op jit(solution)/shard_map/ppermute | solution.py:239
  5.6 1.5 %collective-permute-start.3 = (f32[128,256]{1,0:T(8,128)}, f32[128,256]{1,0:T(8,128)S(1)}, u32[]{:S(2)}, u32[]{:S(2)}) collective-permute-start(f32[128,256]{1,0:T(8,128)} %refs_0_.1), channel_id=1, source_target_pairs={{0,1},{1,0},{2,3},{3,2},{4,5},{5,4},{6,7},{7,6},{8,9},{9,8},{10,11... | collective-permute-start | bytes 393224 | tf_op jit(solution)/shard_map/ppermute | solution.py:239
  7.8 0.8 %pad_add_fusion.lists_hbm = s32[256]{0:T(256)S(1)} fusion(s32[63]{0:T(128)S(1)} %broadcast_in_dim.3, s32[1]{0:T(128)} %bitcast.3, s32[96]{0:T(128)} %bitcast.4, s32[96]{0:T(128)} %bitcast.5), kind=kLoop, calls=%fused_computation | loop fusion | flops 768 | bytes 2048 | tf_op jit(solution)/shard_map/concatenate | solution.py:84
  8.6 2.8 %combine_tiles.1 = (bf16[8,512,128]{2,1,0:T(8,128)(2,1)S(1)}, f32[4,8,128]{2,1,0:T(8,128)S(1)}) custom-call(s32[256]{0:T(256)S(1)} %pad_add_fusion.lists_hbm, bf16[1,1,96,128,128]{4,3,2,1,0:T(8,128)(2,1)} %adj_hbm.1), custom_call_target="tpu_custom_call" | custom-call | tf_op jit(solution)/shard_map/combine_tiles/pallas_call | solution.py:85
  11.3 0.0 copy-start.2
  11.3 0.0 copy-start.3
  11.3 0.0 copy-start.1
  11.3 0.0 collective-permute-done.refs_1_
  11.4 0.0 collective-permute-done.1.refs_2_
  11.4 0.9 %collective-permute-start.2 = (f32[128,256]{1,0:T(8,128)S(1)}, f32[128,256]{1,0:T(8,128)S(1)}, u32[]{:S(2)}, u32[]{:S(2)}) collective-permute-start(f32[128,256]{1,0:T(8,128)S(1)} %collective-permute-done.refs_1_), channel_id=1, source_target_pairs={{0,2},{1,3},{2,0},{3,1},{4,6},{5,7},{6,4},{7,5},{8,10},{9,11},{10,... | collective-permute-start | bytes 393224 | tf_op jit(solution)/shard_map/ppermute | solution.py:239
  12.3 1.5 %collective-permute-start.4 = (f32[128,256]{1,0:T(8,128)S(1)}, f32[128,256]{1,0:T(8,128)S(1)}, u32[]{:S(2)}, u32[]{:S(2)}) collective-permute-start(f32[128,256]{1,0:T(8,128)S(1)} %collective-permute-done.refs_1_), channel_id=1, source_target_pairs={{0,1},{1,0},{2,3},{3,2},{4,5},{5,4},{6,7},{7,6},{8,9},{9,8},{10,11... | collective-permute-start | bytes 393224 | tf_op jit(solution)/shard_map/ppermute | solution.py:239
  13.8 0.5 %collective-permute-start.5 = (f32[128,256]{1,0:T(8,128)S(1)}, f32[128,256]{1,0:T(8,128)S(1)}, u32[]{:S(2)}, u32[]{:S(2)}) collective-permute-start(f32[128,256]{1,0:T(8,128)S(1)} %collective-permute-done.1.refs_2_), channel_id=1, source_target_pairs={{0,1},{1,0},{2,3},{3,2},{4,5},{5,4},{6,7},{7,6},{8,9},{9,8},{10,11... | collective-permute-start | bytes 393224 | tf_op jit(solution)/shard_map/ppermute | solution.py:239
  14.3 0.0 collective-permute-done.3.refs_3_
  14.3 2.1 %collective-permute-done.2.refs_2_ = f32[128,256]{1,0:T(8,128)S(1)} collective-permute-done((f32[128,256]{1,0:T(8,128)S(1)}, f32[128,256]{1,0:T(8,128)S(1)}, u32[]{:S(2)}, u32[]{:S(2)}) %collective-permute-start.2) | collective-permute-done | bytes 131104 | tf_op jit(solution)/shard_map/ppermute | solution.py:239
  16.4 1.0 %collective-permute-start.6 = (f32[128,256]{1,0:T(8,128)S(1)}, f32[128,256]{1,0:T(8,128)S(1)}, u32[]{:S(2)}, u32[]{:S(2)}) collective-permute-start(f32[128,256]{1,0:T(8,128)S(1)} %collective-permute-done.2.refs_2_), channel_id=1, source_target_pairs={{0,1},{1,0},{2,3},{3,2},{4,5},{5,4},{6,7},{7,6},{8,9},{9,8},{10,11... | collective-permute-start | bytes 393224 | tf_op jit(solution)/shard_map/ppermute | solution.py:239
  17.4 0.0 copy-done
  17.4 1.0 %early_products.1.acc_ref = f32[512,256]{1,0:T(8,128)S(1)} custom-call(bf16[8,512,128]{2,1,0:T(8,128)(2,1)S(1)} %get-tuple-element.17.a_ref, f32[128,256]{1,0:T(8,128)S(1)} %copy-done, f32[128,256]{1,0:T(8,128)S(1)} %collective-permute-done.refs_1_, f32[128,256]{1,0:T(8,128)S(1)} %collective-permute-done.1.refs_2_, f32[128,256]{1,0:T(8,128)S(1)} %collective-permute-done.3.refs_3_), custom_call_target="tpu_custom_call" | custom-call | tf_op jit(solution)/shard_map/early_products/pallas_call | solution.py:189
  18.4 0.3 %collective-permute-done.4.refs_0_ = f32[128,256]{1,0:T(8,128)S(1)} collective-permute-done((f32[128,256]{1,0:T(8,128)S(1)}, f32[128,256]{1,0:T(8,128)S(1)}, u32[]{:S(2)}, u32[]{:S(2)}) %collective-permute-start.4) | collective-permute-done | bytes 131104 | tf_op jit(solution)/shard_map/ppermute | solution.py:239
  18.7 2.0 %collective-permute-done.5.refs_1_ = f32[128,256]{1,0:T(8,128)S(1)} collective-permute-done((f32[128,256]{1,0:T(8,128)S(1)}, f32[128,256]{1,0:T(8,128)S(1)}, u32[]{:S(2)}, u32[]{:S(2)}) %collective-permute-start.5) | collective-permute-done | bytes 131104 | tf_op jit(solution)/shard_map/ppermute | solution.py:239
  20.7 1.4 %collective-permute-done.6.refs_3_ = f32[128,256]{1,0:T(8,128)S(1)} collective-permute-done((f32[128,256]{1,0:T(8,128)S(1)}, f32[128,256]{1,0:T(8,128)S(1)}, u32[]{:S(2)}, u32[]{:S(2)}) %collective-permute-start.6) | collective-permute-done | bytes 131104 | tf_op jit(solution)/shard_map/ppermute | solution.py:239
  22.1 0.4 %late_products.1 = (f32[272,256]{1,0:T(8,128)S(1)}, f32[272,256]{1,0:T(8,128)S(1)}) custom-call(bf16[8,512,128]{2,1,0:T(8,128)(2,1)S(1)} %get-tuple-element.17.a_ref, f32[4,8,128]{2,1,0:T(8,128)S(1)} %get-tuple-element.18.deg_ref, f32[512,256]{1,0:T(8,128)S(1)} %early_products.1.acc_ref, f32[128,256]{1,0:T(8,128)S(1)} %collective-permute-done.4.refs_0_, ...), custom_call_target="tpu_custom_call" | custom-call | tf_op jit(solution)/shard_map/late_products/pallas_call | solution.py:202
  22.6 0.1 collective-permute-start.7
  22.7 1.5 %collective-permute-done.7.came_ref = f32[272,256]{1,0:T(8,128)S(1)} collective-permute-done((f32[272,256]{1,0:T(8,128)S(1)}, f32[272,256]{1,0:T(8,128)S(1)}, u32[]{:S(2)}, u32[]{:S(2)}) %collective-permute-start.7) | collective-permute-done | bytes 278560 | tf_op jit(solution)/shard_map/ppermute | solution.py:239
  24.3 1.5 %collective-permute-start.8 = (f32[136,256]{1,0:T(8,128)S(1)}, f32[136,256]{1,0:T(8,128)S(1)}, u32[]{:S(2)}, u32[]{:S(2)}) collective-permute-start(f32[136,256]{1,0:T(8,128)S(1)} %get-tuple-element.26), channel_id=1, source_target_pairs={{0,16},{8,24},{16,0},{24,8},{1,17},{9,25},{17,1},{25,9},{2,18},{10... | collective-permute-start | bytes 417800 | tf_op jit(solution)/shard_map/ppermute | solution.py:239
  25.8 0.0 copy-done.2
  25.8 0.0 copy-done.3
  25.8 0.2 own_rows.1.own_ref
  26.0 4.0 %collective-permute-done.8.refs_1_ = f32[136,256]{1,0:T(8,128)S(1)} collective-permute-done((f32[136,256]{1,0:T(8,128)S(1)}, f32[136,256]{1,0:T(8,128)S(1)}, u32[]{:S(2)}, u32[]{:S(2)}) %collective-permute-start.8) | collective-permute-done | bytes 139296 | tf_op jit(solution)/shard_map/ppermute | solution.py:239
  30.0 0.0 copy-done.1
  30.0 0.9 %finish_rows.1 = f32[128,256]{1,0:T(8,128)} custom-call(f32[128,256]{1,0:T(8,128)S(1)} %own_rows.1.own_ref, f32[256,256]{1,0:T(8,128)S(1)} %copy-done.1, f32[136,256]{1,0:T(8,128)S(1)} %get-tuple-element.25.refs_0_, f32[136,256]{1,0:T(8,128)S(1)} %collective-permute-done.8.refs_1_), custom_call_target="tpu_custom_call" | custom-call | tf_op jit(solution)/shard_map/finish_rows/pallas_call | solution.py:227
  (2 shorter events, 0.0 us)
Async XLA Ops:
  0.0 17.4 %copy-start = (f32[128,256]{1,0:T(8,128)S(1)}, f32[128,256]{1,0:T(8,128)}, u32[]{:S(2)}) copy-start(f32[128,256]{1,0:T(8,128)} %refs_0_.1) | copy-start | bytes 393220
  0.0 11.3 %collective-permute-start = (f32[128,256]{1,0:T(8,128)}, f32[128,256]{1,0:T(8,128)S(1)}, u32[]{:S(2)}, u32[]{:S(2)}) collective-permute-start(f32[128,256]{1,0:T(8,128)} %refs_0_.1), channel_id=1, source_target_pairs={{0,4},{1,5},{2,6},{3,7},{4,0},{5,1},{6,2},{7,3},{8,12},{9,13},{10,... | collective-permute-start | bytes 393224 | tf_op jit(solution)/shard_map/ppermute | solution.py:239
  4.0 7.3 %collective-permute-start.1 = (f32[128,256]{1,0:T(8,128)}, f32[128,256]{1,0:T(8,128)S(1)}, u32[]{:S(2)}, u32[]{:S(2)}) collective-permute-start(f32[128,256]{1,0:T(8,128)} %refs_0_.1), channel_id=1, source_target_pairs={{0,2},{1,3},{2,0},{3,1},{4,6},{5,7},{6,4},{7,5},{8,10},{9,11},{10,... | collective-permute-start | bytes 393224 | tf_op jit(solution)/shard_map/ppermute | solution.py:239
  5.6 8.7 %collective-permute-start.3 = (f32[128,256]{1,0:T(8,128)}, f32[128,256]{1,0:T(8,128)S(1)}, u32[]{:S(2)}, u32[]{:S(2)}) collective-permute-start(f32[128,256]{1,0:T(8,128)} %refs_0_.1), channel_id=1, source_target_pairs={{0,1},{1,0},{2,3},{3,2},{4,5},{5,4},{6,7},{7,6},{8,9},{9,8},{10,11... | collective-permute-start | bytes 393224 | tf_op jit(solution)/shard_map/ppermute | solution.py:239
  11.3 14.5 %copy-start.2 = (f32[256,256]{1,0:T(8,128)S(1)}, f32[256,256]{1,0:T(8,128)}, u32[]{:S(2)}) copy-start(f32[256,256]{1,0:T(8,128)} %ws_ref.1) | copy-start | bytes 786436
  11.3 14.5 %copy-start.3 = (f32[256]{0:T(256)S(1)}, f32[256]{0:T(256)}, u32[]{:S(2)}) copy-start(f32[256]{0:T(256)} %b_ref.1) | copy-start | bytes 3076
  11.3 18.7 %copy-start.1 = (f32[256,256]{1,0:T(8,128)S(1)}, f32[256,256]{1,0:T(8,128)}, u32[]{:S(2)}) copy-start(f32[256,256]{1,0:T(8,128)} %wn_ref.1) | copy-start | bytes 786436
  11.4 5.0 %collective-permute-start.2 = (f32[128,256]{1,0:T(8,128)S(1)}, f32[128,256]{1,0:T(8,128)S(1)}, u32[]{:S(2)}, u32[]{:S(2)}) collective-permute-start(f32[128,256]{1,0:T(8,128)S(1)} %collective-permute-done.refs_1_), channel_id=1, source_target_pairs={{0,2},{1,3},{2,0},{3,1},{4,6},{5,7},{6,4},{7,5},{8,10},{9,11},{10,... | collective-permute-start | bytes 393224 | tf_op jit(solution)/shard_map/ppermute | solution.py:239
  12.3 6.4 %collective-permute-start.4 = (f32[128,256]{1,0:T(8,128)S(1)}, f32[128,256]{1,0:T(8,128)S(1)}, u32[]{:S(2)}, u32[]{:S(2)}) collective-permute-start(f32[128,256]{1,0:T(8,128)S(1)} %collective-permute-done.refs_1_), channel_id=1, source_target_pairs={{0,1},{1,0},{2,3},{3,2},{4,5},{5,4},{6,7},{7,6},{8,9},{9,8},{10,11... | collective-permute-start | bytes 393224 | tf_op jit(solution)/shard_map/ppermute | solution.py:239
  13.8 6.9 %collective-permute-start.5 = (f32[128,256]{1,0:T(8,128)S(1)}, f32[128,256]{1,0:T(8,128)S(1)}, u32[]{:S(2)}, u32[]{:S(2)}) collective-permute-start(f32[128,256]{1,0:T(8,128)S(1)} %collective-permute-done.1.refs_2_), channel_id=1, source_target_pairs={{0,1},{1,0},{2,3},{3,2},{4,5},{5,4},{6,7},{7,6},{8,9},{9,8},{10,11... | collective-permute-start | bytes 393224 | tf_op jit(solution)/shard_map/ppermute | solution.py:239
  16.4 5.7 %collective-permute-start.6 = (f32[128,256]{1,0:T(8,128)S(1)}, f32[128,256]{1,0:T(8,128)S(1)}, u32[]{:S(2)}, u32[]{:S(2)}) collective-permute-start(f32[128,256]{1,0:T(8,128)S(1)} %collective-permute-done.2.refs_2_), channel_id=1, source_target_pairs={{0,1},{1,0},{2,3},{3,2},{4,5},{5,4},{6,7},{7,6},{8,9},{9,8},{10,11... | collective-permute-start | bytes 393224 | tf_op jit(solution)/shard_map/ppermute | solution.py:239
  22.6 1.6 %collective-permute-start.7 = (f32[272,256]{1,0:T(8,128)S(1)}, f32[272,256]{1,0:T(8,128)S(1)}, u32[]{:S(2)}, u32[]{:S(2)}) collective-permute-start(f32[272,256]{1,0:T(8,128)S(1)} %get-tuple-element.24), channel_id=1, source_target_pairs={{0,8},{8,0},{16,24},{24,16},{1,9},{9,1},{17,25},{25,17},{2,10},{10... | collective-permute-start | bytes 835592 | tf_op jit(solution)/shard_map/ppermute | solution.py:239
  24.3 5.8 %collective-permute-start.8 = (f32[136,256]{1,0:T(8,128)S(1)}, f32[136,256]{1,0:T(8,128)S(1)}, u32[]{:S(2)}, u32[]{:S(2)}) collective-permute-start(f32[136,256]{1,0:T(8,128)S(1)} %get-tuple-element.26), channel_id=1, source_target_pairs={{0,16},{8,24},{16,0},{24,8},{1,17},{9,25},{17,1},{25,9},{2,18},{10... | collective-permute-start | bytes 417800 | tf_op jit(solution)/shard_map/ppermute | solution.py:239

commit v3 on v2

--- a/solution.py
+++ b/solution.py
@@ -78,10 +78,8 @@
     lax.fori_loop(0, n_dst, row_sums, 0)
 
 
-def combine(adj, dst, src, count, n_src, n_dst):
+def combine(adj, lists, n_src, n_dst):
     maxt, tile = adj.shape[2], adj.shape[3]
-    fill = -(2 * maxt + 1) % 128
-    lists = jnp.concatenate([dst[0, 0], src[0, 0], count[0], jnp.zeros((fill,), jnp.int32)])
     return pl.pallas_call(
         combine_kernel,
         in_specs=[whole(pltpu.HBM)] * 2,
@@ -234,6 +232,10 @@
     )(own, wn, *parts)
 
 
+def after(value, *earlier):
+    return lax.optimization_barrier((value, *earlier))[0]
+
+
 def exchange(value, axis, mask):
     pairs = [(i, i ^ mask) for i in range(lax.axis_size(axis))]
     return lax.ppermute(value, axis, pairs)
@@ -246,32 +248,27 @@
     tile = adj_tiles.shape[-1]
     assert features.shape[0] == tile and adj_tiles.shape[2] <= 256
 
-    a, deg = combine(adj_tiles, tile_dst, tile_src, tile_count, n_col, n_row)
+    bits = [1 << k for k in reversed(range(1, n_col.bit_length() - 1))]
     tiles = {0: features}
-    bits = [1 << k for k in reversed(range(1, n_col.bit_length() - 1))]
-    for bit in bits:
-        tiles[bit] = exchange(features, "col", bit)
-    near = exchange(features, "col", 1)
-    heads = [tiles[bit] for bit in bits]
-    heads, a = lax.optimization_barrier((heads, a))
-    tiles.update(zip(bits, heads))
-    ready = [0] + bits
-    for bit in bits:
-        tiles[bit | 1] = exchange(tiles[bit], "col", 1)
-    done = [0]
-    for bit in bits:
-        for mask in done[1:]:
-            tiles[mask | bit] = exchange(tiles[mask], "col", bit)
-        done = done + [mask | bit for mask in done]
-    rest = [m for m in done if m not in ready]
-    values = [tiles[m] for m in rest]
-    values, near = lax.optimization_barrier((values, near))
-    tiles[1] = near
-    for mask, value in zip(rest, values):
-        tiles[mask] = value
-        tiles[mask | 1] = exchange(value, "col", 1)
-
-    first = ready + [1]
+    across = n_col - 1
+    for mask in bits + [1, across]:
+        tiles[mask] = exchange(features, "col", mask)
+    fill = -(2 * tile_dst.shape[2] + 1) % 128
+    lists = jnp.concatenate(
+        [tile_dst[0, 0], tile_src[0, 0], tile_count[0], jnp.zeros((fill,), jnp.int32)]
+    )
+    tiles[bits[0]], lists = lax.optimization_barrier((tiles[bits[0]], lists))
+
+    for mask in range(2, n_col):
+        top = 1 << (mask.bit_length() - 1)
+        if mask in tiles:
+            continue
+        if mask % 2:
+            tiles[mask] = exchange(tiles[mask ^ 1], "col", 1)
+        else:
+            tiles[mask] = exchange(tiles[top], "col", mask ^ top)
+    a, deg = combine(adj_tiles, lists, n_col, n_row)
+    first = [0, 1] + bits + [across]
     last = [m for m in tiles if m not in first]
     acc = early(a, [tiles[m] for m in first], first)
     own = own_rows(features, self_weight, layer_bias)

time: 31.1 us -> 29.3 us (0.942)
  starting transfers between devices: 12.7 us -> 10.7 us
    ppermute x9, starting transfers between devices: 12.7 us -> 10.7 us  [exchange(): return lax.ppermute(value, axis, pairs)]
  transfers between devices with their start and end apart: 9 -> 9, of which waited for: 6 -> 6; matrix products, arithmetic and copies ran while one was open for 2% -> 3% of each run, Pallas kernels for 13% -> 14%
where the time goes in v3:
time: 29.3 us; the launch traced here: 29.2 us
  waiting for transfers between devices  11.5 us (39%)
  starting transfers between devices  10.7 us (37%)
  Pallas kernels  5.42 us (18%)
  between operations  0.76 us (3%)
  other arithmetic  0.75 us (3%)
    ppermute x9, waiting for transfers between devices, exchange(): return lax.ppermute(value, axis, pairs)  11.5 us
    ppermute x9, starting transfers between devices, exchange(): return lax.ppermute(value, axis, pairs)  10.7 us
    pallas_call x1, Pallas kernels, combine(): pl.pallas_call(combine_kernel, in_specs=[whole(pltpu.HBM)] * 2, out_specs...  2.75 us
    pallas_call x1, Pallas kernels, early(): pl.pallas_call(functools.partial(early_kernel, masks), in_specs=[whole(pl...  1.13 us
    pallas_call x1, Pallas kernels, finish(): pl.pallas_call(finish_kernel, in_specs=[whole(pltpu.VMEM)] * (2 + len(par...  0.92 us
    concatenate x1, other arithmetic, on_device(): jnp.concatenate([tile_dst[0, 0], tile_src[0, 0], tile_count[0], jnp.zeros...  0.75 us
  transfers between devices with their start and end apart: 9, of which 6 were waited for; matrix products, arithmetic and copies ran while one was open for 3% of the time, Pallas kernels for 14%

profile of v3, /device:TPU:0, one launch (start us, length us, event | category | flops | bytes accessed | tf_op | source)
XLA Modules:
  0.0 29.2 jit_solution(13131180815350442457)
XLA Ops:
  0.0 0.0 copy-start
  0.0 4.0 %collective-permute-start = (f32[128,256]{1,0:T(8,128)}, f32[128,256]{1,0:T(8,128)S(1)}, u32[]{:S(2)}, u32[]{:S(2)}) collective-permute-start(f32[128,256]{1,0:T(8,128)} %refs_0_.1), channel_id=1, source_target_pairs={{0,4},{1,5},{2,6},{3,7},{4,0},{5,1},{6,2},{7,3},{8,12},{9,13},{10,... | collective-permute-start | bytes 393224 | tf_op jit(solution)/shard_map/ppermute | solution.py:241
  4.0 1.6 %collective-permute-start.2 = (f32[128,256]{1,0:T(8,128)}, f32[128,256]{1,0:T(8,128)S(1)}, u32[]{:S(2)}, u32[]{:S(2)}) collective-permute-start(f32[128,256]{1,0:T(8,128)} %refs_0_.1), channel_id=1, source_target_pairs={{0,2},{1,3},{2,0},{3,1},{4,6},{5,7},{6,4},{7,5},{8,10},{9,11},{10,... | collective-permute-start | bytes 393224 | tf_op jit(solution)/shard_map/ppermute | solution.py:241
  5.6 1.5 %collective-permute-start.1 = (f32[128,256]{1,0:T(8,128)}, f32[128,256]{1,0:T(8,128)S(1)}, u32[]{:S(2)}, u32[]{:S(2)}) collective-permute-start(f32[128,256]{1,0:T(8,128)} %refs_0_.1), channel_id=1, source_target_pairs={{0,1},{1,0},{2,3},{3,2},{4,5},{5,4},{6,7},{7,6},{8,9},{9,8},{10,11... | collective-permute-start | bytes 393224 | tf_op jit(solution)/shard_map/ppermute | solution.py:241
  7.1 0.0 collective-permute-start.3
  7.8 0.8 %pad_add_fusion.lists_hbm = s32[256]{0:T(256)S(1)} fusion(s32[63]{0:T(128)S(1)} %broadcast_in_dim.3, s32[1]{0:T(128)} %bitcast.3, s32[96]{0:T(128)} %bitcast.4, s32[96]{0:T(128)} %bitcast.5), kind=kLoop, calls=%fused_computation | loop fusion | flops 768 | bytes 2048 | tf_op jit(solution)/shard_map/concatenate | solution.py:257
  8.6 3.6 %collective-permute-done.refs_2_ = f32[128,256]{1,0:T(8,128)S(1)} collective-permute-done((f32[128,256]{1,0:T(8,128)}, f32[128,256]{1,0:T(8,128)S(1)}, u32[]{:S(2)}, u32[]{:S(2)}) %collective-permute-start) | collective-permute-done | bytes 131104 | tf_op jit(solution)/shard_map/ppermute | solution.py:241
  12.2 2.1 %collective-permute-start.5 = (f32[128,256]{1,0:T(8,128)S(1)}, f32[128,256]{1,0:T(8,128)S(1)}, u32[]{:S(2)}, u32[]{:S(2)}) collective-permute-start(f32[128,256]{1,0:T(8,128)S(1)} %collective-permute-done.refs_2_), channel_id=1, source_target_pairs={{0,1},{1,0},{2,3},{3,2},{4,5},{5,4},{6,7},{7,6},{8,9},{9,8},{10,11... | collective-permute-start | bytes 393224 | tf_op jit(solution)/shard_map/ppermute | solution.py:241
  14.2 0.0 collective-permute-start.6
  14.2 0.0 collective-permute-done.2.refs_3_
  14.2 0.2 collective-permute-start.4
  14.4 2.7 %combine_tiles.1 = (bf16[8,512,128]{2,1,0:T(8,128)(2,1)S(1)}, f32[4,8,128]{2,1,0:T(8,128)S(1)}) custom-call(s32[256]{0:T(256)S(1)} %pad_add_fusion.lists_hbm, bf16[1,1,96,128,128]{4,3,2,1,0:T(8,128)(2,1)} %adj_hbm.1), custom_call_target="tpu_custom_call" | custom-call | tf_op jit(solution)/shard_map/combine_tiles/pallas_call | solution.py:83
  17.2 0.0 copy-start.2
  17.2 0.0 copy-start.3
  17.2 0.0 copy-start.1
  17.2 0.0 collective-permute-done.1.refs_1_
  17.2 0.0 collective-permute-done.3.refs_4_
  17.2 0.0 copy-done
  17.2 1.1 %early_products.1.acc_ref = f32[512,256]{1,0:T(8,128)S(1)} custom-call(bf16[8,512,128]{2,1,0:T(8,128)(2,1)S(1)} %get-tuple-element.14.a_ref, f32[128,256]{1,0:T(8,128)S(1)} %copy-done, f32[128,256]{1,0:T(8,128)S(1)} %collective-permute-done.1.refs_1_, f32[128,256]{1,0:T(8,128)S(1)} %collective-permute-done.refs_2_, ...), custom_call_target="tpu_custom_call" | custom-call | tf_op jit(solution)/shard_map/early_products/pallas_call | solution.py:187
  18.4 0.3 collective-permute-done.5.refs_1_
  18.6 0.6 %collective-permute-done.6.refs_2_ = f32[128,256]{1,0:T(8,128)S(1)} collective-permute-done((f32[128,256]{1,0:T(8,128)S(1)}, f32[128,256]{1,0:T(8,128)S(1)}, u32[]{:S(2)}, u32[]{:S(2)}) %collective-permute-start.6) | collective-permute-done | bytes 131104 | tf_op jit(solution)/shard_map/ppermute | solution.py:241
  19.2 1.3 %collective-permute-done.4.refs_0_ = f32[128,256]{1,0:T(8,128)S(1)} collective-permute-done((f32[128,256]{1,0:T(8,128)S(1)}, f32[128,256]{1,0:T(8,128)S(1)}, u32[]{:S(2)}, u32[]{:S(2)}) %collective-permute-start.4) | collective-permute-done | bytes 131104 | tf_op jit(solution)/shard_map/ppermute | solution.py:241
  20.4 0.4 %late_products.1 = (f32[272,256]{1,0:T(8,128)S(1)}, f32[272,256]{1,0:T(8,128)S(1)}) custom-call(bf16[8,512,128]{2,1,0:T(8,128)(2,1)S(1)} %get-tuple-element.14.a_ref, f32[4,8,128]{2,1,0:T(8,128)S(1)} %get-tuple-element.15.deg_ref, f32[512,256]{1,0:T(8,128)S(1)} %early_products.1.acc_ref, f32[128,256]{1,0:T(8,128)S(1)} %collective-permute-done.4.refs_0_, ...), custom_call_target="tpu_custom_call" | custom-call | tf_op jit(solution)/shard_map/late_products/pallas_call | solution.py:200
  20.8 0.1 collective-permute-start.7
  20.9 1.5 %collective-permute-done.7.came_ref = f32[272,256]{1,0:T(8,128)S(1)} collective-permute-done((f32[272,256]{1,0:T(8,128)S(1)}, f32[272,256]{1,0:T(8,128)S(1)}, u32[]{:S(2)}, u32[]{:S(2)}) %collective-permute-start.7) | collective-permute-done | bytes 278560 | tf_op jit(solution)/shard_map/ppermute | solution.py:241
  22.5 1.3 %collective-permute-start.8 = (f32[136,256]{1,0:T(8,128)S(1)}, f32[136,256]{1,0:T(8,128)S(1)}, u32[]{:S(2)}, u32[]{:S(2)}) collective-permute-start(f32[136,256]{1,0:T(8,128)S(1)} %get-tuple-element.20), channel_id=1, source_target_pairs={{0,16},{8,24},{16,0},{24,8},{1,17},{9,25},{17,1},{25,9},{2,18},{10... | collective-permute-start | bytes 417800 | tf_op jit(solution)/shard_map/ppermute | solution.py:241
  23.7 0.0 copy-done.2
  23.7 0.0 copy-done.3
  23.8 0.2 own_rows.1.own_ref
  24.0 4.3 %collective-permute-done.8.refs_1_ = f32[136,256]{1,0:T(8,128)S(1)} collective-permute-done((f32[136,256]{1,0:T(8,128)S(1)}, f32[136,256]{1,0:T(8,128)S(1)}, u32[]{:S(2)}, u32[]{:S(2)}) %collective-permute-start.8) | collective-permute-done | bytes 139296 | tf_op jit(solution)/shard_map/ppermute | solution.py:241
  28.3 0.0 copy-done.1
  28.3 0.9 %finish_rows.1 = f32[128,256]{1,0:T(8,128)} custom-call(f32[128,256]{1,0:T(8,128)S(1)} %own_rows.1.own_ref, f32[256,256]{1,0:T(8,128)S(1)} %copy-done.1, f32[136,256]{1,0:T(8,128)S(1)} %get-tuple-element.19.refs_0_, f32[136,256]{1,0:T(8,128)S(1)} %collective-permute-done.8.refs_1_), custom_call_target="tpu_custom_call" | custom-call | tf_op jit(solution)/shard_map/finish_rows/pallas_call | solution.py:225
  (2 shorter events, 0.0 us)
Async XLA Ops:
  0.0 17.2 %copy-start = (f32[128,256]{1,0:T(8,128)S(1)}, f32[128,256]{1,0:T(8,128)}, u32[]{:S(2)}) copy-start(f32[128,256]{1,0:T(8,128)} %refs_0_.1) | copy-start | bytes 393220
  0.0 12.2 %collective-permute-start = (f32[128,256]{1,0:T(8,128)}, f32[128,256]{1,0:T(8,128)S(1)}, u32[]{:S(2)}, u32[]{:S(2)}) collective-permute-start(f32[128,256]{1,0:T(8,128)} %refs_0_.1), channel_id=1, source_target_pairs={{0,4},{1,5},{2,6},{3,7},{4,0},{5,1},{6,2},{7,3},{8,12},{9,13},{10,... | collective-permute-start | bytes 393224 | tf_op jit(solution)/shard_map/ppermute | solution.py:241
  4.0 10.2 %collective-permute-start.2 = (f32[128,256]{1,0:T(8,128)}, f32[128,256]{1,0:T(8,128)S(1)}, u32[]{:S(2)}, u32[]{:S(2)}) collective-permute-start(f32[128,256]{1,0:T(8,128)} %refs_0_.1), channel_id=1, source_target_pairs={{0,2},{1,3},{2,0},{3,1},{4,6},{5,7},{6,4},{7,5},{8,10},{9,11},{10,... | collective-permute-start | bytes 393224 | tf_op jit(solution)/shard_map/ppermute | solution.py:241
  5.6 11.6 %collective-permute-start.1 = (f32[128,256]{1,0:T(8,128)}, f32[128,256]{1,0:T(8,128)S(1)}, u32[]{:S(2)}, u32[]{:S(2)}) collective-permute-start(f32[128,256]{1,0:T(8,128)} %refs_0_.1), channel_id=1, source_target_pairs={{0,1},{1,0},{2,3},{3,2},{4,5},{5,4},{6,7},{7,6},{8,9},{9,8},{10,11... | collective-permute-start | bytes 393224 | tf_op jit(solution)/shard_map/ppermute | solution.py:241
  7.1 10.1 %collective-permute-start.3 = (f32[128,256]{1,0:T(8,128)}, f32[128,256]{1,0:T(8,128)S(1)}, u32[]{:S(2)}, u32[]{:S(2)}) collective-permute-start(f32[128,256]{1,0:T(8,128)} %refs_0_.1), channel_id=1, source_target_pairs={{0,7},{1,6},{2,5},{3,4},{4,3},{5,2},{6,1},{7,0},{8,15},{9,14},{10,... | collective-permute-start | bytes 393224 | tf_op jit(solution)/shard_map/ppermute | solution.py:241
  12.2 6.5 %collective-permute-start.5 = (f32[128,256]{1,0:T(8,128)S(1)}, f32[128,256]{1,0:T(8,128)S(1)}, u32[]{:S(2)}, u32[]{:S(2)}) collective-permute-start(f32[128,256]{1,0:T(8,128)S(1)} %collective-permute-done.refs_2_), channel_id=1, source_target_pairs={{0,1},{1,0},{2,3},{3,2},{4,5},{5,4},{6,7},{7,6},{8,9},{9,8},{10,11... | collective-permute-start | bytes 393224 | tf_op jit(solution)/shard_map/ppermute | solution.py:241
  14.2 5.0 %collective-permute-start.6 = (f32[128,256]{1,0:T(8,128)S(1)}, f32[128,256]{1,0:T(8,128)S(1)}, u32[]{:S(2)}, u32[]{:S(2)}) collective-permute-start(f32[128,256]{1,0:T(8,128)S(1)} %collective-permute-done.refs_2_), channel_id=1, source_target_pairs={{0,2},{1,3},{2,0},{3,1},{4,6},{5,7},{6,4},{7,5},{8,10},{9,11},{10,... | collective-permute-start | bytes 393224 | tf_op jit(solution)/shard_map/ppermute | solution.py:241
  14.2 6.2 %collective-permute-start.4 = (f32[128,256]{1,0:T(8,128)S(1)}, f32[128,256]{1,0:T(8,128)S(1)}, u32[]{:S(2)}, u32[]{:S(2)}) collective-permute-start(f32[128,256]{1,0:T(8,128)S(1)} %collective-permute-done.2.refs_3_), channel_id=1, source_target_pairs={{0,1},{1,0},{2,3},{3,2},{4,5},{5,4},{6,7},{7,6},{8,9},{9,8},{10,11... | collective-permute-start | bytes 393224 | tf_op jit(solution)/shard_map/ppermute | solution.py:241
  17.2 6.6 %copy-start.2 = (f32[256,256]{1,0:T(8,128)S(1)}, f32[256,256]{1,0:T(8,128)}, u32[]{:S(2)}) copy-start(f32[256,256]{1,0:T(8,128)} %ws_ref.1) | copy-start | bytes 786436
  17.2 6.6 %copy-start.3 = (f32[256]{0:T(256)S(1)}, f32[256]{0:T(256)}, u32[]{:S(2)}) copy-start(f32[256]{0:T(256)} %b_ref.1) | copy-start | bytes 3076
  17.2 11.1 %copy-start.1 = (f32[256,256]{1,0:T(8,128)S(1)}, f32[256,256]{1,0:T(8,128)}, u32[]{:S(2)}) copy-start(f32[256,256]{1,0:T(8,128)} %wn_ref.1) | copy-start | bytes 786436
  20.8 1.6 %collective-permute-start.7 = (f32[272,256]{1,0:T(8,128)S(1)}, f32[272,256]{1,0:T(8,128)S(1)}, u32[]{:S(2)}, u32[]{:S(2)}) collective-permute-start(f32[272,256]{1,0:T(8,128)S(1)} %get-tuple-element.18), channel_id=1, source_target_pairs={{0,8},{8,0},{16,24},{24,16},{1,9},{9,1},{17,25},{25,17},{2,10},{10... | collective-permute-start | bytes 835592 | tf_op jit(solution)/shard_map/ppermute | solution.py:241
  22.5 5.8 %collective-permute-start.8 = (f32[136,256]{1,0:T(8,128)S(1)}, f32[136,256]{1,0:T(8,128)S(1)}, u32[]{:S(2)}, u32[]{:S(2)}) collective-permute-start(f32[136,256]{1,0:T(8,128)S(1)} %get-tuple-element.20), channel_id=1, source_target_pairs={{0,16},{8,24},{16,0},{24,8},{1,17},{9,25},{17,1},{25,9},{2,18},{10... | collective-permute-start | bytes 417800 | tf_op jit(solution)/shard_map/ppermute | solution.py:241

commit v4 on v3

--- a/solution.py
+++ b/solution.py
@@ -9,6 +9,7 @@
 
 CHUNK = 8
 PAD = 8
+EAGER = 4
 VMEM_BYTES = 32 * 1024 * 1024
 COMBINE_VMEM = 51 * 1024 * 1024
 
@@ -35,14 +36,15 @@
     n_src, n_dst = a_ref.shape[0], a_ref.shape[1] // tile
     lists = pltpu.make_async_copy(lists_hbm, lists_ref, list_sem)
     lists.start()
-    blocks = []
-    for first in range(0, maxt, CHUNK):
-        part = pl.ds(first, CHUNK)
-        copy = pltpu.make_async_copy(
-            adj_hbm.at[0, 0, part], held.at[part], sems.at[first // CHUNK]
-        )
-        copy.start()
-        blocks.append(copy)
+
+    def block(index):
+        part = pl.ds(index * CHUNK, CHUNK)
+        return pltpu.make_async_copy(adj_hbm.at[0, 0, part], held.at[part], sems.at[index])
+
+    chunks = maxt // CHUNK
+    ahead = min(EAGER, chunks)
+    for index in range(ahead):
+        block(index).start()
 
     def clear(s, carry):
         a_ref[s] = jnp.zeros(a_ref.shape[1:], a_ref.dtype)
@@ -51,6 +53,12 @@
     lax.fori_loop(0, n_src, clear, 0)
     lists.wait()
     count = lists_ref[2 * maxt]
+
+    for index in range(ahead, chunks):
+
+        @pl.when(index * CHUNK < count)
+        def _():
+            block(index).start()
 
     def add_tile(k, carry):
         rows = pl.ds(pl.multiple_of(lists_ref[k] * tile, tile), tile)
@@ -58,10 +66,16 @@
         a_ref[source, rows, :] = a_ref[source, rows, :] + held[k]
         return carry
 
-    for index, copy in enumerate(blocks):
-        copy.wait()
+    def add_block(index):
+        block(index).wait()
         first = index * CHUNK
         lax.fori_loop(first, jnp.minimum(first + CHUNK, count), add_tile, 0)
+
+    for index in range(chunks):
+        if index < ahead:
+            add_block(index)
+        else:
+            pl.when(index * CHUNK < count)(functools.partial(add_block, index))
 
     ones = jnp.ones((PAD, tile), jnp.bfloat16)
 
@@ -114,10 +128,14 @@
     )(x, ws, b)
 
 
+def by_core(pair):
+    return pair[0] + lax.rem(lax.axis_index("row"), 2) * (pair[1] - pair[0])
+
+
 def product_rows(a_ref, tile_refs, masks, halves, rows):
     total = None
     for index, mask in enumerate(masks):
-        a = a_ref[lax.axis_index("col") ^ mask, rows, :]
+        a = a_ref[lax.axis_index("col") ^ by_core(mask), rows, :]
         term = jnp.dot(
             jnp.concatenate([a, a], axis=1), halves[index], preferred_element_type=jnp.float32
         )
@@ -135,48 +153,40 @@
 
 def early_kernel(masks, a_ref, *refs):
     tile_refs, acc_ref, halves = refs[: len(masks)], refs[-2], refs[-1]
-    tile = tile_refs[0].shape[0]
     stack_halves(tile_refs, halves)
-
-    def visit(d, carry):
-        rows = pl.ds(pl.multiple_of(d * tile, tile), tile)
+    height = min(acc_ref.shape[0], 512)
+
+    def visit(step, carry):
+        rows = pl.ds(pl.multiple_of(step * height, height), height)
         acc_ref[rows, :] = product_rows(a_ref, tile_refs, masks, halves, rows)
         return carry
 
-    lax.fori_loop(0, acc_ref.shape[0] // tile, visit, 0)
+    lax.fori_loop(0, acc_ref.shape[0] // height, visit, 0)
 
 
 def late_kernel(masks, a_ref, deg_ref, acc_ref, *refs):
     tile_refs, out_refs, halves = refs[: len(masks)], refs[len(masks) : -1], refs[-1]
     tile, feat = tile_refs[0].shape
     stack_halves(tile_refs, halves)
-    step = tile + PAD
-    for index in range(acc_ref.shape[0] // tile):
+    for index, out_ref in enumerate(out_refs):
         d = lax.axis_index("row") ^ index
         rows = pl.ds(pl.multiple_of(d * tile, tile), tile)
-        out_ref, first = out_refs[index % 2], index // 2 * step
-        out_ref[first : first + tile, :] = acc_ref[rows, :] + product_rows(
+        out_ref[0:tile, :] = acc_ref[rows, :] + product_rows(
             a_ref, tile_refs, masks, halves, rows
         )
-        out_ref[first + tile : first + step, :] = jnp.concatenate(
-            [deg_ref[d]] * (feat // tile), axis=1
-        )
-
-
-def fold_kernel(step, keep_ref, came_ref, stay_ref, leave_ref):
-    for index in range(keep_ref.shape[0] // step):
-        out_ref, first = (stay_ref, leave_ref)[index % 2], index // 2 * step
-        rows = slice(index * step, (index + 1) * step)
-        out_ref[first : first + step, :] = keep_ref[rows, :] + came_ref[rows, :]
-
-
-def fold(keep, came, step):
-    half = jax.ShapeDtypeStruct((keep.shape[0] // 2, keep.shape[1]), jnp.float32)
-    return pl.pallas_call(
-        functools.partial(fold_kernel, step),
+        out_ref[tile:, :] = jnp.concatenate([deg_ref[d]] * (feat // tile), axis=1)
+
+
+def fold_kernel(keep_ref, came_ref, out_ref):
+    out_ref[...] = keep_ref[...] + came_ref[...]
+
+
+def fold(keep, came):
+    return pl.pallas_call(
+        fold_kernel,
         in_specs=[whole(pltpu.VMEM)] * 2,
-        out_specs=[whole(pltpu.VMEM)] * 2,
-        out_shape=[half, half],
+        out_specs=whole(pltpu.VMEM),
+        out_shape=jax.ShapeDtypeStruct(keep.shape, jnp.float32),
         compiler_params=pltpu.CompilerParams(vmem_limit_bytes=VMEM_BYTES),
         name="fold_sums",
     )(keep, came)
@@ -200,8 +210,8 @@
     return pl.pallas_call(
         functools.partial(late_kernel, masks),
         in_specs=[whole(pltpu.VMEM)] * (3 + len(tiles)),
-        out_specs=[whole(pltpu.VMEM)] * 2,
-        out_shape=[jax.ShapeDtypeStruct((n_row // 2 * (tile + PAD), feat), jnp.float32)] * 2,
+        out_specs=[whole(pltpu.VMEM)] * n_row,
+        out_shape=[jax.ShapeDtypeStruct((tile + PAD, feat), jnp.float32)] * n_row,
         scratch_shapes=[pltpu.VMEM((len(tiles), 2 * tile, feat), jnp.bfloat16)],
         compiler_params=pltpu.CompilerParams(vmem_limit_bytes=VMEM_BYTES),
         name="late_products",
@@ -210,15 +220,15 @@
 
 def finish_kernel(own_ref, wn_ref, *refs):
     part_refs, out_ref = refs[:-1], refs[-1]
-    tile = own_ref.shape[0]
+    tile, width = own_ref.shape
     total = part_refs[0][...]
     for ref in part_refs[1:]:
         total = total + ref[...]
     degree = jnp.broadcast_to(total[tile : tile + 1, 0:tile], (tile, tile)).T
-    degree = jnp.maximum(degree, 1.0)
-    degree = jnp.concatenate([degree] * (total.shape[1] // tile), axis=1)
-    mean = total[0:tile, :] / degree
-    out_ref[...] = jnp.maximum(own_ref[...] + matmul_f32(mean, wn_ref[...]), 0.0)
+    scale = 1.0 / jnp.maximum(degree, 1.0)
+    scale = jnp.concatenate([scale] * (width // tile), axis=1)
+    product = matmul_f32(total[0:tile, :], wn_ref[...])
+    out_ref[...] = jnp.maximum(own_ref[...] + product * scale, 0.0)
 
 
 def finish(own, wn, parts):
@@ -236,6 +246,14 @@
     return lax.optimization_barrier((value, *earlier))[0]
 
 
+def swap(value, pair):
+    n_row, n_col = lax.axis_size("row"), lax.axis_size("col")
+    pairs = [
+        (r * n_col + c, r * n_col + (c ^ pair[r % 2])) for r in range(n_row) for c in range(n_col)
+    ]
+    return lax.ppermute(value, ("row", "col"), pairs)
+
+
 def exchange(value, axis, mask):
     pairs = [(i, i ^ mask) for i in range(lax.axis_size(axis))]
     return lax.ppermute(value, axis, pairs)
@@ -245,39 +263,35 @@
     features, adj_tiles, tile_dst, tile_src, tile_count, self_weight, neighbor_weight, layer_bias
 ):
     n_row, n_col = lax.axis_size("row"), lax.axis_size("col")
-    tile = adj_tiles.shape[-1]
-    assert features.shape[0] == tile and adj_tiles.shape[2] <= 256
-
-    bits = [1 << k for k in reversed(range(1, n_col.bit_length() - 1))]
-    tiles = {0: features}
-    across = n_col - 1
-    for mask in bits + [1, across]:
-        tiles[mask] = exchange(features, "col", mask)
-    fill = -(2 * tile_dst.shape[2] + 1) % 128
+    tile, maxt = adj_tiles.shape[-1], adj_tiles.shape[2]
+    assert features.shape[0] == tile and maxt <= 256
+    fill = -(2 * maxt + 1) % 128
     lists = jnp.concatenate(
         [tile_dst[0, 0], tile_src[0, 0], tile_count[0], jnp.zeros((fill,), jnp.int32)]
     )
-    tiles[bits[0]], lists = lax.optimization_barrier((tiles[bits[0]], lists))
-
-    for mask in range(2, n_col):
-        top = 1 << (mask.bit_length() - 1)
-        if mask in tiles:
-            continue
-        if mask % 2:
-            tiles[mask] = exchange(tiles[mask ^ 1], "col", 1)
-        else:
-            tiles[mask] = exchange(tiles[top], "col", mask ^ top)
+
+    half = n_col // 2
+    middle = list(range(3, half))
+    pairs = [(half, half)] + list(zip([1] + middle + [2], [2] + middle + [1]))
+    tiles = {pair: swap(features, pair) for pair in pairs}
+    tiles[0, 0] = features
+    first = list(tiles)
+    far, lists = lax.optimization_barrier((tiles[half, half], lists))
     a, deg = combine(adj_tiles, lists, n_col, n_row)
-    first = [0, 1] + bits + [across]
-    last = [m for m in tiles if m not in first]
-    acc = early(a, [tiles[m] for m in first], first)
+    for mask in reversed(range(1, half)):
+        tiles[half + mask, half + mask] = swap(far, (mask, mask))
+    last = [pair for pair in tiles if pair not in first]
+    acc = early(a, [tiles[pair] for pair in first], first)
     own = own_rows(features, self_weight, layer_bias)
-    keep, send = late(a, deg, acc, [tiles[m] for m in last], last, n_row)
-    bit = 1
-    while 2 * bit < n_row:
-        keep, send = fold(keep, exchange(send, "row", bit), tile + PAD)
-        bit *= 2
-    return finish(own, neighbor_weight, [keep, exchange(send, "row", bit)])
+
+    blocks = late(a, deg, acc, [tiles[pair] for pair in last], last, n_row)
+    while len(blocks) > 4:
+        bit = len(blocks) // 2
+        blocks = [fold(blocks[m], exchange(blocks[m | bit], "row", bit)) for m in range(bit)]
+    own_sum, beside, across, both = blocks
+    across = exchange(fold(across, exchange(both, "row", 1)), "row", 2)
+    beside = after(exchange(beside, "row", 1), across)
+    return finish(own, neighbor_weight, [own_sum, beside, across])
 
 
 def solution(mesh):

time: 29.3 us -> 28.5 us (0.973)
  waiting for transfers between devices: 11.5 us -> 7.05 us
  starting transfers between devices: 10.7 us -> 14.6 us
    ppermute x0 -> x7, starting transfers between devices: none -> 12.5 us  [swap(): return lax.ppermute(value, ('row', 'col'), pairs)]
    ppermute x9 -> x3, starting transfers between devices: 10.7 us -> 2.12 us  [exchange(): return lax.ppermute(value, axis, pairs)]
    ppermute x9 -> x3, waiting for transfers between devices: 11.5 us -> 4.84 us  [exchange(): return lax.ppermute(value, axis, pairs)]
    ppermute x0 -> x7, waiting for transfers between devices: none -> 2.21 us  [swap(): return lax.ppermute(value, ('row', 'col'), pairs)]
    pallas_call x1, Pallas kernels: 1.13 us -> 0.52 us  [early(): pl.pallas_call(functools.partial(early_kernel, masks), in_specs=[whole(pl...]
    pallas_call x1, Pallas kernels: 2.75 us -> 3.18 us  [combine(): pl.pallas_call(combine_kernel, in_specs=[whole(pltpu.HBM)] * 2, out_specs...]
  transfers between devices with their start and end apart: 9 -> 10, of which waited for: 6 -> 4; matrix products, arithmetic and copies ran while one was open for 3% -> 3% of each run, Pallas kernels for 14% -> 14%
where the time goes in v4:
time: 28.5 us; the launch traced here: 28.4 us
  starting transfers between devices  14.6 us (51%)
  waiting for transfers between devices  7.05 us (25%)
  Pallas kernels  5.19 us (18%)
  between operations  0.76 us (3%)
  other arithmetic  0.75 us (3%)
    ppermute x7, starting transfers between devices, swap(): return lax.ppermute(value, ('row', 'col'), pairs)  12.5 us
    ppermute x3, waiting for transfers between devices, exchange(): return lax.ppermute(value, axis, pairs)  4.84 us
    pallas_call x1, Pallas kernels, combine(): pl.pallas_call(combine_kernel, in_specs=[whole(pltpu.HBM)] * 2, out_specs...  3.18 us
    ppermute x7, waiting for transfers between devices, swap(): return lax.ppermute(value, ('row', 'col'), pairs)  2.21 us
    ppermute x3, starting transfers between devices, exchange(): return lax.ppermute(value, axis, pairs)  2.12 us
    pallas_call x1, Pallas kernels, finish(): pl.pallas_call(finish_kernel, in_specs=[whole(pltpu.VMEM)] * (2 + len(par...  0.88 us
    concatenate x1, other arithmetic, on_device(): jnp.concatenate([tile_dst[0, 0], tile_src[0, 0], tile_count[0], jnp.zeros...  0.75 us
  transfers between devices with their start and end apart: 10, of which 4 were waited for; matrix products, arithmetic and copies ran while one was open for 3% of the time, Pallas kernels for 14%

profile of v4, /device:TPU:0, one launch (start us, length us, event | category | flops | bytes accessed | tf_op | source)
XLA Modules:
  0.0 28.4 jit_solution(4664809308301414964)
XLA Ops:
  0.0 0.0 copy-start
  0.0 4.0 %collective-permute-start = (f32[128,256]{1,0:T(8,128)}, f32[128,256]{1,0:T(8,128)S(1)}, u32[]{:S(2)}, u32[]{:S(2)}) collective-permute-start(f32[128,256]{1,0:T(8,128)} %refs_4_.1), channel_id=1, source_target_pairs={{0,4},{1,5},{2,6},{3,7},{4,0},{5,1},{6,2},{7,3},{8,12},{9,13},{10,... | collective-permute-start | bytes 393224 | tf_op jit(solution)/shard_map/ppermute | solution.py:254
  4.0 1.5 %collective-permute-start.1 = (f32[128,256]{1,0:T(8,128)}, f32[128,256]{1,0:T(8,128)S(1)}, u32[]{:S(2)}, u32[]{:S(2)}) collective-permute-start(f32[128,256]{1,0:T(8,128)} %refs_4_.1), channel_id=1, source_target_pairs={{0,1},{1,0},{2,3},{3,2},{4,5},{5,4},{6,7},{7,6},{8,10},{9,11},{10,... | collective-permute-start | bytes 393224 | tf_op jit(solution)/shard_map/ppermute | solution.py:254
  5.6 1.5 %collective-permute-start.2 = (f32[128,256]{1,0:T(8,128)}, f32[128,256]{1,0:T(8,128)S(1)}, u32[]{:S(2)}, u32[]{:S(2)}) collective-permute-start(f32[128,256]{1,0:T(8,128)} %refs_4_.1), channel_id=1, source_target_pairs={{0,3},{1,2},{2,1},{3,0},{4,7},{5,6},{6,5},{7,4},{8,11},{9,10},{10,... | collective-permute-start | bytes 393224 | tf_op jit(solution)/shard_map/ppermute | solution.py:254
  7.1 0.4 %collective-permute-start.3 = (f32[128,256]{1,0:T(8,128)}, f32[128,256]{1,0:T(8,128)S(1)}, u32[]{:S(2)}, u32[]{:S(2)}) collective-permute-start(f32[128,256]{1,0:T(8,128)} %refs_4_.1), channel_id=1, source_target_pairs={{0,2},{1,3},{2,0},{3,1},{4,6},{5,7},{6,4},{7,5},{8,9},{9,8},{10,11... | collective-permute-start | bytes 393224 | tf_op jit(solution)/shard_map/ppermute | solution.py:254
  8.2 0.8 %pad_add_fusion.lists_hbm = s32[256]{0:T(256)S(1)} fusion(s32[63]{0:T(128)S(1)} %broadcast_in_dim.3, s32[1]{0:T(128)} %bitcast.3, s32[96]{0:T(128)} %bitcast.4, s32[96]{0:T(128)} %bitcast.5), kind=kLoop, calls=%fused_computation | loop fusion | flops 768 | bytes 2048 | tf_op jit(solution)/shard_map/concatenate | solution.py:269
  8.9 0.0 copy-start.2
  8.9 0.0 copy-start.3
  8.9 1.8 %collective-permute-done.refs_0_ = f32[128,256]{1,0:T(8,128)S(1)} collective-permute-done((f32[128,256]{1,0:T(8,128)}, f32[128,256]{1,0:T(8,128)S(1)}, u32[]{:S(2)}, u32[]{:S(2)}) %collective-permute-start) | collective-permute-done | bytes 131104 | tf_op jit(solution)/shard_map/ppermute | solution.py:254
  10.7 1.7 %collective-permute-start.4 = (f32[128,256]{1,0:T(8,128)S(1)}, f32[128,256]{1,0:T(8,128)S(1)}, u32[]{:S(2)}, u32[]{:S(2)}) collective-permute-start(f32[128,256]{1,0:T(8,128)S(1)} %collective-permute-done.refs_0_), channel_id=1, source_target_pairs={{0,3},{1,2},{2,1},{3,0},{4,7},{5,6},{6,5},{7,4},{8,11},{9,10},{10,... | collective-permute-start | bytes 393224 | tf_op jit(solution)/shard_map/ppermute | solution.py:254
  12.4 1.3 %collective-permute-start.5 = (f32[128,256]{1,0:T(8,128)S(1)}, f32[128,256]{1,0:T(8,128)S(1)}, u32[]{:S(2)}, u32[]{:S(2)}) collective-permute-start(f32[128,256]{1,0:T(8,128)S(1)} %collective-permute-done.refs_0_), channel_id=1, source_target_pairs={{0,2},{1,3},{2,0},{3,1},{4,6},{5,7},{6,4},{7,5},{8,10},{9,11},{10,... | collective-permute-start | bytes 393224 | tf_op jit(solution)/shard_map/ppermute | solution.py:254
  13.7 0.0 collective-permute-done.1.refs_1_
  13.7 2.0 %collective-permute-start.6 = (f32[128,256]{1,0:T(8,128)S(1)}, f32[128,256]{1,0:T(8,128)S(1)}, u32[]{:S(2)}, u32[]{:S(2)}) collective-permute-start(f32[128,256]{1,0:T(8,128)S(1)} %collective-permute-done.refs_0_), channel_id=1, source_target_pairs={{0,1},{1,0},{2,3},{3,2},{4,5},{5,4},{6,7},{7,6},{8,9},{9,8},{10,11... | collective-permute-start | bytes 393224 | tf_op jit(solution)/shard_map/ppermute | solution.py:254
  15.7 3.2 %combine_tiles.1 = (bf16[8,512,128]{2,1,0:T(8,128)(2,1)S(1)}, f32[4,8,128]{2,1,0:T(8,128)S(1)}) custom-call(s32[256]{0:T(256)S(1)} %pad_add_fusion.lists_hbm, bf16[1,1,96,128,128]{4,3,2,1,0:T(8,128)(2,1)} %adj_hbm.1), custom_call_target="tpu_custom_call" | custom-call | tf_op jit(solution)/shard_map/combine_tiles/pallas_call | solution.py:97
  18.8 0.0 copy-start.1
  18.9 0.0 collective-permute-done.2.refs_2_
  18.9 0.0 collective-permute-done.3.refs_3_
  18.9 0.0 copy-done
  18.9 0.5 %early_products.1.acc_ref = f32[512,256]{1,0:T(8,128)S(1)} custom-call(bf16[8,512,128]{2,1,0:T(8,128)(2,1)S(1)} %get-tuple-element.15.a_ref, f32[128,256]{1,0:T(8,128)S(1)} %collective-permute-done.refs_0_, f32[128,256]{1,0:T(8,128)S(1)} %collective-permute-done.1.refs_1_, f32[128,256]{1,0:T(8,128)S(1)} %collective-permute-done.2.refs_2_, ...), custom_call_target="tpu_custom_call" | custom-call | tf_op jit(solution)/shard_map/early_products/pallas_call | solution.py:197
  19.4 0.0 collective-permute-done.4.refs_0_
  19.4 0.4 %collective-permute-done.5.refs_1_ = f32[128,256]{1,0:T(8,128)S(1)} collective-permute-done((f32[128,256]{1,0:T(8,128)S(1)}, f32[128,256]{1,0:T(8,128)S(1)}, u32[]{:S(2)}, u32[]{:S(2)}) %collective-permute-start.5) | collective-permute-done | bytes 131104 | tf_op jit(solution)/shard_map/ppermute | solution.py:254
  19.8 0.0 collective-permute-done.6.refs_2_
  19.9 0.4 %late_products.1 = (f32[136,256]{1,0:T(8,128)S(1)}, f32[136,256]{1,0:T(8,128)S(1)}, f32[136,256]{1,0:T(8,128)S(1)}, f32[136,256]{1,0:T(8,128)S(1)}) custom-call(bf16[8,512,128]{2,1,0:T(8,128)(2,1)S(1)} %get-tuple-element.15.a_ref, f32[4,8,128]{2,1,0:T(8,128)S(1)} %get-tuple-element.16.deg_ref, f32[512,256]{1,0:T(8,128)S(1)} %early_products.1.acc_ref, ...), custom_call_target="tpu_custom_call" | custom-call | tf_op jit(solution)/shard_map/late_products/pallas_call | solution.py:210
  20.2 0.1 collective-permute-start.8
  20.3 0.5 %collective-permute-start.7 = (f32[136,256]{1,0:T(8,128)S(1)}, f32[136,256]{1,0:T(8,128)S(1)}, u32[]{:S(2)}, u32[]{:S(2)}) collective-permute-start(f32[136,256]{1,0:T(8,128)S(1)} %get-tuple-element.19), channel_id=1, source_target_pairs={{0,8},{8,0},{16,24},{24,16},{1,9},{9,1},{17,25},{25,17},{2,10},{10... | collective-permute-start | bytes 417800 | tf_op jit(solution)/shard_map/ppermute | solution.py:259
  20.8 0.8 %collective-permute-done.8.came_ref = f32[136,256]{1,0:T(8,128)S(1)} collective-permute-done((f32[136,256]{1,0:T(8,128)S(1)}, f32[136,256]{1,0:T(8,128)S(1)}, u32[]{:S(2)}, u32[]{:S(2)}) %collective-permute-start.8) | collective-permute-done | bytes 139296 | tf_op jit(solution)/shard_map/ppermute | solution.py:259
  21.7 1.6 %collective-permute-start.9 = (f32[136,256]{1,0:T(8,128)S(1)}, f32[136,256]{1,0:T(8,128)S(1)}, u32[]{:S(2)}, u32[]{:S(2)}) collective-permute-start(f32[136,256]{1,0:T(8,128)S(1)} %fold_sums.1), channel_id=1, source_target_pairs={{0,16},{8,24},{16,0},{24,8},{1,17},{9,25},{17,1},{25,9},{2,18},{10... | collective-permute-start | bytes 417800 | tf_op jit(solution)/shard_map/ppermute | solution.py:259
  23.2 0.0 copy-done.2
  23.2 0.0 copy-done.3
  23.2 0.2 own_rows.1.own_ref
  23.5 0.0 collective-permute-done.7.refs_1_
  23.5 4.0 %collective-permute-done.9.refs_2_ = f32[136,256]{1,0:T(8,128)S(1)} collective-permute-done((f32[136,256]{1,0:T(8,128)S(1)}, f32[136,256]{1,0:T(8,128)S(1)}, u32[]{:S(2)}, u32[]{:S(2)}) %collective-permute-start.9) | collective-permute-done | bytes 139296 | tf_op jit(solution)/shard_map/ppermute | solution.py:259
  27.5 0.0 copy-done.1
  27.5 0.9 %finish_rows.1 = f32[128,256]{1,0:T(8,128)} custom-call(f32[128,256]{1,0:T(8,128)S(1)} %own_rows.1.own_ref, f32[256,256]{1,0:T(8,128)S(1)} %copy-done.1, f32[136,256]{1,0:T(8,128)S(1)} %get-tuple-element.18.refs_0_, f32[136,256]{1,0:T(8,128)S(1)} %collective-permute-done.7.refs_1_, f32[136,256]{1,0:T(8,128)S(1)} %collective-permute-done.9.refs_2_), custom_call_target="tpu_custom_call" | custom-call | tf_op jit(solution)/shard_map/finish_rows/pallas_call | solution.py:235
  (2 shorter events, 0.0 us)
Async XLA Ops:
  0.0 18.9 %copy-start = (f32[128,256]{1,0:T(8,128)S(1)}, f32[128,256]{1,0:T(8,128)}, u32[]{:S(2)}) copy-start(f32[128,256]{1,0:T(8,128)} %refs_4_.1) | copy-start | bytes 393220
  0.0 10.7 %collective-permute-start = (f32[128,256]{1,0:T(8,128)}, f32[128,256]{1,0:T(8,128)S(1)}, u32[]{:S(2)}, u32[]{:S(2)}) collective-permute-start(f32[128,256]{1,0:T(8,128)} %refs_4_.1), channel_id=1, source_target_pairs={{0,4},{1,5},{2,6},{3,7},{4,0},{5,1},{6,2},{7,3},{8,12},{9,13},{10,... | collective-permute-start | bytes 393224 | tf_op jit(solution)/shard_map/ppermute | solution.py:254
  4.0 9.7 %collective-permute-start.1 = (f32[128,256]{1,0:T(8,128)}, f32[128,256]{1,0:T(8,128)S(1)}, u32[]{:S(2)}, u32[]{:S(2)}) collective-permute-start(f32[128,256]{1,0:T(8,128)} %refs_4_.1), channel_id=1, source_target_pairs={{0,1},{1,0},{2,3},{3,2},{4,5},{5,4},{6,7},{7,6},{8,10},{9,11},{10,... | collective-permute-start | bytes 393224 | tf_op jit(solution)/shard_map/ppermute | solution.py:254
  5.6 13.3 %collective-permute-start.2 = (f32[128,256]{1,0:T(8,128)}, f32[128,256]{1,0:T(8,128)S(1)}, u32[]{:S(2)}, u32[]{:S(2)}) collective-permute-start(f32[128,256]{1,0:T(8,128)} %refs_4_.1), channel_id=1, source_target_pairs={{0,3},{1,2},{2,1},{3,0},{4,7},{5,6},{6,5},{7,4},{8,11},{9,10},{10,... | collective-permute-start | bytes 393224 | tf_op jit(solution)/shard_map/ppermute | solution.py:254
  7.1 11.8 %collective-permute-start.3 = (f32[128,256]{1,0:T(8,128)}, f32[128,256]{1,0:T(8,128)S(1)}, u32[]{:S(2)}, u32[]{:S(2)}) collective-permute-start(f32[128,256]{1,0:T(8,128)} %refs_4_.1), channel_id=1, source_target_pairs={{0,2},{1,3},{2,0},{3,1},{4,6},{5,7},{6,4},{7,5},{8,9},{9,8},{10,11... | collective-permute-start | bytes 393224 | tf_op jit(solution)/shard_map/ppermute | solution.py:254
  8.9 14.3 %copy-start.2 = (f32[256,256]{1,0:T(8,128)S(1)}, f32[256,256]{1,0:T(8,128)}, u32[]{:S(2)}) copy-start(f32[256,256]{1,0:T(8,128)} %ws_ref.1) | copy-start | bytes 786436
  8.9 14.3 %copy-start.3 = (f32[256]{0:T(256)S(1)}, f32[256]{0:T(256)}, u32[]{:S(2)}) copy-start(f32[256]{0:T(256)} %b_ref.1) | copy-start | bytes 3076
  10.7 8.7 %collective-permute-start.4 = (f32[128,256]{1,0:T(8,128)S(1)}, f32[128,256]{1,0:T(8,128)S(1)}, u32[]{:S(2)}, u32[]{:S(2)}) collective-permute-start(f32[128,256]{1,0:T(8,128)S(1)} %collective-permute-done.refs_0_), channel_id=1, source_target_pairs={{0,3},{1,2},{2,1},{3,0},{4,7},{5,6},{6,5},{7,4},{8,11},{9,10},{10,... | collective-permute-start | bytes 393224 | tf_op jit(solution)/shard_map/ppermute | solution.py:254
  12.4 7.5 %collective-permute-start.5 = (f32[128,256]{1,0:T(8,128)S(1)}, f32[128,256]{1,0:T(8,128)S(1)}, u32[]{:S(2)}, u32[]{:S(2)}) collective-permute-start(f32[128,256]{1,0:T(8,128)S(1)} %collective-permute-done.refs_0_), channel_id=1, source_target_pairs={{0,2},{1,3},{2,0},{3,1},{4,6},{5,7},{6,4},{7,5},{8,10},{9,11},{10,... | collective-permute-start | bytes 393224 | tf_op jit(solution)/shard_map/ppermute | solution.py:254
  13.7 6.1 %collective-permute-start.6 = (f32[128,256]{1,0:T(8,128)S(1)}, f32[128,256]{1,0:T(8,128)S(1)}, u32[]{:S(2)}, u32[]{:S(2)}) collective-permute-start(f32[128,256]{1,0:T(8,128)S(1)} %collective-permute-done.refs_0_), channel_id=1, source_target_pairs={{0,1},{1,0},{2,3},{3,2},{4,5},{5,4},{6,7},{7,6},{8,9},{9,8},{10,11... | collective-permute-start | bytes 393224 | tf_op jit(solution)/shard_map/ppermute | solution.py:254
  18.8 8.6 %copy-start.1 = (f32[256,256]{1,0:T(8,128)S(1)}, f32[256,256]{1,0:T(8,128)}, u32[]{:S(2)}) copy-start(f32[256,256]{1,0:T(8,128)} %wn_ref.1) | copy-start | bytes 786436
  20.2 1.4 %collective-permute-start.8 = (f32[136,256]{1,0:T(8,128)S(1)}, f32[136,256]{1,0:T(8,128)S(1)}, u32[]{:S(2)}, u32[]{:S(2)}) collective-permute-start(f32[136,256]{1,0:T(8,128)S(1)} %get-tuple-element.21), channel_id=1, source_target_pairs={{0,8},{8,0},{16,24},{24,16},{1,9},{9,1},{17,25},{25,17},{2,10},{10... | collective-permute-start | bytes 417800 | tf_op jit(solution)/shard_map/ppermute | solution.py:259
  20.3 3.2 %collective-permute-start.7 = (f32[136,256]{1,0:T(8,128)S(1)}, f32[136,256]{1,0:T(8,128)S(1)}, u32[]{:S(2)}, u32[]{:S(2)}) collective-permute-start(f32[136,256]{1,0:T(8,128)S(1)} %get-tuple-element.19), channel_id=1, source_target_pairs={{0,8},{8,0},{16,24},{24,16},{1,9},{9,1},{17,25},{25,17},{2,10},{10... | collective-permute-start | bytes 417800 | tf_op jit(solution)/shard_map/ppermute | solution.py:259
  21.7 5.8 %collective-permute-start.9 = (f32[136,256]{1,0:T(8,128)S(1)}, f32[136,256]{1,0:T(8,128)S(1)}, u32[]{:S(2)}, u32[]{:S(2)}) collective-permute-start(f32[136,256]{1,0:T(8,128)S(1)} %fold_sums.1), channel_id=1, source_target_pairs={{0,16},{8,24},{16,0},{24,8},{1,17},{9,25},{17,1},{25,9},{2,18},{10... | collective-permute-start | bytes 417800 | tf_op jit(solution)/shard_map/ppermute | solution.py:259

commit v5 on v4

--- a/solution.py
+++ b/solution.py
@@ -128,14 +128,10 @@
     )(x, ws, b)
 
 
-def by_core(pair):
-    return pair[0] + lax.rem(lax.axis_index("row"), 2) * (pair[1] - pair[0])
-
-
 def product_rows(a_ref, tile_refs, masks, halves, rows):
     total = None
     for index, mask in enumerate(masks):
-        a = a_ref[lax.axis_index("col") ^ by_core(mask), rows, :]
+        a = a_ref[lax.axis_index("col") ^ mask, rows, :]
         term = jnp.dot(
             jnp.concatenate([a, a], axis=1), halves[index], preferred_element_type=jnp.float32
         )
@@ -246,14 +242,6 @@
     return lax.optimization_barrier((value, *earlier))[0]
 
 
-def swap(value, pair):
-    n_row, n_col = lax.axis_size("row"), lax.axis_size("col")
-    pairs = [
-        (r * n_col + c, r * n_col + (c ^ pair[r % 2])) for r in range(n_row) for c in range(n_col)
-    ]
-    return lax.ppermute(value, ("row", "col"), pairs)
-
-
 def exchange(value, axis, mask):
     pairs = [(i, i ^ mask) for i in range(lax.axis_size(axis))]
     return lax.ppermute(value, axis, pairs)
@@ -271,20 +259,23 @@
     )
 
     half = n_col // 2
-    middle = list(range(3, half))
-    pairs = [(half, half)] + list(zip([1] + middle + [2], [2] + middle + [1]))
-    tiles = {pair: swap(features, pair) for pair in pairs}
-    tiles[0, 0] = features
+    evens, odds = list(range(2, half, 2)), list(range(half - 1, 0, -2))
+    tiles = {0: features}
+    for mask in evens + [half, 1]:
+        tiles[mask] = exchange(features, "col", mask)
+    for mask in evens:
+        tiles[mask + 1] = exchange(tiles[mask], "col", 1)
     first = list(tiles)
-    far, lists = lax.optimization_barrier((tiles[half, half], lists))
+    far, lists = lax.optimization_barrier((tiles[half], lists))
+    tiles[half] = far
+    for mask in odds + evens:
+        tiles[half + mask] = exchange(far, "col", mask)
     a, deg = combine(adj_tiles, lists, n_col, n_row)
-    for mask in reversed(range(1, half)):
-        tiles[half + mask, half + mask] = swap(far, (mask, mask))
-    last = [pair for pair in tiles if pair not in first]
-    acc = early(a, [tiles[pair] for pair in first], first)
+    last = [mask for mask in tiles if mask not in first]
+    acc = early(a, [tiles[mask] for mask in first], first)
     own = own_rows(features, self_weight, layer_bias)
 
-    blocks = late(a, deg, acc, [tiles[pair] for pair in last], last, n_row)
+    blocks = late(a, deg, acc, [tiles[mask] for mask in last], last, n_row)
     while len(blocks) > 4:
         bit = len(blocks) // 2
         blocks = [fold(blocks[m], exchange(blocks[m | bit], "row", bit)) for m in range(bit)]

time: 28.5 us -> 28.1 us (0.986)
  waiting for transfers between devices: 7.05 us -> 6.74 us
    ppermute x7 -> x0, starting transfers between devices: 12.5 us -> none  [swap(): return lax.ppermute(value, ('row', 'col'), pairs)]
    ppermute x3 -> x10, starting transfers between devices: 2.12 us -> 14.5 us  [exchange(): return lax.ppermute(value, axis, pairs)]
    ppermute x7 -> x0, waiting for transfers between devices: 2.21 us -> none  [swap(): return lax.ppermute(value, ('row', 'col'), pairs)]
    ppermute x3 -> x10, waiting for transfers between devices: 4.84 us -> 6.74 us  [exchange(): return lax.ppermute(value, axis, pairs)]
  transfers between devices with their start and end apart: 10 -> 10, of which waited for: 4 -> 5; matrix products, arithmetic and copies ran while one was open for 3% -> 3% of each run, Pallas kernels for 14% -> 14%
where the time goes in v5:
time: 28.1 us; the launch traced here: 28 us
  starting transfers between devices  14.5 us (52%)
  waiting for transfers between devices  6.74 us (24%)
  Pallas kernels  5.23 us (19%)
  between operations  0.76 us (3%)
  other arithmetic  0.75 us (3%)
    ppermute x10, starting transfers between devices, exchange(): return lax.ppermute(value, axis, pairs)  14.5 us
    ppermute x10, waiting for transfers between devices, exchange(): return lax.ppermute(value, axis, pairs)  6.74 us
    pallas_call x1, Pallas kernels, combine(): pl.pallas_call(combine_kernel, in_specs=[whole(pltpu.HBM)] * 2, out_specs...  3.22 us
    pallas_call x1, Pallas kernels, finish(): pl.pallas_call(finish_kernel, in_specs=[whole(pltpu.VMEM)] * (2 + len(par...  0.88 us
    concatenate x1, other arithmetic, on_device(): jnp.concatenate([tile_dst[0, 0], tile_src[0, 0], tile_count[0], jnp.zeros...  0.75 us
  transfers between devices with their start and end apart: 10, of which 5 were waited for; matrix products, arithmetic and copies ran while one was open for 3% of the time, Pallas kernels for 14%

profile of v5, /device:TPU:0, one launch (start us, length us, event | category | flops | bytes accessed | tf_op | source)
XLA Modules:
  0.0 28.0 jit_solution(2900187695211447148)
XLA Ops:
  0.0 0.0 copy-start
  0.0 3.0 %collective-permute-start.1 = (f32[128,256]{1,0:T(8,128)}, f32[128,256]{1,0:T(8,128)S(1)}, u32[]{:S(2)}, u32[]{:S(2)}) collective-permute-start(f32[128,256]{1,0:T(8,128)} %refs_0_.1), channel_id=1, source_target_pairs={{0,2},{1,3},{2,0},{3,1},{4,6},{5,7},{6,4},{7,5},{8,10},{9,11},{10,... | collective-permute-start | bytes 393224 | tf_op jit(solution)/shard_map/ppermute | solution.py:247
  3.0 2.6 %collective-permute-start = (f32[128,256]{1,0:T(8,128)}, f32[128,256]{1,0:T(8,128)S(1)}, u32[]{:S(2)}, u32[]{:S(2)}) collective-permute-start(f32[128,256]{1,0:T(8,128)} %refs_0_.1), channel_id=1, source_target_pairs={{0,4},{1,5},{2,6},{3,7},{4,0},{5,1},{6,2},{7,3},{8,12},{9,13},{10,... | collective-permute-start | bytes 393224 | tf_op jit(solution)/shard_map/ppermute | solution.py:247
  5.6 1.5 %collective-permute-start.2 = (f32[128,256]{1,0:T(8,128)}, f32[128,256]{1,0:T(8,128)S(1)}, u32[]{:S(2)}, u32[]{:S(2)}) collective-permute-start(f32[128,256]{1,0:T(8,128)} %refs_0_.1), channel_id=1, source_target_pairs={{0,1},{1,0},{2,3},{3,2},{4,5},{5,4},{6,7},{7,6},{8,9},{9,8},{10,11... | collective-permute-start | bytes 393224 | tf_op jit(solution)/shard_map/ppermute | solution.py:247
  7.8 0.8 %pad_add_fusion.lists_hbm = s32[256]{0:T(256)S(1)} fusion(s32[63]{0:T(128)S(1)} %broadcast_in_dim.3, s32[1]{0:T(128)} %bitcast.3, s32[96]{0:T(128)} %bitcast.4, s32[96]{0:T(128)} %bitcast.5), kind=kLoop, calls=%fused_computation | loop fusion | flops 768 | bytes 2048 | tf_op jit(solution)/shard_map/concatenate | solution.py:257
  8.6 0.0 copy-start.2
  8.6 0.0 copy-start.3
  8.6 0.1 collective-permute-done.1.refs_1_
  8.7 1.7 %collective-permute-start.3 = (f32[128,256]{1,0:T(8,128)S(1)}, f32[128,256]{1,0:T(8,128)S(1)}, u32[]{:S(2)}, u32[]{:S(2)}) collective-permute-start(f32[128,256]{1,0:T(8,128)S(1)} %collective-permute-done.1.refs_1_), channel_id=1, source_target_pairs={{0,1},{1,0},{2,3},{3,2},{4,5},{5,4},{6,7},{7,6},{8,9},{9,8},{10,11... | collective-permute-start | bytes 393224 | tf_op jit(solution)/shard_map/ppermute | solution.py:247
  10.4 1.6 %collective-permute-done.refs_2_ = f32[128,256]{1,0:T(8,128)S(1)} collective-permute-done((f32[128,256]{1,0:T(8,128)}, f32[128,256]{1,0:T(8,128)S(1)}, u32[]{:S(2)}, u32[]{:S(2)}) %collective-permute-start) | collective-permute-done | bytes 131104 | tf_op jit(solution)/shard_map/ppermute | solution.py:247
  12.0 1.4 %collective-permute-start.4 = (f32[128,256]{1,0:T(8,128)S(1)}, f32[128,256]{1,0:T(8,128)S(1)}, u32[]{:S(2)}, u32[]{:S(2)}) collective-permute-start(f32[128,256]{1,0:T(8,128)S(1)} %collective-permute-done.refs_2_), channel_id=1, source_target_pairs={{0,3},{1,2},{2,1},{3,0},{4,7},{5,6},{6,5},{7,4},{8,11},{9,10},{10,... | collective-permute-start | bytes 393224 | tf_op jit(solution)/shard_map/ppermute | solution.py:247
  13.4 0.5 %collective-permute-start.5 = (f32[128,256]{1,0:T(8,128)S(1)}, f32[128,256]{1,0:T(8,128)S(1)}, u32[]{:S(2)}, u32[]{:S(2)}) collective-permute-start(f32[128,256]{1,0:T(8,128)S(1)} %collective-permute-done.refs_2_), channel_id=1, source_target_pairs={{0,1},{1,0},{2,3},{3,2},{4,5},{5,4},{6,7},{7,6},{8,9},{9,8},{10,11... | collective-permute-start | bytes 393224 | tf_op jit(solution)/shard_map/ppermute | solution.py:247
  13.9 1.6 %collective-permute-start.6 = (f32[128,256]{1,0:T(8,128)S(1)}, f32[128,256]{1,0:T(8,128)S(1)}, u32[]{:S(2)}, u32[]{:S(2)}) collective-permute-start(f32[128,256]{1,0:T(8,128)S(1)} %collective-permute-done.refs_2_), channel_id=1, source_target_pairs={{0,2},{1,3},{2,0},{3,1},{4,6},{5,7},{6,4},{7,5},{8,10},{9,11},{10,... | collective-permute-start | bytes 393224 | tf_op jit(solution)/shard_map/ppermute | solution.py:247
  15.5 3.2 %combine_tiles.1 = (bf16[8,512,128]{2,1,0:T(8,128)(2,1)S(1)}, f32[4,8,128]{2,1,0:T(8,128)S(1)}) custom-call(s32[256]{0:T(256)S(1)} %pad_add_fusion.lists_hbm, bf16[1,1,96,128,128]{4,3,2,1,0:T(8,128)(2,1)} %adj_hbm.1), custom_call_target="tpu_custom_call" | custom-call | tf_op jit(solution)/shard_map/combine_tiles/pallas_call | solution.py:97
  18.7 0.0 copy-start.1
  18.7 0.0 collective-permute-done.2.refs_3_
  18.7 0.0 collective-permute-done.3.refs_4_
  18.7 0.0 copy-done
  18.7 0.5 %early_products.1.acc_ref = f32[512,256]{1,0:T(8,128)S(1)} custom-call(bf16[8,512,128]{2,1,0:T(8,128)(2,1)S(1)} %get-tuple-element.15.a_ref, f32[128,256]{1,0:T(8,128)S(1)} %copy-done, f32[128,256]{1,0:T(8,128)S(1)} %collective-permute-done.1.refs_1_, f32[128,256]{1,0:T(8,128)S(1)} %collective-permute-done.refs_2_, ...), custom_call_target="tpu_custom_call" | custom-call | tf_op jit(solution)/shard_map/early_products/pallas_call | solution.py:193
  19.3 0.0 collective-permute-done.4.refs_0_
  19.3 0.2 collective-permute-done.5.refs_1_
  19.5 0.0 collective-permute-done.6.refs_2_
  19.5 0.4 %late_products.1 = (f32[136,256]{1,0:T(8,128)S(1)}, f32[136,256]{1,0:T(8,128)S(1)}, f32[136,256]{1,0:T(8,128)S(1)}, f32[136,256]{1,0:T(8,128)S(1)}) custom-call(bf16[8,512,128]{2,1,0:T(8,128)(2,1)S(1)} %get-tuple-element.15.a_ref, f32[4,8,128]{2,1,0:T(8,128)S(1)} %get-tuple-element.16.deg_ref, f32[512,256]{1,0:T(8,128)S(1)} %early_products.1.acc_ref, ...), custom_call_target="tpu_custom_call" | custom-call | tf_op jit(solution)/shard_map/late_products/pallas_call | solution.py:206
  19.8 0.1 collective-permute-start.8
  19.9 0.5 %collective-permute-start.7 = (f32[136,256]{1,0:T(8,128)S(1)}, f32[136,256]{1,0:T(8,128)S(1)}, u32[]{:S(2)}, u32[]{:S(2)}) collective-permute-start(f32[136,256]{1,0:T(8,128)S(1)} %get-tuple-element.19), channel_id=1, source_target_pairs={{0,8},{8,0},{16,24},{24,16},{1,9},{9,1},{17,25},{25,17},{2,10},{10... | collective-permute-start | bytes 417800 | tf_op jit(solution)/shard_map/ppermute | solution.py:247
  20.4 0.8 %collective-permute-done.8.came_ref = f32[136,256]{1,0:T(8,128)S(1)} collective-permute-done((f32[136,256]{1,0:T(8,128)S(1)}, f32[136,256]{1,0:T(8,128)S(1)}, u32[]{:S(2)}, u32[]{:S(2)}) %collective-permute-start.8) | collective-permute-done | bytes 139296 | tf_op jit(solution)/shard_map/ppermute | solution.py:247
  21.3 1.6 %collective-permute-start.9 = (f32[136,256]{1,0:T(8,128)S(1)}, f32[136,256]{1,0:T(8,128)S(1)}, u32[]{:S(2)}, u32[]{:S(2)}) collective-permute-start(f32[136,256]{1,0:T(8,128)S(1)} %fold_sums.1), channel_id=1, source_target_pairs={{0,16},{8,24},{16,0},{24,8},{1,17},{9,25},{17,1},{25,9},{2,18},{10... | collective-permute-start | bytes 417800 | tf_op jit(solution)/shard_map/ppermute | solution.py:247
  22.8 0.0 copy-done.2
  22.9 0.0 copy-done.3
  22.9 0.2 own_rows.1.own_ref
  23.1 0.0 collective-permute-done.7.refs_1_
  23.1 4.0 %collective-permute-done.9.refs_2_ = f32[136,256]{1,0:T(8,128)S(1)} collective-permute-done((f32[136,256]{1,0:T(8,128)S(1)}, f32[136,256]{1,0:T(8,128)S(1)}, u32[]{:S(2)}, u32[]{:S(2)}) %collective-permute-start.9) | collective-permute-done | bytes 139296 | tf_op jit(solution)/shard_map/ppermute | solution.py:247
  27.1 0.0 copy-done.1
  27.1 0.9 %finish_rows.1 = f32[128,256]{1,0:T(8,128)} custom-call(f32[128,256]{1,0:T(8,128)S(1)} %own_rows.1.own_ref, f32[256,256]{1,0:T(8,128)S(1)} %copy-done.1, f32[136,256]{1,0:T(8,128)S(1)} %get-tuple-element.18.refs_0_, f32[136,256]{1,0:T(8,128)S(1)} %collective-permute-done.7.refs_1_, f32[136,256]{1,0:T(8,128)S(1)} %collective-permute-done.9.refs_2_), custom_call_target="tpu_custom_call" | custom-call | tf_op jit(solution)/shard_map/finish_rows/pallas_call | solution.py:231
  (2 shorter events, 0.0 us)
Async XLA Ops:
  0.0 18.7 %copy-start = (f32[128,256]{1,0:T(8,128)S(1)}, f32[128,256]{1,0:T(8,128)}, u32[]{:S(2)}) copy-start(f32[128,256]{1,0:T(8,128)} %refs_0_.1) | copy-start | bytes 393220
  0.0 8.7 %collective-permute-start.1 = (f32[128,256]{1,0:T(8,128)}, f32[128,256]{1,0:T(8,128)S(1)}, u32[]{:S(2)}, u32[]{:S(2)}) collective-permute-start(f32[128,256]{1,0:T(8,128)} %refs_0_.1), channel_id=1, source_target_pairs={{0,2},{1,3},{2,0},{3,1},{4,6},{5,7},{6,4},{7,5},{8,10},{9,11},{10,... | collective-permute-start | bytes 393224 | tf_op jit(solution)/shard_map/ppermute | solution.py:247
  3.0 8.9 %collective-permute-start = (f32[128,256]{1,0:T(8,128)}, f32[128,256]{1,0:T(8,128)S(1)}, u32[]{:S(2)}, u32[]{:S(2)}) collective-permute-start(f32[128,256]{1,0:T(8,128)} %refs_0_.1), channel_id=1, source_target_pairs={{0,4},{1,5},{2,6},{3,7},{4,0},{5,1},{6,2},{7,3},{8,12},{9,13},{10,... | collective-permute-start | bytes 393224 | tf_op jit(solution)/shard_map/ppermute | solution.py:247
  5.6 13.1 %collective-permute-start.2 = (f32[128,256]{1,0:T(8,128)}, f32[128,256]{1,0:T(8,128)S(1)}, u32[]{:S(2)}, u32[]{:S(2)}) collective-permute-start(f32[128,256]{1,0:T(8,128)} %refs_0_.1), channel_id=1, source_target_pairs={{0,1},{1,0},{2,3},{3,2},{4,5},{5,4},{6,7},{7,6},{8,9},{9,8},{10,11... | collective-permute-start | bytes 393224 | tf_op jit(solution)/shard_map/ppermute | solution.py:247
  8.6 14.3 %copy-start.2 = (f32[256,256]{1,0:T(8,128)S(1)}, f32[256,256]{1,0:T(8,128)}, u32[]{:S(2)}) copy-start(f32[256,256]{1,0:T(8,128)} %ws_ref.1) | copy-start | bytes 786436
  8.6 14.3 %copy-start.3 = (f32[256]{0:T(256)S(1)}, f32[256]{0:T(256)}, u32[]{:S(2)}) copy-start(f32[256]{0:T(256)} %b_ref.1) | copy-start | bytes 3076
  8.7 10.0 %collective-permute-start.3 = (f32[128,256]{1,0:T(8,128)S(1)}, f32[128,256]{1,0:T(8,128)S(1)}, u32[]{:S(2)}, u32[]{:S(2)}) collective-permute-start(f32[128,256]{1,0:T(8,128)S(1)} %collective-permute-done.1.refs_1_), channel_id=1, source_target_pairs={{0,1},{1,0},{2,3},{3,2},{4,5},{5,4},{6,7},{7,6},{8,9},{9,8},{10,11... | collective-permute-start | bytes 393224 | tf_op jit(solution)/shard_map/ppermute | solution.py:247
  12.0 7.3 %collective-permute-start.4 = (f32[128,256]{1,0:T(8,128)S(1)}, f32[128,256]{1,0:T(8,128)S(1)}, u32[]{:S(2)}, u32[]{:S(2)}) collective-permute-start(f32[128,256]{1,0:T(8,128)S(1)} %collective-permute-done.refs_2_), channel_id=1, source_target_pairs={{0,3},{1,2},{2,1},{3,0},{4,7},{5,6},{6,5},{7,4},{8,11},{9,10},{10,... | collective-permute-start | bytes 393224 | tf_op jit(solution)/shard_map/ppermute | solution.py:247
  13.4 6.1 %collective-permute-start.5 = (f32[128,256]{1,0:T(8,128)S(1)}, f32[128,256]{1,0:T(8,128)S(1)}, u32[]{:S(2)}, u32[]{:S(2)}) collective-permute-start(f32[128,256]{1,0:T(8,128)S(1)} %collective-permute-done.refs_2_), channel_id=1, source_target_pairs={{0,1},{1,0},{2,3},{3,2},{4,5},{5,4},{6,7},{7,6},{8,9},{9,8},{10,11... | collective-permute-start | bytes 393224 | tf_op jit(solution)/shard_map/ppermute | solution.py:247
  13.9 5.6 %collective-permute-start.6 = (f32[128,256]{1,0:T(8,128)S(1)}, f32[128,256]{1,0:T(8,128)S(1)}, u32[]{:S(2)}, u32[]{:S(2)}) collective-permute-start(f32[128,256]{1,0:T(8,128)S(1)} %collective-permute-done.refs_2_), channel_id=1, source_target_pairs={{0,2},{1,3},{2,0},{3,1},{4,6},{5,7},{6,4},{7,5},{8,10},{9,11},{10,... | collective-permute-start | bytes 393224 | tf_op jit(solution)/shard_map/ppermute | solution.py:247
  18.7 8.4 %copy-start.1 = (f32[256,256]{1,0:T(8,128)S(1)}, f32[256,256]{1,0:T(8,128)}, u32[]{:S(2)}) copy-start(f32[256,256]{1,0:T(8,128)} %wn_ref.1) | copy-start | bytes 786436
  19.8 1.4 %collective-permute-start.8 = (f32[136,256]{1,0:T(8,128)S(1)}, f32[136,256]{1,0:T(8,128)S(1)}, u32[]{:S(2)}, u32[]{:S(2)}) collective-permute-start(f32[136,256]{1,0:T(8,128)S(1)} %get-tuple-element.21), channel_id=1, source_target_pairs={{0,8},{8,0},{16,24},{24,16},{1,9},{9,1},{17,25},{25,17},{2,10},{10... | collective-permute-start | bytes 417800 | tf_op jit(solution)/shard_map/ppermute | solution.py:247
  19.9 3.2 %collective-permute-start.7 = (f32[136,256]{1,0:T(8,128)S(1)}, f32[136,256]{1,0:T(8,128)S(1)}, u32[]{:S(2)}, u32[]{:S(2)}) collective-permute-start(f32[136,256]{1,0:T(8,128)S(1)} %get-tuple-element.19), channel_id=1, source_target_pairs={{0,8},{8,0},{16,24},{24,16},{1,9},{9,1},{17,25},{25,17},{2,10},{10... | collective-permute-start | bytes 417800 | tf_op jit(solution)/shard_map/ppermute | solution.py:247
  21.3 5.8 %collective-permute-start.9 = (f32[136,256]{1,0:T(8,128)S(1)}, f32[136,256]{1,0:T(8,128)S(1)}, u32[]{:S(2)}, u32[]{:S(2)}) collective-permute-start(f32[136,256]{1,0:T(8,128)S(1)} %fold_sums.1), channel_id=1, source_target_pairs={{0,16},{8,24},{16,0},{24,8},{1,17},{9,25},{17,1},{25,9},{2,18},{10... | collective-permute-start | bytes 417800 | tf_op jit(solution)/shard_map/ppermute | solution.py:247

commit v6 on v5

--- a/solution.py
+++ b/solution.py
@@ -160,12 +160,12 @@
     lax.fori_loop(0, acc_ref.shape[0] // height, visit, 0)
 
 
-def late_kernel(masks, a_ref, deg_ref, acc_ref, *refs):
+def late_kernel(masks, places, a_ref, deg_ref, acc_ref, *refs):
     tile_refs, out_refs, halves = refs[: len(masks)], refs[len(masks) : -1], refs[-1]
     tile, feat = tile_refs[0].shape
     stack_halves(tile_refs, halves)
-    for index, out_ref in enumerate(out_refs):
-        d = lax.axis_index("row") ^ index
+    for place, out_ref in zip(places, out_refs):
+        d = lax.axis_index("row") ^ place
         rows = pl.ds(pl.multiple_of(d * tile, tile), tile)
         out_ref[0:tile, :] = acc_ref[rows, :] + product_rows(
             a_ref, tile_refs, masks, halves, rows
@@ -201,13 +201,13 @@
     )(a, *tiles)
 
 
-def late(a, deg, acc, tiles, masks, n_row):
+def late(a, deg, acc, tiles, masks, places):
     tile, feat = tiles[0].shape
     return pl.pallas_call(
-        functools.partial(late_kernel, masks),
+        functools.partial(late_kernel, masks, places),
         in_specs=[whole(pltpu.VMEM)] * (3 + len(tiles)),
-        out_specs=[whole(pltpu.VMEM)] * n_row,
-        out_shape=[jax.ShapeDtypeStruct((tile + PAD, feat), jnp.float32)] * n_row,
+        out_specs=[whole(pltpu.VMEM)] * len(places),
+        out_shape=[jax.ShapeDtypeStruct((tile + PAD, feat), jnp.float32)] * len(places),
         scratch_shapes=[pltpu.VMEM((len(tiles), 2 * tile, feat), jnp.bfloat16)],
         compiler_params=pltpu.CompilerParams(vmem_limit_bytes=VMEM_BYTES),
         name="late_products",
@@ -275,7 +275,10 @@
     acc = early(a, [tiles[mask] for mask in first], first)
     own = own_rows(features, self_weight, layer_bias)
 
-    blocks = late(a, deg, acc, [tiles[mask] for mask in last], last, n_row)
+    split = max(3, n_row // 2)
+    groups = [range(split, n_row), range(split)]
+    sent, kept = [late(a, deg, acc, [tiles[m] for m in last], last, g) for g in groups]
+    blocks = list(kept) + list(sent)
     while len(blocks) > 4:
         bit = len(blocks) // 2
         blocks = [fold(blocks[m], exchange(blocks[m | bit], "row", bit)) for m in range(bit)]

time: 28.1 us -> 28 us (level)
  Pallas kernels: 5.23 us -> 4.33 us
  waiting for transfers between devices: 6.74 us -> 7.42 us
    pallas_call x1, Pallas kernels: 3.22 us -> 2.14 us  [combine(): pl.pallas_call(combine_kernel, in_specs=[whole(pltpu.HBM)] * 2, out_specs...]
    ppermute x10, waiting for transfers between devices: 6.74 us -> 7.42 us  [exchange(): return lax.ppermute(value, axis, pairs)]
  transfers between devices with their start and end apart: 10 -> 10, of which waited for: 5 -> 6; matrix products, arithmetic and copies ran while one was open for 3% -> 3% of each run, Pallas kernels for 14% -> 12%
where the time goes in v6:
time: 28 us; the launch traced here: 27.8 us
  starting transfers between devices  14.5 us (52%)
  waiting for transfers between devices  7.42 us (26%)
  Pallas kernels  4.33 us (15%)
  between operations  0.78 us (3%)
  other arithmetic  0.75 us (3%)
    ppermute x10, starting transfers between devices, exchange(): return lax.ppermute(value, axis, pairs)  14.5 us
    ppermute x10, waiting for transfers between devices, exchange(): return lax.ppermute(value, axis, pairs)  7.42 us
    pallas_call x1, Pallas kernels, combine(): pl.pallas_call(combine_kernel, in_specs=[whole(pltpu.HBM)] * 2, out_specs...  2.14 us
    pallas_call x1, Pallas kernels, finish(): pl.pallas_call(finish_kernel, in_specs=[whole(pltpu.VMEM)] * (2 + len(par...  0.88 us
    concatenate x1, other arithmetic, on_device(): jnp.concatenate([tile_dst[0, 0], tile_src[0, 0], tile_count[0], jnp.zeros...  0.75 us
  transfers between devices with their start and end apart: 10, of which 6 were waited for; matrix products, arithmetic and copies ran while one was open for 3% of the time, Pallas kernels for 12%

profile of v6, /device:TPU:0, one launch (start us, length us, event | category | flops | bytes accessed | tf_op | source)
XLA Modules:
  0.0 27.8 jit_solution(1734630899510258743)
XLA Ops:
  0.0 0.0 copy-start
  0.0 3.0 %collective-permute-start.1 = (f32[128,256]{1,0:T(8,128)}, f32[128,256]{1,0:T(8,128)S(1)}, u32[]{:S(2)}, u32[]{:S(2)}) collective-permute-start(f32[128,256]{1,0:T(8,128)} %refs_0_.1), channel_id=1, source_target_pairs={{0,2},{1,3},{2,0},{3,1},{4,6},{5,7},{6,4},{7,5},{8,10},{9,11},{10,... | collective-permute-start | bytes 393224 | tf_op jit(solution)/shard_map/ppermute | solution.py:247
  3.0 2.6 %collective-permute-start = (f32[128,256]{1,0:T(8,128)}, f32[128,256]{1,0:T(8,128)S(1)}, u32[]{:S(2)}, u32[]{:S(2)}) collective-permute-start(f32[128,256]{1,0:T(8,128)} %refs_0_.1), channel_id=1, source_target_pairs={{0,4},{1,5},{2,6},{3,7},{4,0},{5,1},{6,2},{7,3},{8,12},{9,13},{10,... | collective-permute-start | bytes 393224 | tf_op jit(solution)/shard_map/ppermute | solution.py:247
  5.6 1.5 %collective-permute-start.2 = (f32[128,256]{1,0:T(8,128)}, f32[128,256]{1,0:T(8,128)S(1)}, u32[]{:S(2)}, u32[]{:S(2)}) collective-permute-start(f32[128,256]{1,0:T(8,128)} %refs_0_.1), channel_id=1, source_target_pairs={{0,1},{1,0},{2,3},{3,2},{4,5},{5,4},{6,7},{7,6},{8,9},{9,8},{10,11... | collective-permute-start | bytes 393224 | tf_op jit(solution)/shard_map/ppermute | solution.py:247
  7.8 0.8 %pad_add_fusion.lists_hbm = s32[256]{0:T(256)S(1)} fusion(s32[63]{0:T(128)S(1)} %broadcast_in_dim.3, s32[1]{0:T(128)} %bitcast.3, s32[96]{0:T(128)} %bitcast.4, s32[96]{0:T(128)} %bitcast.5), kind=kLoop, calls=%fused_computation | loop fusion | flops 768 | bytes 2048 | tf_op jit(solution)/shard_map/concatenate | solution.py:257
  8.6 0.1 collective-permute-done.1.refs_1_
  8.7 1.7 %collective-permute-start.3 = (f32[128,256]{1,0:T(8,128)S(1)}, f32[128,256]{1,0:T(8,128)S(1)}, u32[]{:S(2)}, u32[]{:S(2)}) collective-permute-start(f32[128,256]{1,0:T(8,128)S(1)} %collective-permute-done.1.refs_1_), channel_id=1, source_target_pairs={{0,1},{1,0},{2,3},{3,2},{4,5},{5,4},{6,7},{7,6},{8,9},{9,8},{10,11... | collective-permute-start | bytes 393224 | tf_op jit(solution)/shard_map/ppermute | solution.py:247
  10.4 1.6 %collective-permute-done.refs_2_ = f32[128,256]{1,0:T(8,128)S(1)} collective-permute-done((f32[128,256]{1,0:T(8,128)}, f32[128,256]{1,0:T(8,128)S(1)}, u32[]{:S(2)}, u32[]{:S(2)}) %collective-permute-start) | collective-permute-done | bytes 131104 | tf_op jit(solution)/shard_map/ppermute | solution.py:247
  12.0 1.4 %collective-permute-start.4 = (f32[128,256]{1,0:T(8,128)S(1)}, f32[128,256]{1,0:T(8,128)S(1)}, u32[]{:S(2)}, u32[]{:S(2)}) collective-permute-start(f32[128,256]{1,0:T(8,128)S(1)} %collective-permute-done.refs_2_), channel_id=1, source_target_pairs={{0,3},{1,2},{2,1},{3,0},{4,7},{5,6},{6,5},{7,4},{8,11},{9,10},{10,... | collective-permute-start | bytes 393224 | tf_op jit(solution)/shard_map/ppermute | solution.py:247
  13.4 0.5 %collective-permute-start.5 = (f32[128,256]{1,0:T(8,128)S(1)}, f32[128,256]{1,0:T(8,128)S(1)}, u32[]{:S(2)}, u32[]{:S(2)}) collective-permute-start(f32[128,256]{1,0:T(8,128)S(1)} %collective-permute-done.refs_2_), channel_id=1, source_target_pairs={{0,1},{1,0},{2,3},{3,2},{4,5},{5,4},{6,7},{7,6},{8,9},{9,8},{10,11... | collective-permute-start | bytes 393224 | tf_op jit(solution)/shard_map/ppermute | solution.py:247
  13.9 1.6 %collective-permute-start.6 = (f32[128,256]{1,0:T(8,128)S(1)}, f32[128,256]{1,0:T(8,128)S(1)}, u32[]{:S(2)}, u32[]{:S(2)}) collective-permute-start(f32[128,256]{1,0:T(8,128)S(1)} %collective-permute-done.refs_2_), channel_id=1, source_target_pairs={{0,2},{1,3},{2,0},{3,1},{4,6},{5,7},{6,4},{7,5},{8,10},{9,11},{10,... | collective-permute-start | bytes 393224 | tf_op jit(solution)/shard_map/ppermute | solution.py:247
  15.5 2.1 %combine_tiles.1 = (bf16[8,512,128]{2,1,0:T(8,128)(2,1)S(1)}, f32[4,8,128]{2,1,0:T(8,128)S(1)}) custom-call(s32[256]{0:T(256)S(1)} %pad_add_fusion.lists_hbm, bf16[1,1,96,128,128]{4,3,2,1,0:T(8,128)(2,1)} %adj_hbm.1), custom_call_target="tpu_custom_call" | custom-call | tf_op jit(solution)/shard_map/combine_tiles/pallas_call | solution.py:97
  17.6 0.0 collective-permute-done.2.refs_3_
  17.6 0.0 collective-permute-done.3.refs_4_
  17.6 0.0 copy-done
  17.6 0.0 copy-start.2
  17.6 0.0 copy-start.3
  17.7 0.0 copy-start.1
  17.7 0.5 %early_products.1.acc_ref = f32[512,256]{1,0:T(8,128)S(1)} custom-call(bf16[8,512,128]{2,1,0:T(8,128)(2,1)S(1)} %get-tuple-element.14.a_ref, f32[128,256]{1,0:T(8,128)S(1)} %copy-done, f32[128,256]{1,0:T(8,128)S(1)} %collective-permute-done.1.refs_1_, f32[128,256]{1,0:T(8,128)S(1)} %collective-permute-done.refs_2_, ...), custom_call_target="tpu_custom_call" | custom-call | tf_op jit(solution)/shard_map/early_products/pallas_call | solution.py:193
  18.2 0.4 %collective-permute-done.4.refs_0_ = f32[128,256]{1,0:T(8,128)S(1)} collective-permute-done((f32[128,256]{1,0:T(8,128)S(1)}, f32[128,256]{1,0:T(8,128)S(1)}, u32[]{:S(2)}, u32[]{:S(2)}) %collective-permute-start.4) | collective-permute-done | bytes 131104 | tf_op jit(solution)/shard_map/ppermute | solution.py:247
  18.6 0.9 %collective-permute-done.5.refs_1_ = f32[128,256]{1,0:T(8,128)S(1)} collective-permute-done((f32[128,256]{1,0:T(8,128)S(1)}, f32[128,256]{1,0:T(8,128)S(1)}, u32[]{:S(2)}, u32[]{:S(2)}) %collective-permute-start.5) | collective-permute-done | bytes 131104 | tf_op jit(solution)/shard_map/ppermute | solution.py:247
  19.5 0.0 collective-permute-done.6.refs_2_
  19.5 0.2 late_products.3
  19.7 0.1 collective-permute-start.8
  19.8 0.3 %late_products.2 = (f32[136,256]{1,0:T(8,128)S(1)}, f32[136,256]{1,0:T(8,128)S(1)}, f32[136,256]{1,0:T(8,128)S(1)}) custom-call(bf16[8,512,128]{2,1,0:T(8,128)(2,1)S(1)} %get-tuple-element.14.a_ref, f32[4,8,128]{2,1,0:T(8,128)S(1)} %get-tuple-element.15.deg_ref, f32[512,256]{1,0:T(8,128)S(1)} %early_products.1.acc_ref, ...), custom_call_target="tpu_custom_call" | custom-call | tf_op jit(solution)/shard_map/late_products/pallas_call | solution.py:206
  20.1 0.6 %collective-permute-start.7 = (f32[136,256]{1,0:T(8,128)S(1)}, f32[136,256]{1,0:T(8,128)S(1)}, u32[]{:S(2)}, u32[]{:S(2)}) collective-permute-start(f32[136,256]{1,0:T(8,128)S(1)} %get-tuple-element.18), channel_id=1, source_target_pairs={{0,8},{8,0},{16,24},{24,16},{1,9},{9,1},{17,25},{25,17},{2,10},{10... | collective-permute-start | bytes 417800 | tf_op jit(solution)/shard_map/ppermute | solution.py:247
  20.7 0.4 %collective-permute-done.8.came_ref = f32[136,256]{1,0:T(8,128)S(1)} collective-permute-done((f32[136,256]{1,0:T(8,128)S(1)}, f32[136,256]{1,0:T(8,128)S(1)}, u32[]{:S(2)}, u32[]{:S(2)}) %collective-permute-start.8) | collective-permute-done | bytes 139296 | tf_op jit(solution)/shard_map/ppermute | solution.py:247
  21.1 1.6 %collective-permute-start.9 = (f32[136,256]{1,0:T(8,128)S(1)}, f32[136,256]{1,0:T(8,128)S(1)}, u32[]{:S(2)}, u32[]{:S(2)}) collective-permute-start(f32[136,256]{1,0:T(8,128)S(1)} %fold_sums.1), channel_id=1, source_target_pairs={{0,16},{8,24},{16,0},{24,8},{1,17},{9,25},{17,1},{25,9},{2,18},{10... | collective-permute-start | bytes 417800 | tf_op jit(solution)/shard_map/ppermute | solution.py:247
  22.7 0.0 copy-done.2
  22.7 0.0 copy-done.3
  22.7 0.2 own_rows.1.own_ref
  22.9 0.0 collective-permute-done.7.refs_1_
  22.9 4.0 %collective-permute-done.9.refs_2_ = f32[136,256]{1,0:T(8,128)S(1)} collective-permute-done((f32[136,256]{1,0:T(8,128)S(1)}, f32[136,256]{1,0:T(8,128)S(1)}, u32[]{:S(2)}, u32[]{:S(2)}) %collective-permute-start.9) | collective-permute-done | bytes 139296 | tf_op jit(solution)/shard_map/ppermute | solution.py:247
  26.9 0.0 copy-done.1
  26.9 0.9 %finish_rows.1 = f32[128,256]{1,0:T(8,128)} custom-call(f32[128,256]{1,0:T(8,128)S(1)} %own_rows.1.own_ref, f32[256,256]{1,0:T(8,128)S(1)} %copy-done.1, f32[136,256]{1,0:T(8,128)S(1)} %get-tuple-element.17.refs_0_, f32[136,256]{1,0:T(8,128)S(1)} %collective-permute-done.7.refs_1_, f32[136,256]{1,0:T(8,128)S(1)} %collective-permute-done.9.refs_2_), custom_call_target="tpu_custom_call" | custom-call | tf_op jit(solution)/shard_map/finish_rows/pallas_call | solution.py:231
  (2 shorter events, 0.0 us)
Async XLA Ops:
  0.0 17.6 %copy-start = (f32[128,256]{1,0:T(8,128)S(1)}, f32[128,256]{1,0:T(8,128)}, u32[]{:S(2)}) copy-start(f32[128,256]{1,0:T(8,128)} %refs_0_.1) | copy-start | bytes 393220
  0.0 8.7 %collective-permute-start.1 = (f32[128,256]{1,0:T(8,128)}, f32[128,256]{1,0:T(8,128)S(1)}, u32[]{:S(2)}, u32[]{:S(2)}) collective-permute-start(f32[128,256]{1,0:T(8,128)} %refs_0_.1), channel_id=1, source_target_pairs={{0,2},{1,3},{2,0},{3,1},{4,6},{5,7},{6,4},{7,5},{8,10},{9,11},{10,... | collective-permute-start | bytes 393224 | tf_op jit(solution)/shard_map/ppermute | solution.py:247
  3.0 8.9 %collective-permute-start = (f32[128,256]{1,0:T(8,128)}, f32[128,256]{1,0:T(8,128)S(1)}, u32[]{:S(2)}, u32[]{:S(2)}) collective-permute-start(f32[128,256]{1,0:T(8,128)} %refs_0_.1), channel_id=1, source_target_pairs={{0,4},{1,5},{2,6},{3,7},{4,0},{5,1},{6,2},{7,3},{8,12},{9,13},{10,... | collective-permute-start | bytes 393224 | tf_op jit(solution)/shard_map/ppermute | solution.py:247
  5.6 12.0 %collective-permute-start.2 = (f32[128,256]{1,0:T(8,128)}, f32[128,256]{1,0:T(8,128)S(1)}, u32[]{:S(2)}, u32[]{:S(2)}) collective-permute-start(f32[128,256]{1,0:T(8,128)} %refs_0_.1), channel_id=1, source_target_pairs={{0,1},{1,0},{2,3},{3,2},{4,5},{5,4},{6,7},{7,6},{8,9},{9,8},{10,11... | collective-permute-start | bytes 393224 | tf_op jit(solution)/shard_map/ppermute | solution.py:247
  8.7 8.9 %collective-permute-start.3 = (f32[128,256]{1,0:T(8,128)S(1)}, f32[128,256]{1,0:T(8,128)S(1)}, u32[]{:S(2)}, u32[]{:S(2)}) collective-permute-start(f32[128,256]{1,0:T(8,128)S(1)} %collective-permute-done.1.refs_1_), channel_id=1, source_target_pairs={{0,1},{1,0},{2,3},{3,2},{4,5},{5,4},{6,7},{7,6},{8,9},{9,8},{10,11... | collective-permute-start | bytes 393224 | tf_op jit(solution)/shard_map/ppermute | solution.py:247
  12.0 6.6 %collective-permute-start.4 = (f32[128,256]{1,0:T(8,128)S(1)}, f32[128,256]{1,0:T(8,128)S(1)}, u32[]{:S(2)}, u32[]{:S(2)}) collective-permute-start(f32[128,256]{1,0:T(8,128)S(1)} %collective-permute-done.refs_2_), channel_id=1, source_target_pairs={{0,3},{1,2},{2,1},{3,0},{4,7},{5,6},{6,5},{7,4},{8,11},{9,10},{10,... | collective-permute-start | bytes 393224 | tf_op jit(solution)/shard_map/ppermute | solution.py:247
  13.4 6.1 %collective-permute-start.5 = (f32[128,256]{1,0:T(8,128)S(1)}, f32[128,256]{1,0:T(8,128)S(1)}, u32[]{:S(2)}, u32[]{:S(2)}) collective-permute-start(f32[128,256]{1,0:T(8,128)S(1)} %collective-permute-done.refs_2_), channel_id=1, source_target_pairs={{0,1},{1,0},{2,3},{3,2},{4,5},{5,4},{6,7},{7,6},{8,9},{9,8},{10,11... | collective-permute-start | bytes 393224 | tf_op jit(solution)/shard_map/ppermute | solution.py:247
  13.9 5.6 %collective-permute-start.6 = (f32[128,256]{1,0:T(8,128)S(1)}, f32[128,256]{1,0:T(8,128)S(1)}, u32[]{:S(2)}, u32[]{:S(2)}) collective-permute-start(f32[128,256]{1,0:T(8,128)S(1)} %collective-permute-done.refs_2_), channel_id=1, source_target_pairs={{0,2},{1,3},{2,0},{3,1},{4,6},{5,7},{6,4},{7,5},{8,10},{9,11},{10,... | collective-permute-start | bytes 393224 | tf_op jit(solution)/shard_map/ppermute | solution.py:247
  17.6 5.1 %copy-start.2 = (f32[256,256]{1,0:T(8,128)S(1)}, f32[256,256]{1,0:T(8,128)}, u32[]{:S(2)}) copy-start(f32[256,256]{1,0:T(8,128)} %ws_ref.1) | copy-start | bytes 786436
  17.6 5.1 %copy-start.3 = (f32[256]{0:T(256)S(1)}, f32[256]{0:T(256)}, u32[]{:S(2)}) copy-start(f32[256]{0:T(256)} %b_ref.1) | copy-start | bytes 3076
  17.7 9.3 %copy-start.1 = (f32[256,256]{1,0:T(8,128)S(1)}, f32[256,256]{1,0:T(8,128)}, u32[]{:S(2)}) copy-start(f32[256,256]{1,0:T(8,128)} %wn_ref.1) | copy-start | bytes 786436
  19.7 1.4 %collective-permute-start.8 = (f32[136,256]{1,0:T(8,128)S(1)}, f32[136,256]{1,0:T(8,128)S(1)}, u32[]{:S(2)}, u32[]{:S(2)}) collective-permute-start(f32[136,256]{1,0:T(8,128)S(1)} %late_products.3), channel_id=1, source_target_pairs={{0,8},{8,0},{16,24},{24,16},{1,9},{9,1},{17,25},{25,17},{2,10},{10... | collective-permute-start | bytes 417800 | tf_op jit(solution)/shard_map/ppermute | solution.py:247
  20.1 2.8 %collective-permute-start.7 = (f32[136,256]{1,0:T(8,128)S(1)}, f32[136,256]{1,0:T(8,128)S(1)}, u32[]{:S(2)}, u32[]{:S(2)}) collective-permute-start(f32[136,256]{1,0:T(8,128)S(1)} %get-tuple-element.18), channel_id=1, source_target_pairs={{0,8},{8,0},{16,24},{24,16},{1,9},{9,1},{17,25},{25,17},{2,10},{10... | collective-permute-start | bytes 417800 | tf_op jit(solution)/shard_map/ppermute | solution.py:247
  21.1 5.8 %collective-permute-start.9 = (f32[136,256]{1,0:T(8,128)S(1)}, f32[136,256]{1,0:T(8,128)S(1)}, u32[]{:S(2)}, u32[]{:S(2)}) collective-permute-start(f32[136,256]{1,0:T(8,128)S(1)} %fold_sums.1), channel_id=1, source_target_pairs={{0,16},{8,24},{16,0},{24,8},{1,17},{9,25},{17,1},{25,9},{2,18},{10... | collective-permute-start | bytes 417800 | tf_op jit(solution)/shard_map/ppermute | solution.py:247

commit v7 on v6

--- a/solution.py
+++ b/solution.py
@@ -113,19 +113,21 @@
     )(lists, adj)
 
 
-def own_kernel(x_ref, ws_ref, b_ref, own_ref):
+def own_kernel(x_ref, ws_ref, b_ref, wn_ref, own_ref, high_ref, low_ref):
     own_ref[...] = matmul_f32(x_ref[...], ws_ref[...]) + b_ref[...][None, :]
-
-
-def own_rows(x, ws, b):
+    high_ref[...], low_ref[...] = split_bf16(wn_ref[...])
+
+
+def own_rows(x, ws, b, wn):
+    half = jax.ShapeDtypeStruct(wn.shape, jnp.bfloat16)
     return pl.pallas_call(
         own_kernel,
-        in_specs=[whole(pltpu.VMEM)] * 3,
-        out_specs=whole(pltpu.VMEM),
-        out_shape=jax.ShapeDtypeStruct((x.shape[0], ws.shape[1]), jnp.float32),
+        in_specs=[whole(pltpu.VMEM)] * 4,
+        out_specs=[whole(pltpu.VMEM)] * 3,
+        out_shape=[jax.ShapeDtypeStruct((x.shape[0], ws.shape[1]), jnp.float32), half, half],
         compiler_params=pltpu.CompilerParams(vmem_limit_bytes=VMEM_BYTES),
         name="own_rows",
-    )(x, ws, b)
+    )(x, ws, b, wn)
 
 
 def product_rows(a_ref, tile_refs, masks, halves, rows):
@@ -214,28 +216,27 @@
     )(a, deg, acc, *tiles)
 
 
-def finish_kernel(own_ref, wn_ref, *refs):
-    part_refs, out_ref = refs[:-1], refs[-1]
+def finish_kernel(own_ref, high_ref, low_ref, here_ref, came_ref, out_ref):
     tile, width = own_ref.shape
-    total = part_refs[0][...]
-    for ref in part_refs[1:]:
-        total = total + ref[...]
+    total = here_ref[...] + came_ref[...]
     degree = jnp.broadcast_to(total[tile : tile + 1, 0:tile], (tile, tile)).T
     scale = 1.0 / jnp.maximum(degree, 1.0)
     scale = jnp.concatenate([scale] * (width // tile), axis=1)
-    product = matmul_f32(total[0:tile, :], wn_ref[...])
+    high, low = split_bf16(total[0:tile, :])
+    dot = functools.partial(jnp.dot, preferred_element_type=jnp.float32)
+    product = dot(high, high_ref[...]) + dot(high, low_ref[...]) + dot(low, high_ref[...])
     out_ref[...] = jnp.maximum(own_ref[...] + product * scale, 0.0)
 
 
-def finish(own, wn, parts):
+def finish(own, high, low, here, came):
     return pl.pallas_call(
         finish_kernel,
-        in_specs=[whole(pltpu.VMEM)] * (2 + len(parts)),
+        in_specs=[whole(pltpu.VMEM)] * 5,
         out_specs=whole(pltpu.VMEM),
         out_shape=jax.ShapeDtypeStruct(own.shape, jnp.float32),
         compiler_params=pltpu.CompilerParams(vmem_limit_bytes=VMEM_BYTES),
         name="finish_rows",
-    )(own, wn, *parts)
+    )(own, high, low, here, came)
 
 
 def after(value, *earlier):
@@ -273,7 +274,7 @@
     a, deg = combine(adj_tiles, lists, n_col, n_row)
     last = [mask for mask in tiles if mask not in first]
     acc = early(a, [tiles[mask] for mask in first], first)
-    own = own_rows(features, self_weight, layer_bias)
+    own, high, low = own_rows(features, self_weight, layer_bias, neighbor_weight)
 
     split = max(3, n_row // 2)
     groups = [range(split, n_row), range(split)]
@@ -284,8 +285,8 @@
         blocks = [fold(blocks[m], exchange(blocks[m | bit], "row", bit)) for m in range(bit)]
     own_sum, beside, across, both = blocks
     across = exchange(fold(across, exchange(both, "row", 1)), "row", 2)
-    beside = after(exchange(beside, "row", 1), across)
-    return finish(own, neighbor_weight, [own_sum, beside, across])
+    here = fold(own_sum, exchange(beside, "row", 1))
+    return finish(own, high, low, here, across)
 
 
 def solution(mesh):

time: 28 us -> 28 us (level)
  waiting for transfers between devices: 7.42 us -> 6.19 us
  Pallas kernels: 4.33 us -> 5.53 us
    ppermute x10, waiting for transfers between devices: 7.42 us -> 6.19 us  [exchange(): return lax.ppermute(value, axis, pairs)]
    pallas_call x1, Pallas kernels: 2.14 us -> 3.32 us  [combine(): pl.pallas_call(combine_kernel, in_specs=[whole(pltpu.HBM)] * 2, out_specs...]
  transfers between devices with their start and end apart: 10 -> 10, of which waited for: 6 -> 5; matrix products, arithmetic and copies ran while one was open for 3% -> 3% of each run, Pallas kernels for 12% -> 16%
where the time goes in v7:
time: 28 us; the launch traced here: 27.8 us
  starting transfers between devices  14.5 us (52%)
  waiting for transfers between devices  6.19 us (22%)
  Pallas kernels  5.53 us (20%)
  between operations  0.79 us (3%)
  other arithmetic  0.75 us (3%)
    ppermute x10, starting transfers between devices, exchange(): return lax.ppermute(value, axis, pairs)  14.5 us
    ppermute x10, waiting for transfers between devices, exchange(): return lax.ppermute(value, axis, pairs)  6.19 us
    pallas_call x1, Pallas kernels, combine(): pl.pallas_call(combine_kernel, in_specs=[whole(pltpu.HBM)] * 2, out_specs...  3.32 us
    pallas_call x1, Pallas kernels, finish(): pl.pallas_call(finish_kernel, in_specs=[whole(pltpu.VMEM)] * 5, out_specs...  0.88 us
    concatenate x1, other arithmetic, on_device(): jnp.concatenate([tile_dst[0, 0], tile_src[0, 0], tile_count[0], jnp.zeros...  0.75 us
  transfers between devices with their start and end apart: 10, of which 5 were waited for; matrix products, arithmetic and copies ran while one was open for 3% of the time, Pallas kernels for 16%

profile of v7, /device:TPU:0, one launch (start us, length us, event | category | flops | bytes accessed | tf_op | source)
XLA Modules:
  0.0 27.8 jit_solution(11982573604311678755)
XLA Ops:
  0.0 0.0 copy-start
  0.0 3.0 %collective-permute-start.1 = (f32[128,256]{1,0:T(8,128)}, f32[128,256]{1,0:T(8,128)S(1)}, u32[]{:S(2)}, u32[]{:S(2)}) collective-permute-start(f32[128,256]{1,0:T(8,128)} %refs_0_.1), channel_id=1, source_target_pairs={{0,2},{1,3},{2,0},{3,1},{4,6},{5,7},{6,4},{7,5},{8,10},{9,11},{10,... | collective-permute-start | bytes 393224 | tf_op jit(solution)/shard_map/ppermute | solution.py:248
  3.0 2.6 %collective-permute-start = (f32[128,256]{1,0:T(8,128)}, f32[128,256]{1,0:T(8,128)S(1)}, u32[]{:S(2)}, u32[]{:S(2)}) collective-permute-start(f32[128,256]{1,0:T(8,128)} %refs_0_.1), channel_id=1, source_target_pairs={{0,4},{1,5},{2,6},{3,7},{4,0},{5,1},{6,2},{7,3},{8,12},{9,13},{10,... | collective-permute-start | bytes 393224 | tf_op jit(solution)/shard_map/ppermute | solution.py:248
  5.6 1.5 %collective-permute-start.2 = (f32[128,256]{1,0:T(8,128)}, f32[128,256]{1,0:T(8,128)S(1)}, u32[]{:S(2)}, u32[]{:S(2)}) collective-permute-start(f32[128,256]{1,0:T(8,128)} %refs_0_.1), channel_id=1, source_target_pairs={{0,1},{1,0},{2,3},{3,2},{4,5},{5,4},{6,7},{7,6},{8,9},{9,8},{10,11... | collective-permute-start | bytes 393224 | tf_op jit(solution)/shard_map/ppermute | solution.py:248
  7.8 0.8 %pad_add_fusion.lists_hbm = s32[256]{0:T(256)S(1)} fusion(s32[63]{0:T(128)S(1)} %broadcast_in_dim.3, s32[1]{0:T(128)} %bitcast.3, s32[96]{0:T(128)} %bitcast.4, s32[96]{0:T(128)} %bitcast.5), kind=kLoop, calls=%fused_computation | loop fusion | flops 768 | bytes 2048 | tf_op jit(solution)/shard_map/concatenate | solution.py:258
  8.6 0.1 collective-permute-done.1.refs_1_
  8.7 1.7 %collective-permute-start.3 = (f32[128,256]{1,0:T(8,128)S(1)}, f32[128,256]{1,0:T(8,128)S(1)}, u32[]{:S(2)}, u32[]{:S(2)}) collective-permute-start(f32[128,256]{1,0:T(8,128)S(1)} %collective-permute-done.1.refs_1_), channel_id=1, source_target_pairs={{0,1},{1,0},{2,3},{3,2},{4,5},{5,4},{6,7},{7,6},{8,9},{9,8},{10,11... | collective-permute-start | bytes 393224 | tf_op jit(solution)/shard_map/ppermute | solution.py:248
  10.4 1.6 %collective-permute-done.refs_2_ = f32[128,256]{1,0:T(8,128)S(1)} collective-permute-done((f32[128,256]{1,0:T(8,128)}, f32[128,256]{1,0:T(8,128)S(1)}, u32[]{:S(2)}, u32[]{:S(2)}) %collective-permute-start) | collective-permute-done | bytes 131104 | tf_op jit(solution)/shard_map/ppermute | solution.py:248
  12.0 1.4 %collective-permute-start.4 = (f32[128,256]{1,0:T(8,128)S(1)}, f32[128,256]{1,0:T(8,128)S(1)}, u32[]{:S(2)}, u32[]{:S(2)}) collective-permute-start(f32[128,256]{1,0:T(8,128)S(1)} %collective-permute-done.refs_2_), channel_id=1, source_target_pairs={{0,3},{1,2},{2,1},{3,0},{4,7},{5,6},{6,5},{7,4},{8,11},{9,10},{10,... | collective-permute-start | bytes 393224 | tf_op jit(solution)/shard_map/ppermute | solution.py:248
  13.4 0.5 %collective-permute-start.5 = (f32[128,256]{1,0:T(8,128)S(1)}, f32[128,256]{1,0:T(8,128)S(1)}, u32[]{:S(2)}, u32[]{:S(2)}) collective-permute-start(f32[128,256]{1,0:T(8,128)S(1)} %collective-permute-done.refs_2_), channel_id=1, source_target_pairs={{0,1},{1,0},{2,3},{3,2},{4,5},{5,4},{6,7},{7,6},{8,9},{9,8},{10,11... | collective-permute-start | bytes 393224 | tf_op jit(solution)/shard_map/ppermute | solution.py:248
  13.9 1.6 %collective-permute-start.6 = (f32[128,256]{1,0:T(8,128)S(1)}, f32[128,256]{1,0:T(8,128)S(1)}, u32[]{:S(2)}, u32[]{:S(2)}) collective-permute-start(f32[128,256]{1,0:T(8,128)S(1)} %collective-permute-done.refs_2_), channel_id=1, source_target_pairs={{0,2},{1,3},{2,0},{3,1},{4,6},{5,7},{6,4},{7,5},{8,10},{9,11},{10,... | collective-permute-start | bytes 393224 | tf_op jit(solution)/shard_map/ppermute | solution.py:248
  15.5 3.3 %combine_tiles.1 = (bf16[8,512,128]{2,1,0:T(8,128)(2,1)S(1)}, f32[4,8,128]{2,1,0:T(8,128)S(1)}) custom-call(s32[256]{0:T(256)S(1)} %pad_add_fusion.lists_hbm, bf16[1,1,96,128,128]{4,3,2,1,0:T(8,128)(2,1)} %adj_hbm.1), custom_call_target="tpu_custom_call" | custom-call | tf_op jit(solution)/shard_map/combine_tiles/pallas_call | solution.py:97
  18.8 0.0 collective-permute-done.2.refs_3_
  18.8 0.0 collective-permute-done.3.refs_4_
  18.8 0.0 copy-done
  18.8 0.0 copy-start.1
  18.8 0.0 copy-start.2
  18.8 0.0 copy-start.3
  18.8 0.5 %early_products.1.acc_ref = f32[512,256]{1,0:T(8,128)S(1)} custom-call(bf16[8,512,128]{2,1,0:T(8,128)(2,1)S(1)} %get-tuple-element.19.a_ref, f32[128,256]{1,0:T(8,128)S(1)} %copy-done, f32[128,256]{1,0:T(8,128)S(1)} %collective-permute-done.1.refs_1_, f32[128,256]{1,0:T(8,128)S(1)} %collective-permute-done.refs_2_, ...), custom_call_target="tpu_custom_call" | custom-call | tf_op jit(solution)/shard_map/early_products/pallas_call | solution.py:195
  19.4 0.0 collective-permute-done.4.refs_0_
  19.4 0.1 collective-permute-done.5.refs_1_
  19.5 0.0 collective-permute-done.6.refs_2_
  19.5 0.2 late_products.3
  19.7 0.1 collective-permute-start.8
  19.8 0.3 %late_products.2 = (f32[136,256]{1,0:T(8,128)S(1)}, f32[136,256]{1,0:T(8,128)S(1)}, f32[136,256]{1,0:T(8,128)S(1)}) custom-call(bf16[8,512,128]{2,1,0:T(8,128)(2,1)S(1)} %get-tuple-element.19.a_ref, f32[4,8,128]{2,1,0:T(8,128)S(1)} %get-tuple-element.20.deg_ref, f32[512,256]{1,0:T(8,128)S(1)} %early_products.1.acc_ref, ...), custom_call_target="tpu_custom_call" | custom-call | tf_op jit(solution)/shard_map/late_products/pallas_call | solution.py:208
  20.1 0.6 %collective-permute-start.7 = (f32[136,256]{1,0:T(8,128)S(1)}, f32[136,256]{1,0:T(8,128)S(1)}, u32[]{:S(2)}, u32[]{:S(2)}) collective-permute-start(f32[136,256]{1,0:T(8,128)S(1)} %get-tuple-element.23), channel_id=1, source_target_pairs={{0,8},{8,0},{16,24},{24,16},{1,9},{9,1},{17,25},{25,17},{2,10},{10... | collective-permute-start | bytes 417800 | tf_op jit(solution)/shard_map/ppermute | solution.py:248
  20.7 0.4 %collective-permute-done.8.came_ref = f32[136,256]{1,0:T(8,128)S(1)} collective-permute-done((f32[136,256]{1,0:T(8,128)S(1)}, f32[136,256]{1,0:T(8,128)S(1)}, u32[]{:S(2)}, u32[]{:S(2)}) %collective-permute-start.8) | collective-permute-done | bytes 139296 | tf_op jit(solution)/shard_map/ppermute | solution.py:248
  21.1 1.6 %collective-permute-start.9 = (f32[136,256]{1,0:T(8,128)S(1)}, f32[136,256]{1,0:T(8,128)S(1)}, u32[]{:S(2)}, u32[]{:S(2)}) collective-permute-start(f32[136,256]{1,0:T(8,128)S(1)} %fold_sums.3), channel_id=1, source_target_pairs={{0,16},{8,24},{16,0},{24,8},{1,17},{9,25},{17,1},{25,9},{2,18},{10... | collective-permute-start | bytes 417800 | tf_op jit(solution)/shard_map/ppermute | solution.py:248
  22.7 0.0 copy-done.1
  22.7 0.0 copy-done.2
  22.7 0.0 copy-done.3
  22.7 0.2 own_rows.1
  22.9 0.0 collective-permute-done.7.came_ref
  23.0 4.0 %collective-permute-done.9.came_ref = f32[136,256]{1,0:T(8,128)S(1)} collective-permute-done((f32[136,256]{1,0:T(8,128)S(1)}, f32[136,256]{1,0:T(8,128)S(1)}, u32[]{:S(2)}, u32[]{:S(2)}) %collective-permute-start.9) | collective-permute-done | bytes 139296 | tf_op jit(solution)/shard_map/ppermute | solution.py:248
  26.9 0.9 %finish_rows.1 = f32[128,256]{1,0:T(8,128)} custom-call(f32[128,256]{1,0:T(8,128)S(1)} %get-tuple-element.15.own_ref, bf16[256,256]{1,0:T(8,128)(2,1)S(1)} %get-tuple-element.16.high_ref, bf16[256,256]{1,0:T(8,128)(2,1)S(1)} %get-tuple-element.17.low_ref, f32[136,256]{1,0:T(8,128)S(1)} %fold_sums.2.here_ref, f32[136,256]{1,0:T(8,128)S(1)} %collective-permute-done.9.came_ref), custom_call_target="tpu_custom_call" | custom-call | tf_op jit(solution)/shard_map/finish_rows/pallas_call | solution.py:232
  (3 shorter events, 0.0 us)
Async XLA Ops:
  0.0 18.8 %copy-start = (f32[128,256]{1,0:T(8,128)S(1)}, f32[128,256]{1,0:T(8,128)}, u32[]{:S(2)}) copy-start(f32[128,256]{1,0:T(8,128)} %refs_0_.1) | copy-start | bytes 393220
  0.0 8.7 %collective-permute-start.1 = (f32[128,256]{1,0:T(8,128)}, f32[128,256]{1,0:T(8,128)S(1)}, u32[]{:S(2)}, u32[]{:S(2)}) collective-permute-start(f32[128,256]{1,0:T(8,128)} %refs_0_.1), channel_id=1, source_target_pairs={{0,2},{1,3},{2,0},{3,1},{4,6},{5,7},{6,4},{7,5},{8,10},{9,11},{10,... | collective-permute-start | bytes 393224 | tf_op jit(solution)/shard_map/ppermute | solution.py:248
  3.0 8.9 %collective-permute-start = (f32[128,256]{1,0:T(8,128)}, f32[128,256]{1,0:T(8,128)S(1)}, u32[]{:S(2)}, u32[]{:S(2)}) collective-permute-start(f32[128,256]{1,0:T(8,128)} %refs_0_.1), channel_id=1, source_target_pairs={{0,4},{1,5},{2,6},{3,7},{4,0},{5,1},{6,2},{7,3},{8,12},{9,13},{10,... | collective-permute-start | bytes 393224 | tf_op jit(solution)/shard_map/ppermute | solution.py:248
  5.6 13.2 %collective-permute-start.2 = (f32[128,256]{1,0:T(8,128)}, f32[128,256]{1,0:T(8,128)S(1)}, u32[]{:S(2)}, u32[]{:S(2)}) collective-permute-start(f32[128,256]{1,0:T(8,128)} %refs_0_.1), channel_id=1, source_target_pairs={{0,1},{1,0},{2,3},{3,2},{4,5},{5,4},{6,7},{7,6},{8,9},{9,8},{10,11... | collective-permute-start | bytes 393224 | tf_op jit(solution)/shard_map/ppermute | solution.py:248
  8.7 10.1 %collective-permute-start.3 = (f32[128,256]{1,0:T(8,128)S(1)}, f32[128,256]{1,0:T(8,128)S(1)}, u32[]{:S(2)}, u32[]{:S(2)}) collective-permute-start(f32[128,256]{1,0:T(8,128)S(1)} %collective-permute-done.1.refs_1_), channel_id=1, source_target_pairs={{0,1},{1,0},{2,3},{3,2},{4,5},{5,4},{6,7},{7,6},{8,9},{9,8},{10,11... | collective-permute-start | bytes 393224 | tf_op jit(solution)/shard_map/ppermute | solution.py:248
  12.0 7.4 %collective-permute-start.4 = (f32[128,256]{1,0:T(8,128)S(1)}, f32[128,256]{1,0:T(8,128)S(1)}, u32[]{:S(2)}, u32[]{:S(2)}) collective-permute-start(f32[128,256]{1,0:T(8,128)S(1)} %collective-permute-done.refs_2_), channel_id=1, source_target_pairs={{0,3},{1,2},{2,1},{3,0},{4,7},{5,6},{6,5},{7,4},{8,11},{9,10},{10,... | collective-permute-start | bytes 393224 | tf_op jit(solution)/shard_map/ppermute | solution.py:248
  13.4 6.1 %collective-permute-start.5 = (f32[128,256]{1,0:T(8,128)S(1)}, f32[128,256]{1,0:T(8,128)S(1)}, u32[]{:S(2)}, u32[]{:S(2)}) collective-permute-start(f32[128,256]{1,0:T(8,128)S(1)} %collective-permute-done.refs_2_), channel_id=1, source_target_pairs={{0,1},{1,0},{2,3},{3,2},{4,5},{5,4},{6,7},{7,6},{8,9},{9,8},{10,11... | collective-permute-start | bytes 393224 | tf_op jit(solution)/shard_map/ppermute | solution.py:248
  13.9 5.6 %collective-permute-start.6 = (f32[128,256]{1,0:T(8,128)S(1)}, f32[128,256]{1,0:T(8,128)S(1)}, u32[]{:S(2)}, u32[]{:S(2)}) collective-permute-start(f32[128,256]{1,0:T(8,128)S(1)} %collective-permute-done.refs_2_), channel_id=1, source_target_pairs={{0,2},{1,3},{2,0},{3,1},{4,6},{5,7},{6,4},{7,5},{8,10},{9,11},{10,... | collective-permute-start | bytes 393224 | tf_op jit(solution)/shard_map/ppermute | solution.py:248
  18.8 3.9 %copy-start.1 = (f32[256,256]{1,0:T(8,128)S(1)}, f32[256,256]{1,0:T(8,128)}, u32[]{:S(2)}) copy-start(f32[256,256]{1,0:T(8,128)} %ws_ref.1) | copy-start | bytes 786436
  18.8 3.9 %copy-start.2 = (f32[256,256]{1,0:T(8,128)S(1)}, f32[256,256]{1,0:T(8,128)}, u32[]{:S(2)}) copy-start(f32[256,256]{1,0:T(8,128)} %wn_ref.1) | copy-start | bytes 786436
  18.8 3.9 %copy-start.3 = (f32[256]{0:T(256)S(1)}, f32[256]{0:T(256)}, u32[]{:S(2)}) copy-start(f32[256]{0:T(256)} %b_ref.1) | copy-start | bytes 3076
  19.7 1.4 %collective-permute-start.8 = (f32[136,256]{1,0:T(8,128)S(1)}, f32[136,256]{1,0:T(8,128)S(1)}, u32[]{:S(2)}, u32[]{:S(2)}) collective-permute-start(f32[136,256]{1,0:T(8,128)S(1)} %late_products.3), channel_id=1, source_target_pairs={{0,8},{8,0},{16,24},{24,16},{1,9},{9,1},{17,25},{25,17},{2,10},{10... | collective-permute-start | bytes 417800 | tf_op jit(solution)/shard_map/ppermute | solution.py:248
  20.1 2.8 %collective-permute-start.7 = (f32[136,256]{1,0:T(8,128)S(1)}, f32[136,256]{1,0:T(8,128)S(1)}, u32[]{:S(2)}, u32[]{:S(2)}) collective-permute-start(f32[136,256]{1,0:T(8,128)S(1)} %get-tuple-element.23), channel_id=1, source_target_pairs={{0,8},{8,0},{16,24},{24,16},{1,9},{9,1},{17,25},{25,17},{2,10},{10... | collective-permute-start | bytes 417800 | tf_op jit(solution)/shard_map/ppermute | solution.py:248
  21.1 5.8 %collective-permute-start.9 = (f32[136,256]{1,0:T(8,128)S(1)}, f32[136,256]{1,0:T(8,128)S(1)}, u32[]{:S(2)}, u32[]{:S(2)}) collective-permute-start(f32[136,256]{1,0:T(8,128)S(1)} %fold_sums.3), channel_id=1, source_target_pairs={{0,16},{8,24},{16,0},{24,8},{1,17},{9,25},{17,1},{25,9},{2,18},{10... | collective-permute-start | bytes 417800 | tf_op jit(solution)/shard_map/ppermute | solution.py:248

commit v8 on v7

--- a/solution.py
+++ b/solution.py
@@ -9,7 +9,7 @@
 
 CHUNK = 8
 PAD = 8
-EAGER = 4
+EAGER = 8
 VMEM_BYTES = 32 * 1024 * 1024
 COMBINE_VMEM = 51 * 1024 * 1024
 

time: 28 us -> 28 us (level)
  waiting for transfers between devices: 6.19 us -> 7.08 us
  Pallas kernels: 5.53 us -> 4.65 us
    ppermute x10, waiting for transfers between devices: 6.19 us -> 7.08 us  [exchange(): return lax.ppermute(value, axis, pairs)]
    pallas_call x1, Pallas kernels: 3.32 us -> 2.44 us  [combine(): pl.pallas_call(combine_kernel, in_specs=[whole(pltpu.HBM)] * 2, out_specs...]
  transfers between devices with their start and end apart: 10 -> 10, of which waited for: 5 -> 6; matrix products, arithmetic and copies ran while one was open for 3% -> 3% of each run, Pallas kernels for 16% -> 13%
where the time goes in v8:
time: 28 us; the launch traced here: 27.8 us
  starting transfers between devices  14.5 us (52%)
  waiting for transfers between devices  7.08 us (25%)
  Pallas kernels  4.65 us (17%)
  between operations  0.78 us (3%)
  other arithmetic  0.75 us (3%)
    ppermute x10, starting transfers between devices, exchange(): return lax.ppermute(value, axis, pairs)  14.5 us
    ppermute x10, waiting for transfers between devices, exchange(): return lax.ppermute(value, axis, pairs)  7.08 us
    pallas_call x1, Pallas kernels, combine(): pl.pallas_call(combine_kernel, in_specs=[whole(pltpu.HBM)] * 2, out_specs...  2.44 us
    pallas_call x1, Pallas kernels, finish(): pl.pallas_call(finish_kernel, in_specs=[whole(pltpu.VMEM)] * 5, out_specs...  0.88 us
    concatenate x1, other arithmetic, on_device(): jnp.concatenate([tile_dst[0, 0], tile_src[0, 0], tile_count[0], jnp.zeros...  0.75 us
  transfers between devices with their start and end apart: 10, of which 6 were waited for; matrix products, arithmetic and copies ran while one was open for 3% of the time, Pallas kernels for 13%

profile of v8, /device:TPU:0, one launch (start us, length us, event | category | flops | bytes accessed | tf_op | source)
XLA Modules:
  0.0 27.8 jit_solution(16583597236323457894)
XLA Ops:
  0.0 0.0 copy-start
  0.0 3.0 %collective-permute-start.1 = (f32[128,256]{1,0:T(8,128)}, f32[128,256]{1,0:T(8,128)S(1)}, u32[]{:S(2)}, u32[]{:S(2)}) collective-permute-start(f32[128,256]{1,0:T(8,128)} %refs_0_.1), channel_id=1, source_target_pairs={{0,2},{1,3},{2,0},{3,1},{4,6},{5,7},{6,4},{7,5},{8,10},{9,11},{10,... | collective-permute-start | bytes 393224 | tf_op jit(solution)/shard_map/ppermute | solution.py:248
  3.0 2.6 %collective-permute-start = (f32[128,256]{1,0:T(8,128)}, f32[128,256]{1,0:T(8,128)S(1)}, u32[]{:S(2)}, u32[]{:S(2)}) collective-permute-start(f32[128,256]{1,0:T(8,128)} %refs_0_.1), channel_id=1, source_target_pairs={{0,4},{1,5},{2,6},{3,7},{4,0},{5,1},{6,2},{7,3},{8,12},{9,13},{10,... | collective-permute-start | bytes 393224 | tf_op jit(solution)/shard_map/ppermute | solution.py:248
  5.6 1.5 %collective-permute-start.2 = (f32[128,256]{1,0:T(8,128)}, f32[128,256]{1,0:T(8,128)S(1)}, u32[]{:S(2)}, u32[]{:S(2)}) collective-permute-start(f32[128,256]{1,0:T(8,128)} %refs_0_.1), channel_id=1, source_target_pairs={{0,1},{1,0},{2,3},{3,2},{4,5},{5,4},{6,7},{7,6},{8,9},{9,8},{10,11... | collective-permute-start | bytes 393224 | tf_op jit(solution)/shard_map/ppermute | solution.py:248
  7.8 0.8 %pad_add_fusion.lists_hbm = s32[256]{0:T(256)S(1)} fusion(s32[63]{0:T(128)S(1)} %broadcast_in_dim.3, s32[1]{0:T(128)} %bitcast.3, s32[96]{0:T(128)} %bitcast.4, s32[96]{0:T(128)} %bitcast.5), kind=kLoop, calls=%fused_computation | loop fusion | flops 768 | bytes 2048 | tf_op jit(solution)/shard_map/concatenate | solution.py:258
  8.6 0.1 collective-permute-done.1.refs_1_
  8.7 1.7 %collective-permute-start.3 = (f32[128,256]{1,0:T(8,128)S(1)}, f32[128,256]{1,0:T(8,128)S(1)}, u32[]{:S(2)}, u32[]{:S(2)}) collective-permute-start(f32[128,256]{1,0:T(8,128)S(1)} %collective-permute-done.1.refs_1_), channel_id=1, source_target_pairs={{0,1},{1,0},{2,3},{3,2},{4,5},{5,4},{6,7},{7,6},{8,9},{9,8},{10,11... | collective-permute-start | bytes 393224 | tf_op jit(solution)/shard_map/ppermute | solution.py:248
  10.4 1.6 %collective-permute-done.refs_2_ = f32[128,256]{1,0:T(8,128)S(1)} collective-permute-done((f32[128,256]{1,0:T(8,128)}, f32[128,256]{1,0:T(8,128)S(1)}, u32[]{:S(2)}, u32[]{:S(2)}) %collective-permute-start) | collective-permute-done | bytes 131104 | tf_op jit(solution)/shard_map/ppermute | solution.py:248
  12.0 1.4 %collective-permute-start.4 = (f32[128,256]{1,0:T(8,128)S(1)}, f32[128,256]{1,0:T(8,128)S(1)}, u32[]{:S(2)}, u32[]{:S(2)}) collective-permute-start(f32[128,256]{1,0:T(8,128)S(1)} %collective-permute-done.refs_2_), channel_id=1, source_target_pairs={{0,3},{1,2},{2,1},{3,0},{4,7},{5,6},{6,5},{7,4},{8,11},{9,10},{10,... | collective-permute-start | bytes 393224 | tf_op jit(solution)/shard_map/ppermute | solution.py:248
  13.4 0.5 %collective-permute-start.5 = (f32[128,256]{1,0:T(8,128)S(1)}, f32[128,256]{1,0:T(8,128)S(1)}, u32[]{:S(2)}, u32[]{:S(2)}) collective-permute-start(f32[128,256]{1,0:T(8,128)S(1)} %collective-permute-done.refs_2_), channel_id=1, source_target_pairs={{0,1},{1,0},{2,3},{3,2},{4,5},{5,4},{6,7},{7,6},{8,9},{9,8},{10,11... | collective-permute-start | bytes 393224 | tf_op jit(solution)/shard_map/ppermute | solution.py:248
  13.9 1.6 %collective-permute-start.6 = (f32[128,256]{1,0:T(8,128)S(1)}, f32[128,256]{1,0:T(8,128)S(1)}, u32[]{:S(2)}, u32[]{:S(2)}) collective-permute-start(f32[128,256]{1,0:T(8,128)S(1)} %collective-permute-done.refs_2_), channel_id=1, source_target_pairs={{0,2},{1,3},{2,0},{3,1},{4,6},{5,7},{6,4},{7,5},{8,10},{9,11},{10,... | collective-permute-start | bytes 393224 | tf_op jit(solution)/shard_map/ppermute | solution.py:248
  15.5 2.4 %combine_tiles.1 = (bf16[8,512,128]{2,1,0:T(8,128)(2,1)S(1)}, f32[4,8,128]{2,1,0:T(8,128)S(1)}) custom-call(s32[256]{0:T(256)S(1)} %pad_add_fusion.lists_hbm, bf16[1,1,96,128,128]{4,3,2,1,0:T(8,128)(2,1)} %adj_hbm.1), custom_call_target="tpu_custom_call" | custom-call | tf_op jit(solution)/shard_map/combine_tiles/pallas_call | solution.py:97
  17.9 0.0 collective-permute-done.2.refs_3_
  17.9 0.0 collective-permute-done.3.refs_4_
  17.9 0.0 copy-done
  17.9 0.0 copy-start.1
  17.9 0.0 copy-start.2
  18.0 0.0 copy-start.3
  18.0 0.5 %early_products.1.acc_ref = f32[512,256]{1,0:T(8,128)S(1)} custom-call(bf16[8,512,128]{2,1,0:T(8,128)(2,1)S(1)} %get-tuple-element.19.a_ref, f32[128,256]{1,0:T(8,128)S(1)} %copy-done, f32[128,256]{1,0:T(8,128)S(1)} %collective-permute-done.1.refs_1_, f32[128,256]{1,0:T(8,128)S(1)} %collective-permute-done.refs_2_, ...), custom_call_target="tpu_custom_call" | custom-call | tf_op jit(solution)/shard_map/early_products/pallas_call | solution.py:195
  18.5 0.1 collective-permute-done.4.refs_0_
  18.6 0.9 %collective-permute-done.5.refs_1_ = f32[128,256]{1,0:T(8,128)S(1)} collective-permute-done((f32[128,256]{1,0:T(8,128)S(1)}, f32[128,256]{1,0:T(8,128)S(1)}, u32[]{:S(2)}, u32[]{:S(2)}) %collective-permute-start.5) | collective-permute-done | bytes 131104 | tf_op jit(solution)/shard_map/ppermute | solution.py:248
  19.5 0.0 collective-permute-done.6.refs_2_
  19.5 0.2 late_products.3
  19.7 0.1 collective-permute-start.8
  19.8 0.3 %late_products.2 = (f32[136,256]{1,0:T(8,128)S(1)}, f32[136,256]{1,0:T(8,128)S(1)}, f32[136,256]{1,0:T(8,128)S(1)}) custom-call(bf16[8,512,128]{2,1,0:T(8,128)(2,1)S(1)} %get-tuple-element.19.a_ref, f32[4,8,128]{2,1,0:T(8,128)S(1)} %get-tuple-element.20.deg_ref, f32[512,256]{1,0:T(8,128)S(1)} %early_products.1.acc_ref, ...), custom_call_target="tpu_custom_call" | custom-call | tf_op jit(solution)/shard_map/late_products/pallas_call | solution.py:208
  20.1 0.6 %collective-permute-start.7 = (f32[136,256]{1,0:T(8,128)S(1)}, f32[136,256]{1,0:T(8,128)S(1)}, u32[]{:S(2)}, u32[]{:S(2)}) collective-permute-start(f32[136,256]{1,0:T(8,128)S(1)} %get-tuple-element.23), channel_id=1, source_target_pairs={{0,8},{8,0},{16,24},{24,16},{1,9},{9,1},{17,25},{25,17},{2,10},{10... | collective-permute-start | bytes 417800 | tf_op jit(solution)/shard_map/ppermute | solution.py:248
  20.7 0.4 %collective-permute-done.8.came_ref = f32[136,256]{1,0:T(8,128)S(1)} collective-permute-done((f32[136,256]{1,0:T(8,128)S(1)}, f32[136,256]{1,0:T(8,128)S(1)}, u32[]{:S(2)}, u32[]{:S(2)}) %collective-permute-start.8) | collective-permute-done | bytes 139296 | tf_op jit(solution)/shard_map/ppermute | solution.py:248
  21.1 1.6 %collective-permute-start.9 = (f32[136,256]{1,0:T(8,128)S(1)}, f32[136,256]{1,0:T(8,128)S(1)}, u32[]{:S(2)}, u32[]{:S(2)}) collective-permute-start(f32[136,256]{1,0:T(8,128)S(1)} %fold_sums.3), channel_id=1, source_target_pairs={{0,16},{8,24},{16,0},{24,8},{1,17},{9,25},{17,1},{25,9},{2,18},{10... | collective-permute-start | bytes 417800 | tf_op jit(solution)/shard_map/ppermute | solution.py:248
  22.7 0.0 copy-done.1
  22.7 0.0 copy-done.2
  22.7 0.0 copy-done.3
  22.7 0.2 own_rows.1
  22.9 0.0 collective-permute-done.7.came_ref
  23.0 4.0 %collective-permute-done.9.came_ref = f32[136,256]{1,0:T(8,128)S(1)} collective-permute-done((f32[136,256]{1,0:T(8,128)S(1)}, f32[136,256]{1,0:T(8,128)S(1)}, u32[]{:S(2)}, u32[]{:S(2)}) %collective-permute-start.9) | collective-permute-done | bytes 139296 | tf_op jit(solution)/shard_map/ppermute | solution.py:248
  26.9 0.9 %finish_rows.1 = f32[128,256]{1,0:T(8,128)} custom-call(f32[128,256]{1,0:T(8,128)S(1)} %get-tuple-element.15.own_ref, bf16[256,256]{1,0:T(8,128)(2,1)S(1)} %get-tuple-element.16.high_ref, bf16[256,256]{1,0:T(8,128)(2,1)S(1)} %get-tuple-element.17.low_ref, f32[136,256]{1,0:T(8,128)S(1)} %fold_sums.2.here_ref, f32[136,256]{1,0:T(8,128)S(1)} %collective-permute-done.9.came_ref), custom_call_target="tpu_custom_call" | custom-call | tf_op jit(solution)/shard_map/finish_rows/pallas_call | solution.py:232
  (3 shorter events, 0.0 us)
Async XLA Ops:
  0.0 17.9 %copy-start = (f32[128,256]{1,0:T(8,128)S(1)}, f32[128,256]{1,0:T(8,128)}, u32[]{:S(2)}) copy-start(f32[128,256]{1,0:T(8,128)} %refs_0_.1) | copy-start | bytes 393220
  0.0 8.7 %collective-permute-start.1 = (f32[128,256]{1,0:T(8,128)}, f32[128,256]{1,0:T(8,128)S(1)}, u32[]{:S(2)}, u32[]{:S(2)}) collective-permute-start(f32[128,256]{1,0:T(8,128)} %refs_0_.1), channel_id=1, source_target_pairs={{0,2},{1,3},{2,0},{3,1},{4,6},{5,7},{6,4},{7,5},{8,10},{9,11},{10,... | collective-permute-start | bytes 393224 | tf_op jit(solution)/shard_map/ppermute | solution.py:248
  3.0 8.9 %collective-permute-start = (f32[128,256]{1,0:T(8,128)}, f32[128,256]{1,0:T(8,128)S(1)}, u32[]{:S(2)}, u32[]{:S(2)}) collective-permute-start(f32[128,256]{1,0:T(8,128)} %refs_0_.1), channel_id=1, source_target_pairs={{0,4},{1,5},{2,6},{3,7},{4,0},{5,1},{6,2},{7,3},{8,12},{9,13},{10,... | collective-permute-start | bytes 393224 | tf_op jit(solution)/shard_map/ppermute | solution.py:248
  5.6 12.3 %collective-permute-start.2 = (f32[128,256]{1,0:T(8,128)}, f32[128,256]{1,0:T(8,128)S(1)}, u32[]{:S(2)}, u32[]{:S(2)}) collective-permute-start(f32[128,256]{1,0:T(8,128)} %refs_0_.1), channel_id=1, source_target_pairs={{0,1},{1,0},{2,3},{3,2},{4,5},{5,4},{6,7},{7,6},{8,9},{9,8},{10,11... | collective-permute-start | bytes 393224 | tf_op jit(solution)/shard_map/ppermute | solution.py:248
  8.7 9.2 %collective-permute-start.3 = (f32[128,256]{1,0:T(8,128)S(1)}, f32[128,256]{1,0:T(8,128)S(1)}, u32[]{:S(2)}, u32[]{:S(2)}) collective-permute-start(f32[128,256]{1,0:T(8,128)S(1)} %collective-permute-done.1.refs_1_), channel_id=1, source_target_pairs={{0,1},{1,0},{2,3},{3,2},{4,5},{5,4},{6,7},{7,6},{8,9},{9,8},{10,11... | collective-permute-start | bytes 393224 | tf_op jit(solution)/shard_map/ppermute | solution.py:248
  12.0 6.6 %collective-permute-start.4 = (f32[128,256]{1,0:T(8,128)S(1)}, f32[128,256]{1,0:T(8,128)S(1)}, u32[]{:S(2)}, u32[]{:S(2)}) collective-permute-start(f32[128,256]{1,0:T(8,128)S(1)} %collective-permute-done.refs_2_), channel_id=1, source_target_pairs={{0,3},{1,2},{2,1},{3,0},{4,7},{5,6},{6,5},{7,4},{8,11},{9,10},{10,... | collective-permute-start | bytes 393224 | tf_op jit(solution)/shard_map/ppermute | solution.py:248
  13.4 6.1 %collective-permute-start.5 = (f32[128,256]{1,0:T(8,128)S(1)}, f32[128,256]{1,0:T(8,128)S(1)}, u32[]{:S(2)}, u32[]{:S(2)}) collective-permute-start(f32[128,256]{1,0:T(8,128)S(1)} %collective-permute-done.refs_2_), channel_id=1, source_target_pairs={{0,1},{1,0},{2,3},{3,2},{4,5},{5,4},{6,7},{7,6},{8,9},{9,8},{10,11... | collective-permute-start | bytes 393224 | tf_op jit(solution)/shard_map/ppermute | solution.py:248
  13.9 5.6 %collective-permute-start.6 = (f32[128,256]{1,0:T(8,128)S(1)}, f32[128,256]{1,0:T(8,128)S(1)}, u32[]{:S(2)}, u32[]{:S(2)}) collective-permute-start(f32[128,256]{1,0:T(8,128)S(1)} %collective-permute-done.refs_2_), channel_id=1, source_target_pairs={{0,2},{1,3},{2,0},{3,1},{4,6},{5,7},{6,4},{7,5},{8,10},{9,11},{10,... | collective-permute-start | bytes 393224 | tf_op jit(solution)/shard_map/ppermute | solution.py:248
  17.9 4.8 %copy-start.1 = (f32[256,256]{1,0:T(8,128)S(1)}, f32[256,256]{1,0:T(8,128)}, u32[]{:S(2)}) copy-start(f32[256,256]{1,0:T(8,128)} %ws_ref.1) | copy-start | bytes 786436
  17.9 4.7 %copy-start.2 = (f32[256,256]{1,0:T(8,128)S(1)}, f32[256,256]{1,0:T(8,128)}, u32[]{:S(2)}) copy-start(f32[256,256]{1,0:T(8,128)} %wn_ref.1) | copy-start | bytes 786436
  18.0 4.7 %copy-start.3 = (f32[256]{0:T(256)S(1)}, f32[256]{0:T(256)}, u32[]{:S(2)}) copy-start(f32[256]{0:T(256)} %b_ref.1) | copy-start | bytes 3076
  19.7 1.4 %collective-permute-start.8 = (f32[136,256]{1,0:T(8,128)S(1)}, f32[136,256]{1,0:T(8,128)S(1)}, u32[]{:S(2)}, u32[]{:S(2)}) collective-permute-start(f32[136,256]{1,0:T(8,128)S(1)} %late_products.3), channel_id=1, source_target_pairs={{0,8},{8,0},{16,24},{24,16},{1,9},{9,1},{17,25},{25,17},{2,10},{10... | collective-permute-start | bytes 417800 | tf_op jit(solution)/shard_map/ppermute | solution.py:248
  20.1 2.8 %collective-permute-start.7 = (f32[136,256]{1,0:T(8,128)S(1)}, f32[136,256]{1,0:T(8,128)S(1)}, u32[]{:S(2)}, u32[]{:S(2)}) collective-permute-start(f32[136,256]{1,0:T(8,128)S(1)} %get-tuple-element.23), channel_id=1, source_target_pairs={{0,8},{8,0},{16,24},{24,16},{1,9},{9,1},{17,25},{25,17},{2,10},{10... | collective-permute-start | bytes 417800 | tf_op jit(solution)/shard_map/ppermute | solution.py:248
  21.1 5.8 %collective-permute-start.9 = (f32[136,256]{1,0:T(8,128)S(1)}, f32[136,256]{1,0:T(8,128)S(1)}, u32[]{:S(2)}, u32[]{:S(2)}) collective-permute-start(f32[136,256]{1,0:T(8,128)S(1)} %fold_sums.3), channel_id=1, source_target_pairs={{0,16},{8,24},{16,0},{24,8},{1,17},{9,25},{17,1},{25,9},{2,18},{10... | collective-permute-start | bytes 417800 | tf_op jit(solution)/shard_map/ppermute | solution.py:248
